TPU v7x, 1024 devices: a whole 4x8x16 slice. The times are simulated.
1024 devices in a mesh: rep: 8 (over x, core), node: 8 (over y), local: 16 (over z).
Axes of the slice: x: 4, y: 8, z: 16, core: 2. Of those that a mesh axis runs over, the one named last changes fastest.
Arguments:
- tokens: bfloat16 [2048, 3584], P(('rep', 'node', 'local')), may hold values from -6 to 6
- cotangent: bfloat16 [2048, 3584], P(('rep', 'node', 'local')), may hold values from -1.1953125 to 1.1953125
- expert_ids: int32 [2048, 8], P(('rep', 'node', 'local')), may hold values from 0 to 127, as said below
- node_groups: int32 [2048, 4], P(('rep', 'node', 'local')), may hold values from 0 to 7, as said below
- route_weight: bfloat16 [2048, 8], P(('rep', 'node', 'local')), may hold values from 0.099609375 to 1
- w_gate: bfloat16 [128, 3584, 1024], P(('node', 'local'), None, 'rep'), may hold values from -0.09375 to 0.09375
- w_up: bfloat16 [128, 3584, 1024], P(('node', 'local'), None, 'rep'), may hold values from -0.09375 to 0.09375
- w_down: bfloat16 [128, 1024, 3584], P(('node', 'local'), 'rep'), may hold values from -0.1875 to 0.1875
Outputs:
- mixed: bfloat16 [2048, 3584], P(('rep', 'node', 'local'))
- grad_x: bfloat16 [2048, 3584], P(('rep', 'node', 'local'))
- grad_route: bfloat16 [2048, 8], P(('rep', 'node', 'local'))
Inputs may be any that keep to these rules, and one draw needn't show every extreme that they name: `expert_ids`: each row names 8 different experts: one or two in each node group that node_groups lists for the row, and at most one in each other node group. Counting only the picks whose node group the row lists, among the 16 rows of the devices that share one rep index and one local index, no expert is named by more than 2 rows, and in every node group some expert is named by exactly 2 of them. `node_groups`: each row lists 4 different node groups. Among the 16 rows of the devices that share one rep index and one local index, every node group is listed by exactly half of the rows.
All inputs are finite; a program needn't handle non-finite values.
Results may differ from a plain program's by a relative error of at most 0.03.
Values may be sent and summed in bfloat16 or wider, within the bound.
No kernel may reach another device: no remote copies, remote signals or barrier semaphores. Data moves between devices by JAX's collectives and lax.ppermute only.
A program may use at most 32 MiB of HBM per device.

v0:
```python
import jax
import jax.numpy as jnp
from jax import lax
from jax.sharding import PartitionSpec as P


def contract_rows(left_side, right_side):
    return lax.dot_general(
        left_side, right_side, (((0,), (0,)), ((), ())), preferred_element_type=jnp.float32
    )


def contract_cols(left_side, right_side):
    return lax.dot_general(
        left_side, right_side, (((1,), (1,)), ((), ())), preferred_element_type=jnp.float32
    )


def backward_terms(
    all_cot, gate_pre, up_pre, sigmoid_gate, active, gate_weight, up_weight, down_weight
):
    grad_hidden = contract_cols(all_cot, down_weight)
    grad_gate_pre = (
        grad_hidden * up_pre * sigmoid_gate * (1.0 + gate_pre * (1.0 - sigmoid_gate))
    ).astype(jnp.bfloat16)
    grad_up_pre = (grad_hidden * active).astype(jnp.bfloat16)
    part_gx = contract_cols(grad_gate_pre, gate_weight) + contract_cols(grad_up_pre, up_weight)
    return part_gx


def local(tokens, cotangent, expert_ids, node_groups, route_weight, w_gate, w_up, w_down):
    node_count = lax.axis_size("node")
    local_count = lax.axis_size("local")
    tok_rows, model_width = tokens.shape
    top_count = expert_ids.shape[1]
    block_rows = tok_rows * node_count
    capacity = 2 * block_rows // local_count
    slot_count = local_count * capacity
    pick_group = expert_ids // local_count
    group_range = jnp.arange(node_count, dtype=jnp.int32)
    local_range = jnp.arange(local_count, dtype=jnp.int32)
    listed = jnp.any(pick_group[:, :, None] == node_groups[:, None, :], axis=2)
    same_group = (pick_group[:, :, None] == pick_group[:, None, :]) & listed[:, None, :]
    pick_range = jnp.arange(top_count, dtype=jnp.int32)
    earlier = pick_range[None, :] < pick_range[:, None]
    pick_rank = jnp.sum((same_group & earlier[None, :, :]).astype(jnp.int32), axis=2)
    group_hit = pick_group[:, :, None] == group_range[None, None, :]
    rank_hit = pick_rank[:, :, None] == jnp.arange(2, dtype=jnp.int32)[None, None, :]
    pick_slot = (
        listed[:, :, None, None] & group_hit[:, :, :, None] & rank_hit[:, :, None, :]
    ).astype(jnp.float32)
    local_hit = ((expert_ids % local_count)[:, :, None] == local_range[None, None, :]).astype(
        jnp.float32
    )
    weight_f = route_weight.astype(jnp.float32)
    slot_weights = jnp.transpose(jnp.sum(pick_slot * weight_f[:, :, None, None], axis=1), (1, 0, 2))
    occupied = jnp.transpose(jnp.sum(pick_slot, axis=1), (1, 0, 2))
    slot_select = jnp.sum(
        pick_slot[:, :, :, :, None] * (weight_f[:, :, None] * local_hit)[:, :, None, None, :],
        axis=1,
    )
    select = (
        jnp.transpose(slot_select, (1, 0, 2, 3))
        .astype(jnp.bfloat16)
        .reshape(node_count, 2 * tok_rows, local_count)
    )
    keep_picks = occupied[:, :, :, None].astype(jnp.bfloat16)
    rows_out = (tokens[None, :, None, :] * keep_picks).reshape(
        node_count, 2 * tok_rows, model_width
    )
    cot_out = (cotangent[None, :, None, :] * keep_picks).reshape(
        node_count, 2 * tok_rows, model_width
    )
    rows_in, cot_in, select_in = (
        lax.all_to_all(rows_out, "node", split_axis=0, concat_axis=0, tiled=True),
        lax.all_to_all(cot_out, "node", split_axis=0, concat_axis=0, tiled=True),
        lax.all_to_all(select, "node", split_axis=0, concat_axis=0, tiled=True),
    )
    arrived = rows_in.shape[0] * rows_in.shape[1]
    rows_in = rows_in.reshape(arrived, model_width)
    cot_in = cot_in.reshape(arrived, model_width)
    select_in = select_in.reshape(arrived, local_count)
    live_picks = (select_in > 0).astype(jnp.int32)
    before = jnp.cumsum(live_picks, axis=0) - live_picks
    slot_range = jnp.arange(capacity, dtype=jnp.int32)[None, :, None]
    placement = (jnp.transpose(live_picks)[:, None, :] > 0) & (
        jnp.transpose(before)[:, None, :] == slot_range
    )
    place_f = placement.astype(jnp.float32)
    place_b = place_f.astype(jnp.bfloat16).reshape(slot_count, arrived)
    select_cols = jnp.transpose(select_in).astype(jnp.float32)[:, None, :]
    send_rows = jnp.dot(place_b, rows_in, preferred_element_type=jnp.float32).astype(jnp.bfloat16)
    send_cot = jnp.dot(place_b, cot_in, preferred_element_type=jnp.float32).astype(jnp.bfloat16)
    slot_weight = jnp.sum(place_f * select_cols, axis=2).astype(jnp.bfloat16)
    expert_rows, expert_cot, expert_weight = (
        lax.all_to_all(
            send_rows.reshape(local_count, capacity, model_width),
            "local",
            split_axis=0,
            concat_axis=0,
            tiled=True,
        ),
        lax.all_to_all(
            send_cot.reshape(local_count, capacity, model_width),
            "local",
            split_axis=0,
            concat_axis=0,
            tiled=True,
        ),
        lax.all_to_all(slot_weight, "local", split_axis=0, concat_axis=0, tiled=True),
    )
    slot_rows = expert_rows.reshape(slot_count, model_width)
    slot_cot = expert_cot.reshape(slot_count, model_width)
    slot_scale = expert_weight.reshape(slot_count, 1).astype(jnp.float32)
    scaled_cot = (slot_scale * slot_cot.astype(jnp.float32)).astype(jnp.bfloat16)
    all_rows, all_cot = (
        lax.all_gather(slot_rows, "rep", axis=0, tiled=True),
        lax.all_gather(scaled_cot, "rep", axis=0, tiled=True),
    )
    gate_weight = w_gate[0]
    up_weight = w_up[0]
    down_weight = w_down[0]
    gate_pre = jnp.dot(all_rows, gate_weight, preferred_element_type=jnp.float32)
    up_pre = jnp.dot(all_rows, up_weight, preferred_element_type=jnp.float32)
    sigmoid_gate = jax.nn.sigmoid(gate_pre)
    active = gate_pre * sigmoid_gate
    hidden = (active * up_pre).astype(jnp.bfloat16)
    part_out = jnp.dot(hidden, down_weight, preferred_element_type=jnp.float32)
    part_gx = backward_terms(
        all_cot, gate_pre, up_pre, sigmoid_gate, active, gate_weight, up_weight, down_weight
    )
    expert_out, grad_x_sum = (
        lax.psum_scatter(
            part_out.astype(jnp.bfloat16), "rep", scatter_dimension=0, tiled=True
        ).astype(jnp.float32),
        lax.psum_scatter(
            part_gx.astype(jnp.bfloat16), "rep", scatter_dimension=0, tiled=True
        ).astype(jnp.float32),
    )
    out_rounded = expert_out.astype(jnp.bfloat16)
    slot_grad_x = grad_x_sum.astype(jnp.bfloat16)
    slot_route = jnp.sum(slot_cot.astype(jnp.float32) * expert_out, axis=1).astype(jnp.bfloat16)
    back_out, back_grad, back_route = (
        lax.all_to_all(
            out_rounded.reshape(local_count, capacity, model_width),
            "local",
            split_axis=0,
            concat_axis=0,
            tiled=True,
        ),
        lax.all_to_all(
            slot_grad_x.reshape(local_count, capacity, model_width),
            "local",
            split_axis=0,
            concat_axis=0,
            tiled=True,
        ),
        lax.all_to_all(
            slot_route.reshape(local_count, capacity),
            "local",
            split_axis=0,
            concat_axis=0,
            tiled=True,
        ),
    )
    back_out = back_out.reshape(slot_count, model_width)
    back_grad = back_grad.reshape(slot_count, model_width)
    row_route = jnp.transpose(
        jnp.sum(place_f * back_route.astype(jnp.float32)[:, :, None], axis=1)
    ).astype(jnp.bfloat16)
    pick_out = contract_rows(place_b, back_out).astype(jnp.bfloat16)
    pick_grad = contract_rows(place_b, back_grad).astype(jnp.bfloat16)
    got_out, got_grad, got_route = (
        lax.all_to_all(
            pick_out.reshape(node_count, 2 * tok_rows, model_width),
            "node",
            split_axis=0,
            concat_axis=0,
            tiled=True,
        ),
        lax.all_to_all(
            pick_grad.reshape(node_count, 2 * tok_rows, model_width),
            "node",
            split_axis=0,
            concat_axis=0,
            tiled=True,
        ),
        lax.all_to_all(
            row_route.reshape(node_count, 2 * tok_rows, local_count),
            "node",
            split_axis=0,
            concat_axis=0,
            tiled=True,
        ),
    )
    got_out = got_out.reshape(node_count, tok_rows, 2, model_width).astype(jnp.float32)
    got_grad = got_grad.reshape(node_count, tok_rows, 2, model_width).astype(jnp.float32)
    group_out = jnp.sum(got_out * slot_weights[:, :, :, None], axis=2).astype(jnp.bfloat16)
    group_grad = jnp.sum(got_grad, axis=2).astype(jnp.bfloat16)
    mixed = jnp.sum(group_out.astype(jnp.float32), axis=0).astype(jnp.bfloat16)
    grad_x = jnp.sum(group_grad.astype(jnp.float32), axis=0).astype(jnp.bfloat16)
    route_back = jnp.transpose(
        got_route.reshape(node_count, tok_rows, 2, local_count).astype(jnp.float32), (1, 0, 2, 3)
    )
    route_terms = (
        pick_slot[:, :, :, :, None] * local_hit[:, :, None, None, :] * route_back[:, None, :, :, :]
    )
    grad_route = jnp.sum(route_terms, axis=(2, 3, 4)).astype(jnp.bfloat16)
    return (mixed, grad_x, grad_route)


def solution(mesh):
    return jax.shard_map(
        local,
        mesh=mesh,
        in_specs=(
            P(("rep", "node", "local"), None),
            P(("rep", "node", "local"), None),
            P(("rep", "node", "local"), None),
            P(("rep", "node", "local"), None),
            P(("rep", "node", "local"), None),
            P(("node", "local"), None, "rep"),
            P(("node", "local"), None, "rep"),
            P(("node", "local"), "rep", None),
        ),
        out_specs=(
            P(("rep", "node", "local"), None),
            P(("rep", "node", "local"), None),
            P(("rep", "node", "local"), None),
        ),
        check_vma=False,
    )
```

profile of v0, /device:TPU:6, one launch (start us, length us, event | category | flops | bytes accessed | tf_op | source)
XLA Modules:
  0.0 333.3 jit_solution(538504090556055538)
XLA Ops:
  10.6 7.1 %all-to-all-start = ((bf16[8,4,16]{2,1,0:T(4,128)(2,1)}), bf16[8,4,16]{2,1,0:T(4,128)(2,1)S(1)}, u32[]{:S(2)}, u32[]{:S(2)}) async-start(bf16[8,4,16]{2,1,0:T(4,128)(2,1)} %copy.105), calls=%async_computation | async-start | bytes 16384 | tf_op jit(solution)/shard_map/all_to_all | solution.py:77
  19.4 0.9 broadcast_multiply_fusion
  20.3 5.1 %all-to-all-done = bf16[8,4,16]{2,1,0:T(4,128)(2,1)S(1)} async-done(((bf16[8,4,16]{2,1,0:T(4,128)(2,1)}), bf16[8,4,16]{2,1,0:T(4,128)(2,1)S(1)}, u32[]{:S(2)}, u32[]{:S(2)}) %all-to-all-start) | async-done | bytes 1056 | tf_op jit(solution)/shard_map/all_to_all | solution.py:77
  25.4 3.4 %all-to-all-start.1 = ((bf16[8,4,3584]{2,1,0:T(4,128)(2,1)}), bf16[8,4,3584]{2,1,0:T(4,128)(2,1)S(1)}, u32[]{:S(2)}, u32[]{:S(2)}) async-start(bf16[8,4,3584]{2,1,0:T(4,128)(2,1)} %get-tuple-element.8), calls=%async_computation.1 | async-start | bytes 458752 | tf_op jit(solution)/shard_map/all_to_all | solution.py:75
  29.1 9.7 %all-to-all-done.1 = bf16[8,4,3584]{2,1,0:T(4,128)(2,1)S(1)} async-done(((bf16[8,4,3584]{2,1,0:T(4,128)(2,1)}), bf16[8,4,3584]{2,1,0:T(4,128)(2,1)S(1)}, u32[]{:S(2)}, u32[]{:S(2)}) %all-to-all-start.1) | async-done | bytes 229408 | tf_op jit(solution)/shard_map/all_to_all | solution.py:75
  39.2 34.2 %all_to_all.62 = bf16[16,2,3584]{2,1,0:T(2,128)(2,1)S(1)} all-to-all(bf16[16,2,3584]{2,1,0:T(2,128)(2,1)S(1)} %reshape.221), channel_id=1, replica_groups=mesh['rep'=8,'node'=8,'local'=16] {'local'}, dimensions={0} | all-to-all | bytes 458752 | tf_op jit(solution)/shard_map/all_to_all | solution.py:96
  74.3 23.8 %all-gather.3.cloned.1.call-done = bf16[256,3584]{1,0:T(8,128)(2,1)} async-done(((bf16[32,3584]{1,0:T(8,128)(2,1)}), bf16[256,3584]{1,0:T(8,128)(2,1)}) %all-gather.3.cloned.1.call-update) | async-done | bytes 1835024 | tf_op jit(solution)/shard_map/all_gather | solution.py:117
  98.1 2.3 fusion.11
  101.0 1.9 convolution_convert_fusion
  103.0 16.9 %all_to_all.63 = bf16[8,4,3584]{2,1,0:T(4,128)(2,1)S(1)} all-to-all(bf16[8,4,3584]{2,1,0:T(4,128)(2,1)S(1)} %get-tuple-element.7), channel_id=1, replica_groups=mesh['rep'=8,'node'=8,'local'=16] {'node'}, dimensions={0} | all-to-all | bytes 458752 | tf_op jit(solution)/shard_map/all_to_all | solution.py:76
  120.2 29.7 %all_to_all.64 = bf16[16,2,3584]{2,1,0:T(2,128)(2,1)} all-to-all(bf16[16,2,3584]{2,1,0:T(2,128)(2,1)S(1)} %reshape.226), channel_id=1, replica_groups=mesh['rep'=8,'node'=8,'local'=16] {'local'}, dimensions={0} | all-to-all | bytes 458752 | tf_op jit(solution)/shard_map/all_to_all | solution.py:103
  149.9 1.0 reshape.233
  150.9 1.1 multiply_reduce_fusion
  152.7 6.8 %all-to-all-start.10 = ((bf16[16,1,2]{2,1,0:T(2,128)(2,1)}), bf16[16,1,2]{2,1,0:T(2,128)(2,1)S(1)}, u32[]{:S(2)}, u32[]{:S(2)}) async-start(bf16[16,1,2]{2,1,0:T(2,128)(2,1)} %convert_element_type.250), calls=%async_computation.12 | async-start | bytes 16384 | tf_op jit(solution)/shard_map/all_to_all | solution.py:158
  159.6 12.3 %all-to-all-done.10 = bf16[16,1,2]{2,1,0:T(2,128)(2,1)S(1)} async-done(((bf16[16,1,2]{2,1,0:T(2,128)(2,1)}), bf16[16,1,2]{2,1,0:T(2,128)(2,1)S(1)}, u32[]{:S(2)}, u32[]{:S(2)}) %all-to-all-start.10) | async-done | bytes 96 | tf_op jit(solution)/shard_map/all_to_all | solution.py:158
  172.4 14.9 %all_to_all.65 = bf16[16,1,2]{2,1,0:T(2,128)(2,1)S(1)} all-to-all(bf16[16,1,2]{2,1,0:T(2,128)(2,1)S(1)} %copy.115), channel_id=1, replica_groups=mesh['rep'=8,'node'=8,'local'=16] {'local'}, dimensions={0} | all-to-all | bytes 128 | tf_op jit(solution)/shard_map/all_to_all | solution.py:110
  187.5 0.8 multiply_convert_fusion
  188.3 27.0 %all-gather.5.cloned.1.call-done = bf16[256,3584]{1,0:T(8,128)(2,1)} async-done(((bf16[32,3584]{1,0:T(8,128)(2,1)}), bf16[256,3584]{1,0:T(8,128)(2,1)}) %all-gather.5.cloned.1.call-update) | async-done | bytes 1835024 | tf_op jit(solution)/shard_map/all_gather | solution.py:118
  215.3 2.1 fusion.3
  218.1 1.9 fusion
  220.7 5.5 %all-to-all-start.11 = ((bf16[8,4,16]{2,1,0:T(4,128)(2,1)}), bf16[8,4,16]{2,1,0:T(4,128)(2,1)S(1)}, u32[]{:S(2)}, u32[]{:S(2)}) async-start(bf16[8,4,16]{2,1,0:T(4,128)(2,1)} %bitcast.19), calls=%async_computation.13 | async-start | bytes 16384 | tf_op jit(solution)/shard_map/all_to_all | solution.py:188
  226.2 0.8 reshape.223
  227.0 6.9 %all-to-all-done.11 = bf16[8,4,16]{2,1,0:T(4,128)(2,1)S(1)} async-done(((bf16[8,4,16]{2,1,0:T(4,128)(2,1)}), bf16[8,4,16]{2,1,0:T(4,128)(2,1)S(1)}, u32[]{:S(2)}, u32[]{:S(2)}) %all-to-all-start.11) | async-done | bytes 1056 | tf_op jit(solution)/shard_map/all_to_all | solution.py:188
  233.9 13.0 %all-to-all-start.3 = ((bf16[16,2,3584]{2,1,0:T(2,128)(2,1)}), bf16[16,2,3584]{2,1,0:T(2,128)(2,1)S(1)}, u32[]{:S(2)}, u32[]{:S(2)}) async-start(bf16[16,2,3584]{2,1,0:T(2,128)(2,1)} %reshape.223), calls=%async_computation.4 | async-start | bytes 458752 | tf_op jit(solution)/shard_map/all_to_all | solution.py:144
  247.0 14.9 %reduce-scatter.5.cloned.1.call-done = bf16[32,3584]{1,0:T(8,128)(2,1)} async-done(((bf16[256,3584]{1,0:T(8,128)(2,1)}), bf16[32,3584]{1,0:T(8,128)(2,1)}) %reduce-scatter.5.cloned.1.call-update) | async-done | bytes 229392 | tf_op jit(solution)/shard_map/reduce_scatter | solution.py:136
  261.9 1.7 reshape.227
  263.7 12.8 %all-to-all-start.8 = ((bf16[16,2,3584]{2,1,0:T(2,128)(2,1)}), bf16[16,2,3584]{2,1,0:T(2,128)(2,1)S(1)}, u32[]{:S(2)}, u32[]{:S(2)}) async-start(bf16[16,2,3584]{2,1,0:T(2,128)(2,1)} %reshape.227), calls=%async_computation.10 | async-start | bytes 458752 | tf_op jit(solution)/shard_map/all_to_all | solution.py:151
  277.7 15.8 %all-to-all-done.8 = bf16[16,2,3584]{2,1,0:T(2,128)(2,1)S(1)} async-done(((bf16[16,2,3584]{2,1,0:T(2,128)(2,1)}), bf16[16,2,3584]{2,1,0:T(2,128)(2,1)S(1)}, u32[]{:S(2)}, u32[]{:S(2)}) %all-to-all-start.8) | async-done | bytes 229408 | tf_op jit(solution)/shard_map/all_to_all | solution.py:151
  293.5 5.1 %all-to-all-start.4 = ((bf16[8,4,3584]{2,1,0:T(4,128)(2,1)}), bf16[8,4,3584]{2,1,0:T(4,128)(2,1)S(1)}, u32[]{:S(2)}, u32[]{:S(2)}) async-start(bf16[8,4,3584]{2,1,0:T(4,128)(2,1)} %reshape.224), calls=%async_computation.5 | async-start | bytes 458752 | tf_op jit(solution)/shard_map/all_to_all | solution.py:174
  299.6 10.7 %all-to-all-done.4 = bf16[8,4,3584]{2,1,0:T(4,128)(2,1)S(1)} async-done(((bf16[8,4,3584]{2,1,0:T(4,128)(2,1)}), bf16[8,4,3584]{2,1,0:T(4,128)(2,1)S(1)}, u32[]{:S(2)}, u32[]{:S(2)}) %all-to-all-start.4) | async-done | bytes 229408 | tf_op jit(solution)/shard_map/all_to_all | solution.py:174
  310.3 3.4 %all-to-all-start.9 = ((bf16[8,4,3584]{2,1,0:T(4,128)(2,1)}), bf16[8,4,3584]{2,1,0:T(4,128)(2,1)S(1)}, u32[]{:S(2)}, u32[]{:S(2)}) async-start(bf16[8,4,3584]{2,1,0:T(4,128)(2,1)} %reshape.228), calls=%async_computation.11 | async-start | bytes 458752 | tf_op jit(solution)/shard_map/all_to_all | solution.py:181
  316.1 9.9 %all-to-all-done.9 = bf16[8,4,3584]{2,1,0:T(4,128)(2,1)S(1)} async-done(((bf16[8,4,3584]{2,1,0:T(4,128)(2,1)}), bf16[8,4,3584]{2,1,0:T(4,128)(2,1)S(1)}, u32[]{:S(2)}, u32[]{:S(2)}) %all-to-all-start.9) | async-done | bytes 229408 | tf_op jit(solution)/shard_map/all_to_all | solution.py:181
  (80 shorter events, 15.9 us)
Async XLA Ops:
  7.2 93.9 %copy-start = (bf16[1,128,3584]{2,1,0:T(8,128)(2,1)S(1)}, bf16[1,128,3584]{2,1,0:T(8,128)(2,1)}, u32[]{:S(2)}) copy-start(bf16[1,128,3584]{2,1,0:T(8,128)(2,1)} %param.15) | copy-start | bytes 2752516
  10.6 14.8 %all-to-all-start = ((bf16[8,4,16]{2,1,0:T(4,128)(2,1)}), bf16[8,4,16]{2,1,0:T(4,128)(2,1)S(1)}, u32[]{:S(2)}, u32[]{:S(2)}) async-start(bf16[8,4,16]{2,1,0:T(4,128)(2,1)} %copy.105), calls=%async_computation | async-start | bytes 16384 | tf_op jit(solution)/shard_map/all_to_all | solution.py:77
  19.4 78.7 %copy-start.2 = (bf16[1,3584,128]{2,1,0:T(8,128)(2,1)S(1)}, bf16[1,3584,128]{2,1,0:T(8,128)(2,1)}, u32[]{:S(2)}) copy-start(bf16[1,3584,128]{2,1,0:T(8,128)(2,1)} %param.13) | copy-start | bytes 2752516
  25.4 13.5 %all-to-all-start.1 = ((bf16[8,4,3584]{2,1,0:T(4,128)(2,1)}), bf16[8,4,3584]{2,1,0:T(4,128)(2,1)S(1)}, u32[]{:S(2)}, u32[]{:S(2)}) async-start(bf16[8,4,3584]{2,1,0:T(4,128)(2,1)} %get-tuple-element.8), calls=%async_computation.1 | async-start | bytes 458752 | tf_op jit(solution)/shard_map/all_to_all | solution.py:75
  28.8 69.3 %all-gather.3.cloned.1.call-start = ((), (), s32[]{:S(2)}) async-start(), calls=%async_computation.14 | async-start | bytes 2064384 | tf_op jit(solution)/shard_map/all_gather | solution.py:117
  73.4 26.9 %copy-start.3 = (bf16[1,3584,128]{2,1,0:T(8,128)(2,1)S(1)}, bf16[1,3584,128]{2,1,0:T(8,128)(2,1)}, u32[]{:S(2)}) copy-start(bf16[1,3584,128]{2,1,0:T(8,128)(2,1)} %param.14) | copy-start | bytes 2752516
  74.2 76.7 %reduce-scatter.3.cloned.1.call-start = ((), (), s32[]{:S(2)}) async-start(), calls=%async_computation.15 | async-start | bytes 2064384 | tf_op jit(solution)/shard_map/reduce_scatter | solution.py:133
  98.1 2.3 copy-start.1
  152.7 19.1 %all-to-all-start.10 = ((bf16[16,1,2]{2,1,0:T(2,128)(2,1)}), bf16[16,1,2]{2,1,0:T(2,128)(2,1)S(1)}, u32[]{:S(2)}, u32[]{:S(2)}) async-start(bf16[16,1,2]{2,1,0:T(2,128)(2,1)} %convert_element_type.250), calls=%async_computation.12 | async-start | bytes 16384 | tf_op jit(solution)/shard_map/all_to_all | solution.py:158
  159.5 55.8 %all-gather.5.cloned.1.call-start = ((), (), s32[]{:S(2)}) async-start(), calls=%async_computation.16 | async-start | bytes 2064384 | tf_op jit(solution)/shard_map/all_gather | solution.py:118
  188.3 73.6 %reduce-scatter.5.cloned.1.call-start = ((), (), s32[]{:S(2)}) async-start(), calls=%async_computation.17 | async-start | bytes 2064384 | tf_op jit(solution)/shard_map/reduce_scatter | solution.py:136
  220.0 6.2 %copy-start.4 = (bf16[32,3584]{1,0:T(8,128)(2,1)S(1)}, bf16[32,3584]{1,0:T(8,128)(2,1)}, u32[]{:S(2)}) copy-start(bf16[32,3584]{1,0:T(8,128)(2,1)} %reduce-scatter.3.cloned.1.call-done) | copy-start | bytes 688132
  220.7 13.2 %all-to-all-start.11 = ((bf16[8,4,16]{2,1,0:T(4,128)(2,1)}), bf16[8,4,16]{2,1,0:T(4,128)(2,1)S(1)}, u32[]{:S(2)}, u32[]{:S(2)}) async-start(bf16[8,4,16]{2,1,0:T(4,128)(2,1)} %bitcast.19), calls=%async_computation.13 | async-start | bytes 16384 | tf_op jit(solution)/shard_map/all_to_all | solution.py:188
  233.9 29.8 %all-to-all-start.3 = ((bf16[16,2,3584]{2,1,0:T(2,128)(2,1)}), bf16[16,2,3584]{2,1,0:T(2,128)(2,1)S(1)}, u32[]{:S(2)}, u32[]{:S(2)}) async-start(bf16[16,2,3584]{2,1,0:T(2,128)(2,1)} %reshape.223), calls=%async_computation.4 | async-start | bytes 458752 | tf_op jit(solution)/shard_map/all_to_all | solution.py:144
  263.7 29.7 %all-to-all-start.8 = ((bf16[16,2,3584]{2,1,0:T(2,128)(2,1)}), bf16[16,2,3584]{2,1,0:T(2,128)(2,1)S(1)}, u32[]{:S(2)}, u32[]{:S(2)}) async-start(bf16[16,2,3584]{2,1,0:T(2,128)(2,1)} %reshape.227), calls=%async_computation.10 | async-start | bytes 458752 | tf_op jit(solution)/shard_map/all_to_all | solution.py:151
  293.5 16.8 %all-to-all-start.4 = ((bf16[8,4,3584]{2,1,0:T(4,128)(2,1)}), bf16[8,4,3584]{2,1,0:T(4,128)(2,1)S(1)}, u32[]{:S(2)}, u32[]{:S(2)}) async-start(bf16[8,4,3584]{2,1,0:T(4,128)(2,1)} %reshape.224), calls=%async_computation.5 | async-start | bytes 458752 | tf_op jit(solution)/shard_map/all_to_all | solution.py:174
  310.3 15.7 %all-to-all-start.9 = ((bf16[8,4,3584]{2,1,0:T(4,128)(2,1)}), bf16[8,4,3584]{2,1,0:T(4,128)(2,1)S(1)}, u32[]{:S(2)}, u32[]{:S(2)}) async-start(bf16[8,4,3584]{2,1,0:T(4,128)(2,1)} %reshape.228), calls=%async_computation.11 | async-start | bytes 458752 | tf_op jit(solution)/shard_map/all_to_all | solution.py:181
Sparse Core Ops, SparseCore 0:
  74.4 23.6 all-gather.2
  103.1 41.5 reduce-scatter.2
  188.4 26.8 all-gather.4
  220.2 41.6 reduce-scatter.4
where the time goes:
time: 335 us; the launch traced here: 333 us
  waiting for transfers between devices  136 us (41%)
  blocking collectives  95.7 us (29%)
  starting transfers between devices  57.2 us (17%)
  between operations  14.1 us (4%)
  local copies, waits for them, and re-layouts  10.7 us (3%)
  matrix products  10.3 us (3%)
  other arithmetic  8.91 us (3%)
    all_to_all x1, blocking collectives, local(): lax.all_to_all(send_rows.reshape(local_count, capacity, model_width), 'lo...  34.2 us
    all_to_all x1, blocking collectives, local(): lax.all_to_all(send_cot.reshape(local_count, capacity, model_width), 'loc...  29.7 us
    all_gather x1, waiting for transfers between devices, local(): lax.all_gather(scaled_cot, 'rep', axis=0, tiled=True)  27 us
    all_gather x1, waiting for transfers between devices, local(): lax.all_gather(slot_rows, 'rep', axis=0, tiled=True)  23.8 us
    all_to_all x1, blocking collectives, local(): lax.all_to_all(cot_out, 'node', split_axis=0, concat_axis=0, tiled=True)  16.9 us
    all_to_all x1, waiting for transfers between devices, local(): lax.all_to_all(slot_grad_x.reshape(local_count, capacity, model_width), '...  15.8 us
    all_to_all x1, blocking collectives, local(): lax.all_to_all(slot_weight, 'local', split_axis=0, concat_axis=0, tiled=T...  14.9 us
    reduce_scatter x1, waiting for transfers between devices, local(): lax.psum_scatter(part_gx.astype(jnp.bfloat16), 'rep', scatter_dimension=0...  14.9 us
  transfers between devices with their start and end apart: 12, of which 11 were waited for; matrix products, arithmetic and copies ran while one was open for 4% of the time, Pallas kernels for 0%

commit v1 on v0

v1 whole, which is shorter than its diff:
```python
import jax
import jax.numpy as jnp
import numpy as np
from jax import lax
from jax.sharding import Mesh, PartitionSpec as P

BF = jnp.bfloat16
F32 = jnp.float32


def dot(left_side, right_side, left_dim=1, right_dim=0):
    return lax.dot_general(
        left_side,
        right_side,
        (((left_dim,), (right_dim,)), ((), ())),
        preferred_element_type=F32,
    )


def local(tokens, cotangent, expert_ids, node_groups, route_weight, w_gate, w_up, w_down):
    node_count = lax.axis_size("node")
    local_count = lax.axis_size("local")
    tok_rows, width = tokens.shape
    top_count = expert_ids.shape[1]
    limit = node_groups.shape[1]
    rows = tok_rows * node_count
    capacity = 2 * rows // local_count
    slots = local_count * capacity
    swap = [(0, 1), (1, 0)]

    gates = (w_gate[0], lax.ppermute(w_gate[0], "core", swap))
    ups = (w_up[0], lax.ppermute(w_up[0], "core", swap))
    downs = (w_down[0], lax.ppermute(w_down[0], "core", swap))

    used = 2 * top_count + limit
    info = jnp.concatenate(
        [
            expert_ids.astype(BF),
            node_groups.astype(BF),
            route_weight,
            jnp.zeros((tok_rows, 128 - used), BF),
        ],
        axis=1,
    )
    payload = jnp.concatenate([tokens, cotangent, info], axis=1)
    gathered = lax.all_gather(payload, "node", axis=0, tiled=True)
    tok = gathered[:, :width]
    cot = gathered[:, width : 2 * width]
    info = gathered[:, 2 * width :].astype(F32)
    ids = info[:, :top_count].astype(jnp.int32)
    groups = info[:, top_count : top_count + limit].astype(jnp.int32)
    weights = info[:, top_count + limit : used]

    me = lax.axis_index("node")
    listed = jnp.any(groups == me, axis=1)
    mine = (ids // local_count == me) & listed[:, None]
    expert_range = jnp.arange(local_count, dtype=jnp.int32)
    pick_hit = mine[:, None, :] & ((ids % local_count)[:, None, :] == expert_range[None, :, None])
    hit = jnp.any(pick_hit, axis=2)
    weight_of = jnp.sum(jnp.where(pick_hit, weights[:, None, :], 0.0), axis=2)
    hit_i = hit.astype(jnp.int32)
    before = jnp.cumsum(hit_i, axis=0) - hit_i
    slot_range = jnp.arange(capacity, dtype=jnp.int32)
    place = hit[:, :, None] & (before[:, :, None] == slot_range)
    place_f = place.astype(F32)
    place_w = (place_f * weight_of[:, :, None]).astype(BF).reshape(rows, slots)
    place_b = place_f.astype(BF).reshape(rows, slots)
    send_tok = dot(place_b, tok, 0, 0).astype(BF)
    send_cot = dot(place_w, cot, 0, 0).astype(BF)

    got_tok = lax.all_to_all(send_tok, "local", split_axis=0, concat_axis=0, tiled=True)
    got_cot = lax.all_to_all(send_cot, "local", split_axis=0, concat_axis=0, tiled=True)
    all_tok = lax.all_gather(got_tok, "x", axis=0, tiled=True)
    all_cot = lax.all_gather(got_cot, "x", axis=0, tiled=True)

    part_out = 0.0
    kept = []
    for gate_w, up_w, down_w in zip(gates, ups, downs):
        gate_pre = dot(all_tok, gate_w)
        up_pre = dot(all_tok, up_w)
        sig = jax.nn.sigmoid(gate_pre)
        active = gate_pre * sig
        hidden = (active * up_pre).astype(BF)
        part_out = part_out + dot(hidden, down_w)
        kept.append((gate_pre, up_pre, sig, active))
    out_parts = lax.all_to_all(part_out.astype(BF), "x", split_axis=0, concat_axis=0, tiled=True)

    part_gx = 0.0
    for gate_w, up_w, down_w, (gate_pre, up_pre, sig, active) in zip(gates, ups, downs, kept):
        grad_hidden = dot(all_cot, down_w, 1, 1)
        grad_gate = (grad_hidden * up_pre * sig * (1.0 + gate_pre * (1.0 - sig))).astype(BF)
        grad_up = (grad_hidden * active).astype(BF)
        part_gx = part_gx + dot(grad_gate, gate_w, 1, 1) + dot(grad_up, up_w, 1, 1)
    gx_parts = lax.all_to_all(part_gx.astype(BF), "x", split_axis=0, concat_axis=0, tiled=True)

    def reduce_parts(parts):
        return jnp.sum(parts.reshape(-1, slots, width).astype(F32), axis=0).astype(BF)

    back_out = lax.all_to_all(
        reduce_parts(out_parts), "local", split_axis=0, concat_axis=0, tiled=True
    )
    back_gx = lax.all_to_all(
        reduce_parts(gx_parts), "local", split_axis=0, concat_axis=0, tiled=True
    )

    group_out = dot(place_w, back_out).astype(BF)
    pair_sum = dot(cot, back_out, 1, 1).reshape(rows, local_count, capacity)
    slot_route = jnp.sum(pair_sum * place_f, axis=2)
    route = jnp.sum(jnp.where(pick_hit, slot_route[:, :, None], 0.0), axis=1).astype(BF)
    route = jnp.concatenate([route, jnp.zeros((rows, 128 - top_count), BF)], axis=1)
    home_out = lax.all_to_all(
        jnp.concatenate([group_out, route], axis=1),
        "node",
        split_axis=0,
        concat_axis=0,
        tiled=True,
    )
    group_gx = dot(place_b, back_gx).astype(BF)
    home_gx = lax.all_to_all(group_gx, "node", split_axis=0, concat_axis=0, tiled=True)
    home = jnp.sum(home_out.reshape(node_count, tok_rows, -1).astype(F32), axis=0).astype(BF)
    mixed = home[:, :width]
    grad_route = home[:, width : width + top_count]
    grad_x = jnp.sum(home_gx.reshape(node_count, tok_rows, width).astype(F32), axis=0).astype(BF)
    return (mixed, grad_x, grad_route)


def solution(mesh):
    shape = mesh.devices.shape
    split = Mesh(
        np.asarray(mesh.devices).reshape((shape[0] // 2, 2) + shape[1:]),
        ("x", "core", "node", "local"),
    )
    row_spec = P(("x", "core", "node", "local"), None)
    return jax.shard_map(
        local,
        mesh=split,
        in_specs=(
            row_spec,
            row_spec,
            row_spec,
            row_spec,
            row_spec,
            P(("node", "local"), None, ("x", "core")),
            P(("node", "local"), None, ("x", "core")),
            P(("node", "local"), ("x", "core"), None),
        ),
        out_specs=(row_spec, row_spec, row_spec),
        check_vma=False,
    )
```

time: 335 us -> 222 us (0.66)
  waiting for transfers between devices: 136 us -> 49.3 us
  between operations: 14.1 us -> 0.97 us
  starting transfers between devices: 57.2 us -> 46.2 us
  other arithmetic: 8.91 us -> 3.4 us
    all_gather x0 -> x3, blocking collectives: none -> 53.9 us  [the longest x1 26.3 us: local(): gathered = lax.all_gather(payload, 'node', axis=0, tiled=True)]
    all_to_all x4 -> x3, blocking collectives: 95.7 us -> 44.5 us  [the longest x1 19.3 us: local(): lax.all_to_all(send_cot, 'local', split_axis=0, concat_axis=0, tiled=True)]
    all_gather x2 -> x0, waiting for transfers between devices: 50.8 us -> none  [the longest x1 27 us: local(): lax.all_gather(scaled_cot, 'rep', axis=0, tiled=True)]
    all_to_all x8 -> x5, waiting for transfers between devices: 70.5 us -> 49.3 us  [the longest x1 13.7 us: local(): lax.all_to_all(reduce_parts(out_parts), 'local', split_axis=0, concat_axi...]
    all_to_all x8 -> x5, starting transfers between devices: 57.1 us -> 39.9 us  [the longest x1 18.9 us: local(): lax.all_to_all(send_tok, 'local', split_axis=0, concat_axis=0, tiled=True)]
    reduce_scatter x2 -> x0, waiting for transfers between devices: 15 us -> none  [the longest x1 14.9 us: local(): lax.psum_scatter(part_gx.astype(jnp.bfloat16), 'rep', scatter_dimension=0...]
    ppermute x0 -> x3, starting transfers between devices: none -> 6.38 us  [the longest x1 2.41 us: local(): ups = (w_up[0], lax.ppermute(w_up[0], 'core', swap))]
    reshape x10 -> x0, local copies, waits for them, and re-layouts: 5.65 us -> none  [the longest x1 1.7 us: local(): slot_grad_x.reshape(local_count, capacity, model_width)]
  transfers between devices with their start and end apart: 12 -> 8, of which waited for: 11 -> 5; matrix products, arithmetic and copies ran while one was open for 4% -> 3% of each run, Pallas kernels for 0% -> 0%
where the time goes in v1:
time: 222 us; the launch traced here: 219 us
  blocking collectives  98.4 us (44%)
  waiting for transfers between devices  49.3 us (22%)
  starting transfers between devices  46.2 us (21%)
  matrix products  13.1 us (6%)
  local copies, waits for them, and re-layouts  7.97 us (4%)
  other arithmetic  3.4 us (2%)
    all_gather x1, blocking collectives, local(): gathered = lax.all_gather(payload, 'node', axis=0, tiled=True)  26.3 us
    all_to_all x1, blocking collectives, local(): lax.all_to_all(send_cot, 'local', split_axis=0, concat_axis=0, tiled=True)  19.3 us
    all_to_all x1, starting transfers between devices, local(): lax.all_to_all(send_tok, 'local', split_axis=0, concat_axis=0, tiled=True)  18.9 us
    all_gather x1, blocking collectives, local(): all_tok = lax.all_gather(got_tok, 'x', axis=0, tiled=True)  13.8 us
    all_gather x1, blocking collectives, local(): all_cot = lax.all_gather(got_cot, 'x', axis=0, tiled=True)  13.8 us
    all_to_all x1, waiting for transfers between devices, local(): lax.all_to_all(reduce_parts(out_parts), 'local', split_axis=0, concat_axi...  13.7 us
    dot_general x17, matrix products, dot(): lax.dot_general(left_side, right_side, (((left_dim,), (right_dim,)), ((),...  13.1 us
    all_to_all x1, blocking collectives, local(): lax.all_to_all(part_gx.astype(BF), 'x', split_axis=0, concat_axis=0, tile...  12.7 us
  transfers between devices with their start and end apart: 8, of which 5 were waited for; matrix products, arithmetic and copies ran while one was open for 3% of the time, Pallas kernels for 0%

profile of v1, /device:TPU:6, one launch (start us, length us, event | category | flops | bytes accessed | tf_op | source)
XLA Modules:
  0.0 219.4 jit_solution(4752462753661552197)
XLA Ops:
  0.7 0.8 convert_element_type.91
  2.2 0.8 concatenate.6
  3.0 26.3 %all-gather = bf16[8,2,7296]{2,1,0:T(2,128)(2,1)S(1)} all-gather(bf16[1,2,7296]{2,1,0:T(2,128)(2,1)S(1)} %bitcast.50), channel_id=1, replica_groups=mesh['x'=4,'core'=2,'node'=8,'local'=16] {'node'}, dimensions={0}, use_global_device_ids=true | all-gather | bytes 262656 | tf_op jit(solution)/shard_map/all_gather | solution.py:46
  30.5 0.8 all_to_all.52
  31.2 18.9 %all-to-all-start = ((bf16[16,2,3584]{2,1,0:T(2,128)(2,1)}), bf16[16,2,3584]{2,1,0:T(2,128)(2,1)S(1)}, u32[]{:S(2)}, u32[]{:S(2)}) async-start(bf16[16,2,3584]{2,1,0:T(2,128)(2,1)} %all_to_all.52), calls=%async_computation | async-start | bytes 458752 | tf_op jit(solution)/shard_map/all_to_all | solution.py:71
  50.1 2.1 collective-permute-start.2
  52.2 2.4 %collective-permute-start.1 = (bf16[3584,128]{1,0:T(8,128)(2,1)S(1)}, bf16[3584,128]{1,0:T(8,128)(2,1)}, u32[]{:S(2)}, u32[]{:S(2)}) collective-permute-start(bf16[3584,128]{1,0:T(8,128)(2,1)S(1)} %bitcast.45), channel_id=1, source_target_pairs={{0,128},{128,0},{1,129},{129,1},{2,130},{130,2},{3,131},{131,3},{4... | collective-permute-start | bytes 2752520 | tf_op jit(solution)/shard_map/ppermute | solution.py:32
  54.6 1.9 collective-permute-start
  56.6 7.4 %all-to-all-done = bf16[16,2,3584]{2,1,0:T(2,128)(2,1)S(1)} async-done(((bf16[16,2,3584]{2,1,0:T(2,128)(2,1)}), bf16[16,2,3584]{2,1,0:T(2,128)(2,1)S(1)}, u32[]{:S(2)}, u32[]{:S(2)}) %all-to-all-start) | async-done | bytes 229408 | tf_op jit(solution)/shard_map/all_to_all | solution.py:71
  63.9 0.8 all_to_all.54
  64.7 13.8 %all_gather.10 = bf16[128,3584]{1,0:T(8,128)(2,1)S(1)} all-gather(bf16[32,3584]{1,0:T(8,128)(2,1)} %all_to_all.54), channel_id=1, replica_groups=mesh['x'=4,'core'=2,'node'=8,'local'=16] {'x'}, dimensions={0}, use_global_device_ids=true | all-gather | bytes 1146880 | tf_op jit(solution)/shard_map/all_gather | solution.py:73
  79.7 1.6 fusion.60
  81.3 1.6 fusion.59
  82.9 1.6 fusion.1
  84.5 12.4 %all_to_all.78 = bf16[4,32,3584]{2,1,0:T(8,128)(2,1)S(1)} all-to-all(bf16[4,32,3584]{2,1,0:T(8,128)(2,1)S(1)} %bitcast.49), channel_id=1, replica_groups=mesh['x'=4,'core'=2,'node'=8,'local'=16] {'x'}, dimensions={0} | all-to-all | bytes 1835008 | tf_op jit(solution)/shard_map/all_to_all | solution.py:86
  97.1 0.8 all_to_all.57
  97.9 6.8 %all-to-all-start.2 = ((bf16[16,2,3584]{2,1,0:T(2,128)(2,1)}), bf16[16,2,3584]{2,1,0:T(2,128)(2,1)S(1)}, u32[]{:S(2)}, u32[]{:S(2)}) async-start(bf16[16,2,3584]{2,1,0:T(2,128)(2,1)} %all_to_all.57), calls=%async_computation.2 | async-start | bytes 458752 | tf_op jit(solution)/shard_map/all_to_all | solution.py:99
  104.8 13.7 %all-to-all-done.2 = bf16[16,2,3584]{2,1,0:T(2,128)(2,1)S(1)} async-done(((bf16[16,2,3584]{2,1,0:T(2,128)(2,1)}), bf16[16,2,3584]{2,1,0:T(2,128)(2,1)S(1)}, u32[]{:S(2)}, u32[]{:S(2)}) %all-to-all-start.2) | async-done | bytes 229408 | tf_op jit(solution)/shard_map/all_to_all | solution.py:99
  119.5 19.3 %all_to_all.79 = bf16[16,2,3584]{2,1,0:T(2,128)(2,1)S(1)} all-to-all(bf16[16,2,3584]{2,1,0:T(2,128)(2,1)S(1)} %all_to_all.61), channel_id=1, replica_groups=mesh['x'=4,'core'=2,'node'=8,'local'=16] {'local'}, dimensions={0} | all-to-all | bytes 458752 | tf_op jit(solution)/shard_map/all_to_all | solution.py:72
  138.8 0.8 all_to_all.63
  139.6 13.8 %all_gather.11 = bf16[128,3584]{1,0:T(8,128)(2,1)S(1)} all-gather(bf16[32,3584]{1,0:T(8,128)(2,1)} %all_to_all.63), channel_id=1, replica_groups=mesh['x'=4,'core'=2,'node'=8,'local'=16] {'x'}, dimensions={0}, use_global_device_ids=true | all-gather | bytes 1146880 | tf_op jit(solution)/shard_map/all_gather | solution.py:74
  154.6 1.6 fusion.61
  156.1 1.6 fusion.19
  157.7 1.6 fusion.2
  159.3 12.7 %all_to_all.80 = bf16[4,32,3584]{2,1,0:T(8,128)(2,1)S(1)} all-to-all(bf16[4,32,3584]{2,1,0:T(8,128)(2,1)S(1)} %bitcast.48), channel_id=1, replica_groups=mesh['x'=4,'core'=2,'node'=8,'local'=16] {'x'}, dimensions={0} | all-to-all | bytes 1835008 | tf_op jit(solution)/shard_map/all_to_all | solution.py:94
  172.3 0.8 all_to_all.66
  173.0 5.2 %all-to-all-start.6 = ((bf16[16,2,3584]{2,1,0:T(2,128)(2,1)}), bf16[16,2,3584]{2,1,0:T(2,128)(2,1)S(1)}, u32[]{:S(2)}, u32[]{:S(2)}) async-start(bf16[16,2,3584]{2,1,0:T(2,128)(2,1)} %all_to_all.66), calls=%async_computation.6 | async-start | bytes 458752 | tf_op jit(solution)/shard_map/all_to_all | solution.py:102
  179.3 12.6 %all-to-all-done.6 = bf16[16,2,3584]{2,1,0:T(2,128)(2,1)S(1)} async-done(((bf16[16,2,3584]{2,1,0:T(2,128)(2,1)}), bf16[16,2,3584]{2,1,0:T(2,128)(2,1)S(1)}, u32[]{:S(2)}, u32[]{:S(2)}) %all-to-all-start.6) | async-done | bytes 229408 | tf_op jit(solution)/shard_map/all_to_all | solution.py:102
  191.9 5.6 %all-to-all-start.3 = ((bf16[8,2,3712]{2,1,0:T(2,128)(2,1)}), bf16[8,2,3712]{2,1,0:T(2,128)(2,1)S(1)}, u32[]{:S(2)}, u32[]{:S(2)}) async-start(bf16[8,2,3712]{2,1,0:T(2,128)(2,1)} %all_to_all.59), calls=%async_computation.3 | async-start | bytes 237568 | tf_op jit(solution)/shard_map/all_to_all | solution.py:111
  198.4 8.0 %all-to-all-done.3 = bf16[8,2,3712]{2,1,0:T(2,128)(2,1)S(1)} async-done(((bf16[8,2,3712]{2,1,0:T(2,128)(2,1)}), bf16[8,2,3712]{2,1,0:T(2,128)(2,1)S(1)}, u32[]{:S(2)}, u32[]{:S(2)}) %all-to-all-start.3) | async-done | bytes 118816 | tf_op jit(solution)/shard_map/all_to_all | solution.py:111
  206.5 3.4 %all-to-all-start.7 = ((bf16[8,2,3584]{2,1,0:T(2,128)(2,1)}), bf16[8,2,3584]{2,1,0:T(2,128)(2,1)S(1)}, u32[]{:S(2)}, u32[]{:S(2)}) async-start(bf16[8,2,3584]{2,1,0:T(2,128)(2,1)} %all_to_all.68), calls=%async_computation.7 | async-start | bytes 229376 | tf_op jit(solution)/shard_map/all_to_all | solution.py:119
  211.1 7.6 %all-to-all-done.7 = bf16[8,2,3584]{2,1,0:T(2,128)(2,1)S(1)} async-done(((bf16[8,2,3584]{2,1,0:T(2,128)(2,1)}), bf16[8,2,3584]{2,1,0:T(2,128)(2,1)S(1)}, u32[]{:S(2)}, u32[]{:S(2)}) %all-to-all-start.7) | async-done | bytes 114720 | tf_op jit(solution)/shard_map/all_to_all | solution.py:119
  (56 shorter events, 9.5 us)
Async XLA Ops:
  0.6 49.5 %copy-start.1 = (bf16[1,128,3584]{2,1,0:T(8,128)(2,1)S(1)}, bf16[1,128,3584]{2,1,0:T(8,128)(2,1)}, u32[]{:S(2)}) copy-start(bf16[1,128,3584]{2,1,0:T(8,128)(2,1)} %param.15) | copy-start | bytes 2752516
  0.6 51.6 %copy-start = (bf16[1,3584,128]{2,1,0:T(8,128)(2,1)S(1)}, bf16[1,3584,128]{2,1,0:T(8,128)(2,1)}, u32[]{:S(2)}) copy-start(bf16[1,3584,128]{2,1,0:T(8,128)(2,1)} %param.14) | copy-start | bytes 2752516
  31.2 32.7 %all-to-all-start = ((bf16[16,2,3584]{2,1,0:T(2,128)(2,1)}), bf16[16,2,3584]{2,1,0:T(2,128)(2,1)S(1)}, u32[]{:S(2)}, u32[]{:S(2)}) async-start(bf16[16,2,3584]{2,1,0:T(2,128)(2,1)} %all_to_all.52), calls=%async_computation | async-start | bytes 458752 | tf_op jit(solution)/shard_map/all_to_all | solution.py:71
  50.1 28.8 %copy-start.2 = (bf16[1,3584,128]{2,1,0:T(8,128)(2,1)S(1)}, bf16[1,3584,128]{2,1,0:T(8,128)(2,1)}, u32[]{:S(2)}) copy-start(bf16[1,3584,128]{2,1,0:T(8,128)(2,1)} %param.13) | copy-start | bytes 2752516
  50.1 32.8 %collective-permute-start.2 = (bf16[128,3584]{1,0:T(8,128)(2,1)S(1)}, bf16[128,3584]{1,0:T(8,128)(2,1)}, u32[]{:S(2)}, u32[]{:S(2)}) collective-permute-start(bf16[128,3584]{1,0:T(8,128)(2,1)S(1)} %bitcast.46), channel_id=1, source_target_pairs={{0,128},{128,0},{1,129},{129,1},{2,130},{130,2},{3,131},{131,3},{4... | collective-permute-start | bytes 2752520 | tf_op jit(solution)/shard_map/ppermute | solution.py:33
  52.2 27.5 %collective-permute-start.1 = (bf16[3584,128]{1,0:T(8,128)(2,1)S(1)}, bf16[3584,128]{1,0:T(8,128)(2,1)}, u32[]{:S(2)}, u32[]{:S(2)}) collective-permute-start(bf16[3584,128]{1,0:T(8,128)(2,1)S(1)} %bitcast.45), channel_id=1, source_target_pairs={{0,128},{128,0},{1,129},{129,1},{2,130},{130,2},{3,131},{131,3},{4... | collective-permute-start | bytes 2752520 | tf_op jit(solution)/shard_map/ppermute | solution.py:32
  54.6 26.7 %collective-permute-start = (bf16[3584,128]{1,0:T(8,128)(2,1)}, bf16[3584,128]{1,0:T(8,128)(2,1)}, u32[]{:S(2)}, u32[]{:S(2)}) collective-permute-start(bf16[3584,128]{1,0:T(8,128)(2,1)} %bitcast.47), channel_id=1, source_target_pairs={{0,128},{128,0},{1,129},{129,1},{2,130},{130,2},{3,131},{131,3},{4... | collective-permute-start | bytes 2752520 | tf_op jit(solution)/shard_map/ppermute | solution.py:31
  97.9 20.6 %all-to-all-start.2 = ((bf16[16,2,3584]{2,1,0:T(2,128)(2,1)}), bf16[16,2,3584]{2,1,0:T(2,128)(2,1)S(1)}, u32[]{:S(2)}, u32[]{:S(2)}) async-start(bf16[16,2,3584]{2,1,0:T(2,128)(2,1)} %all_to_all.57), calls=%async_computation.2 | async-start | bytes 458752 | tf_op jit(solution)/shard_map/all_to_all | solution.py:99
  138.8 15.0 %copy-start.3 = (bf16[1,3584,128]{2,1,0:T(8,128)(2,1)S(1)}, bf16[1,3584,128]{2,1,0:T(8,128)(2,1)}, u32[]{:S(2)}) copy-start(bf16[1,3584,128]{2,1,0:T(8,128)(2,1)} %param.13) | copy-start | bytes 2752516
  173.0 18.9 %all-to-all-start.6 = ((bf16[16,2,3584]{2,1,0:T(2,128)(2,1)}), bf16[16,2,3584]{2,1,0:T(2,128)(2,1)S(1)}, u32[]{:S(2)}, u32[]{:S(2)}) async-start(bf16[16,2,3584]{2,1,0:T(2,128)(2,1)} %all_to_all.66), calls=%async_computation.6 | async-start | bytes 458752 | tf_op jit(solution)/shard_map/all_to_all | solution.py:102
  191.9 14.6 %all-to-all-start.3 = ((bf16[8,2,3712]{2,1,0:T(2,128)(2,1)}), bf16[8,2,3712]{2,1,0:T(2,128)(2,1)S(1)}, u32[]{:S(2)}, u32[]{:S(2)}) async-start(bf16[8,2,3712]{2,1,0:T(2,128)(2,1)} %all_to_all.59), calls=%async_computation.3 | async-start | bytes 237568 | tf_op jit(solution)/shard_map/all_to_all | solution.py:111
  206.5 12.2 %all-to-all-start.7 = ((bf16[8,2,3584]{2,1,0:T(2,128)(2,1)}), bf16[8,2,3584]{2,1,0:T(2,128)(2,1)S(1)}, u32[]{:S(2)}, u32[]{:S(2)}) async-start(bf16[8,2,3584]{2,1,0:T(2,128)(2,1)} %all_to_all.68), calls=%async_computation.7 | async-start | bytes 229376 | tf_op jit(solution)/shard_map/all_to_all | solution.py:119

commit v2 on v1

v2 whole, which is shorter than its diff:
```python
import functools

import jax
import jax.numpy as jnp
import numpy as np
from jax import lax
from jax.experimental import pallas as pl
from jax.experimental.pallas import tpu as pltpu
from jax.sharding import Mesh, PartitionSpec as P


BF = jnp.bfloat16
F32 = jnp.float32
LANES = 128
VMEM = pl.BlockSpec(memory_space=pltpu.VMEM)
MIB = 1024 * 1024


def dot(left_side, right_side, left_dim=1, right_dim=0):
    return lax.dot_general(
        left_side,
        right_side,
        (((left_dim,), (right_dim,)), ((), ())),
        preferred_element_type=F32,
    )


def iota(shape, dim):
    return lax.broadcasted_iota(jnp.int32, shape, dim)


def payload_kernel(tok_ref, cot_ref, ids_ref, groups_ref, weight_ref, out_ref, block_ref):
    tok_rows, width = tok_ref.shape
    half = width // 2
    lane = iota((tok_rows, LANES), 1)
    info = jnp.zeros((tok_rows, LANES), F32)
    place = 0
    for ref in (ids_ref, groups_ref, weight_ref):
        values = ref[...].astype(F32)
        for k in range(values.shape[1]):
            info = info + jnp.where(lane == place, values[:, k : k + 1], 0.0)
            place += 1
    for h in range(2):
        for kind, ref in enumerate((tok_ref, cot_ref)):
            at = pl.ds((2 * h + kind) * tok_rows, tok_rows)
            block_ref[at, :half] = ref[:, h * half : (h + 1) * half].astype(F32)
            block_ref[at, half:] = info
    block = block_ref[...].astype(BF)
    size = block.shape[0]
    for y in range(out_ref.shape[0] // size):
        out_ref[y * size : (y + 1) * size, :] = block


def routing(info, me, top_count, limit, local_count):
    shape = (info.shape[0], 8 * local_count)
    col = iota(shape, 1)
    row = iota(shape, 0)
    target = (me * local_count + (col >> 3)).astype(F32)
    listed = jnp.zeros((info.shape[0], 1), F32)
    for j in range(limit):
        match = info[:, top_count + j : top_count + j + 1] == me.astype(F32)
        listed = jnp.maximum(listed, match.astype(F32))
    first_weight = top_count + limit
    hit = jnp.zeros(shape, F32)
    weight = jnp.zeros(shape, F32)
    picks = []
    for k in range(top_count):
        match = (info[:, k : k + 1] == target).astype(F32) * listed
        picks.append(match)
        hit = hit + match
        weight = weight + match * info[:, first_weight + k : first_weight + k + 1]
    return row, col, hit, weight, picks


def placed(hit, row, col, kind):
    rows = hit.shape[0]
    mine = (((row >> 1) & 1) == kind) & (((row >> 2) & 1) == ((col >> 2) & 1))
    hit = jnp.where(mine, hit, 0.0)
    earlier = (iota((rows, rows), 1) < iota((rows, rows), 0)).astype(F32).astype(BF)
    before = dot(earlier, hit.astype(BF))
    return jnp.where(before == (col & 1).astype(F32), hit, 0.0)


def side(place, col, p):
    return jnp.where(((col >> 1) & 1) == p, place, 0.0).astype(BF)


def dispatch_kernel(top_count, limit, local_count, me_ref, rows_ref, tok_ref, cot_ref):
    quarter = tok_ref.shape[1]
    info = rows_ref[:, 2 * quarter :].astype(F32)
    row, col, hit, weight, _ = routing(info, me_ref[0], top_count, limit, local_count)
    for kind, out_ref in enumerate((tok_ref, cot_ref)):
        place = placed(hit, row, col, kind)
        if kind == 1:
            place = place * weight
        out_ref[...] = sum(
            dot(side(place, col, p), rows_ref[:, p * quarter : (p + 1) * quarter], 0, 0)
            for p in range(2)
        ).astype(BF)


def plain_order(local_count):
    size = 8 * local_count
    i = iota((size, size), 0)
    quarter = i // (2 * local_count)
    rest = i % (2 * local_count)
    where = (rest >> 1) * 8 + quarter * 2 + (rest & 1)
    return (where == iota((size, size), 1)).astype(F32).astype(BF)


def quarters(local_count, refs):
    order = plain_order(local_count)
    slots = 2 * local_count
    blocks = [dot(order, ref[...]).astype(BF) for ref in refs]
    return [
        jnp.concatenate([block[q * slots : (q + 1) * slots] for block in blocks], axis=0)
        for q in range(4)
    ]


def put_parts(q, value, my_ref, their_refs):
    slots = value.shape[0] // (1 + len(their_refs))
    at = pl.ds(q * slots, slots)
    my_ref[at, :] = value[:slots]
    for b, ref in enumerate(their_refs):
        ref[at, :] = value[(b + 1) * slots : (b + 2) * slots].astype(BF)


def forward_kernel(local_count, *refs):
    rows, weights = refs[:4], refs[4:10]
    outs = refs[10:14]
    slope_ref, active_ref = refs[14:16]
    quarter = rows[0].shape[1]
    tok = quarters(local_count, rows)
    part = slope_ref.shape[1] // 2
    hidden = []
    for c in range(2):
        gate_ref, up_ref, _ = weights[3 * c : 3 * c + 3]
        gate_pre = up_pre = 0.0
        for q in range(4):
            at = pl.ds(q * quarter, quarter)
            gate_pre = gate_pre + dot(tok[q], gate_ref[at, :])
            up_pre = up_pre + dot(tok[q], up_ref[at, :])
        sig = 1.0 / (1.0 + jnp.exp(-gate_pre))
        active = gate_pre * sig
        hidden.append((active * up_pre).astype(BF))
        cols = pl.ds(c * part, part)
        slope_ref[:, cols] = up_pre * sig * (1.0 + gate_pre * (1.0 - sig))
        active_ref[:, cols] = active
    for q in range(4):
        cols = pl.ds(q * quarter, quarter)
        value = dot(hidden[0], weights[2][:, cols]) + dot(hidden[1], weights[5][:, cols])
        put_parts(q, value, outs[0], outs[1:])


def backward_kernel(local_count, *refs):
    rows, slope_ref, active_ref = refs[:4], refs[4], refs[5]
    weights, outs = refs[6:12], refs[12:16]
    quarter = rows[0].shape[1]
    cot = quarters(local_count, rows)
    part = slope_ref.shape[1] // 2
    grads = []
    for c in range(2):
        down_ref = weights[3 * c + 2]
        grad_hidden = 0.0
        for q in range(4):
            grad_hidden = grad_hidden + dot(cot[q], down_ref[:, q * quarter : (q + 1) * quarter], 1, 1)
        cols = pl.ds(c * part, part)
        grads.append((grad_hidden * slope_ref[:, cols]).astype(BF))
        grads.append((grad_hidden * active_ref[:, cols]).astype(BF))
    for q in range(4):
        at = pl.ds(q * quarter, quarter)
        value = 0.0
        for c in range(2):
            value = value + dot(grads[2 * c], weights[3 * c][at, :], 1, 1)
            value = value + dot(grads[2 * c + 1], weights[3 * c + 1][at, :], 1, 1)
        put_parts(q, value, outs[0], outs[1:])


def total_kernel(local_count, my_ref, *refs):
    total = my_ref[...]
    for ref in refs[:-1]:
        total = total + ref[...].astype(F32)
    refs[-1][...] = dot(plain_order(local_count), total.astype(BF), 0, 0).astype(BF)


def combine_kernel(top_count, limit, local_count, me_ref, rows_ref, out_back, grad_back, out_ref):
    quarter = out_back.shape[1]
    info = rows_ref[:, 2 * quarter :].astype(F32)
    row, col, hit, weight, picks = routing(info, me_ref[0], top_count, limit, local_count)
    place_out = placed(hit, row, col, 0) * weight
    place_grad = placed(hit, row, col, 1)
    pair_sum = 0.0
    for p in range(2):
        cols = pl.ds(p * quarter, quarter)
        grad_side = side(place_grad, col, p)
        value = dot(side(place_out, col, p), out_back[...]) + dot(grad_side, grad_back[...])
        out_ref[:, cols] = value.astype(BF)
        pair_sum = pair_sum + dot(rows_ref[:, cols], out_back[...], 1, 1) * grad_side.astype(F32)
    lane = iota((info.shape[0], LANES), 1)
    route = jnp.zeros((info.shape[0], LANES), F32)
    for k in range(top_count):
        value = jnp.sum(pair_sum * picks[k], axis=1, keepdims=True)
        route = route + jnp.where(lane == k, value, 0.0)
    out_ref[:, 2 * quarter :] = route.astype(BF)


def home_kernel(rows_ref, mixed_ref, grad_ref, route_ref, sum_ref):
    tok_rows, width = mixed_ref.shape
    half = width // 2
    size = 4 * tok_rows
    rows = rows_ref[...].astype(F32)
    total = rows[:size]
    for y in range(1, rows_ref.shape[0] // size):
        total = total + rows[y * size : (y + 1) * size]
    sum_ref[...] = total
    for h in range(2):
        cols = slice(h * half, (h + 1) * half)
        first = 2 * h * tok_rows
        mixed_ref[:, cols] = sum_ref[first : first + tok_rows, :half].astype(BF)
        grad_ref[:, cols] = sum_ref[first + tok_rows : first + 2 * tok_rows, :half].astype(BF)
    info = sum_ref[tok_rows : 2 * tok_rows, half:] + sum_ref[3 * tok_rows : 4 * tok_rows, half:]
    route_ref[...] = info[:, : route_ref.shape[1]].astype(BF)


def exchange(array, axis):
    return lax.all_to_all(array, axis, split_axis=0, concat_axis=0, tiled=True)


def call(kernel, outs, name, *args, scratch=(), smem=0, vmem=8, flops=0):
    single = isinstance(outs, jax.ShapeDtypeStruct)
    arrays = args + ((outs,) if single else outs)
    cost = pl.CostEstimate(
        flops=flops,
        bytes_accessed=sum(a.size * a.dtype.itemsize for a in arrays),
        transcendentals=0,
    )
    return pl.pallas_call(
        kernel,
        out_shape=outs,
        in_specs=[pl.BlockSpec(memory_space=pltpu.SMEM)] * smem + [VMEM] * (len(args) - smem),
        out_specs=VMEM if single else (VMEM,) * len(outs),
        scratch_shapes=scratch,
        compiler_params=pltpu.CompilerParams(vmem_limit_bytes=vmem * MIB),
        cost_estimate=cost,
        name=name,
    )(*args)


def after(array, earlier):
    return lax.optimization_barrier((array, earlier))[0]


def local(tokens, cotangent, expert_ids, node_groups, route_weight, w_gate, w_up, w_down):
    x_count = lax.axis_size("x")
    node_count = lax.axis_size("node")
    local_count = lax.axis_size("local")
    tok_rows, width = tokens.shape
    top_count = expert_ids.shape[1]
    limit = node_groups.shape[1]
    half, quarter = width // 2, width // 4
    hid_part = w_gate.shape[2]
    node_rows = 4 * tok_rows * node_count
    swap = [(0, 1), (1, 0)]
    me = lax.axis_index("node").reshape(1).astype(jnp.int32)
    sizes = (top_count, limit, local_count)

    def shape(rows, cols, dtype=BF):
        return jax.ShapeDtypeStruct((rows, cols), dtype)

    slot_shape = shape(8 * local_count, quarter)
    slot_shape_f = shape(8 * local_count, quarter, F32)
    node_shape = shape(node_rows, half + LANES)
    block_scratch = [pltpu.VMEM((4 * tok_rows, half + LANES), F32)]
    kept_shape = shape(2 * local_count * x_count, 2 * hid_part, F32)

    def spread(array):
        return [
            lax.ppermute(array, "x", [(i, (i + k) % x_count) for i in range(x_count)])
            for k in range(1, x_count)
        ]

    def give_back(arrays):
        return [
            lax.ppermute(array, "x", [(i, (i - k) % x_count) for i in range(x_count)])
            for k, array in enumerate(arrays, 1)
        ]

    payload = call(
        payload_kernel,
        node_shape,
        "payload",
        tokens,
        cotangent,
        expert_ids,
        node_groups,
        route_weight,
        scratch=block_scratch,
        vmem=56,
    )
    gathered = exchange(payload, "node")
    send_tok, send_cot = call(
        functools.partial(dispatch_kernel, *sizes),
        (slot_shape, slot_shape),
        "dispatch",
        me,
        gathered,
        smem=1,
        vmem=44,
    )

    own = [w_gate[0], w_up[0], w_down[0]]
    weights = own + [lax.ppermute(w, "core", swap) for w in own]

    tok = exchange(send_tok, "local")
    cot = exchange(send_cot, "local")
    toks = [tok] + spread(tok)
    cots = [cot] + spread(cot)
    toks[0] = after(toks[0], cot)
    my_out, *their_out, slope, active = call(
        functools.partial(forward_kernel, local_count),
        (slot_shape_f, slot_shape, slot_shape, slot_shape, kept_shape, kept_shape),
        "forward",
        *toks,
        *weights,
        vmem=24,
        flops=12 * kept_shape.size * width // 2,
    )
    out_parts = give_back(their_out)
    my_grad, *their_grad = call(
        functools.partial(backward_kernel, local_count),
        (slot_shape_f, slot_shape, slot_shape, slot_shape),
        "backward",
        *cots,
        slope,
        active,
        *weights,
        vmem=24,
        flops=12 * kept_shape.size * width // 2,
    )
    grad_parts = give_back(their_grad)
    my_out = after(my_out, my_grad)
    total = functools.partial(total_kernel, local_count)
    total_out = call(total, slot_shape, "total_out", my_out, *out_parts)
    out_back = exchange(total_out, "local")
    my_grad = after(my_grad, out_back)
    total_grad = call(total, slot_shape, "total_grad", my_grad, *grad_parts)
    grad_back = exchange(total_grad, "local")
    combined = call(
        functools.partial(combine_kernel, *sizes),
        node_shape,
        "combine",
        me,
        gathered,
        out_back,
        grad_back,
        smem=1,
    )
    home = exchange(combined, "node")
    return call(
        home_kernel,
        (shape(tok_rows, width), shape(tok_rows, width), shape(tok_rows, top_count)),
        "home",
        home,
        scratch=block_scratch,
    )


def solution(mesh):
    shape = mesh.devices.shape
    split = Mesh(
        np.asarray(mesh.devices).reshape((shape[0] // 2, 2) + shape[1:]),
        ("x", "core", "node", "local"),
    )
    row_spec = P(("x", "core", "node", "local"), None)
    return jax.shard_map(
        local,
        mesh=split,
        in_specs=(
            row_spec,
            row_spec,
            row_spec,
            row_spec,
            row_spec,
            P(("node", "local"), None, ("x", "core")),
            P(("node", "local"), None, ("x", "core")),
            P(("node", "local"), ("x", "core"), None),
        ),
        out_specs=(row_spec, row_spec, row_spec),
        check_vma=False,
    )
```

time: 222 us -> 183 us (0.82)
  blocking collectives: 98.4 us -> 41.4 us
  starting transfers between devices: 46.2 us -> 87.8 us
  waiting for transfers between devices: 49.3 us -> 35.2 us
  matrix products: 13.1 us -> 0 us
  Pallas kernels: 0 us -> 13.1 us
  local copies, waits for them, and re-layouts: 7.97 us -> 1.89 us
  other arithmetic: 3.4 us -> 0 us
    all_gather x3 -> x0, blocking collectives: 53.9 us -> none  [the longest x1 26.3 us: local(): gathered = lax.all_gather(payload, 'node', axis=0, tiled=True)]
    ppermute x3 -> x15, starting transfers between devices: 6.38 us -> 46.1 us  [the longest x6 20.3 us: give_back(): lax.ppermute(array, 'x', [(i, (i - k) % x_count) for i in range(x_count)])]
    all_to_all x5 -> x4, waiting for transfers between devices: 49.3 us -> 34 us  [exchange(): return lax.all_to_all(array, axis, split_axis=0, concat_axis=0, tiled=True)]
    pallas_call x0 -> x8, Pallas kernels: none -> 13.1 us  [call(): pl.pallas_call(kernel, out_shape=outs, in_specs=[pl.BlockSpec(memory_spac...]
    dot_general x17 -> x0, matrix products: 13.1 us -> none  [dot(): lax.dot_general(left_side, right_side, (((left_dim,), (right_dim,)), ((),...]
    all_to_all x8 -> x0, local copies, waits for them, and re-layouts: 5.36 us -> none  [the longest x2 1.56 us: local(): lax.all_to_all(send_tok, 'local', split_axis=0, concat_axis=0, tiled=True)]
    all_to_all x3 -> x2, blocking collectives: 44.5 us -> 41.4 us  [exchange(): return lax.all_to_all(array, axis, split_axis=0, concat_axis=0, tiled=True)]
    all_to_all x5 -> x4, starting transfers between devices: 39.9 us -> 41.7 us  [exchange(): return lax.all_to_all(array, axis, split_axis=0, concat_axis=0, tiled=True)]
  transfers between devices with their start and end apart: 8 -> 19, of which waited for: 5 -> 6; matrix products, arithmetic and copies ran while one was open for 3% -> 0% of each run, Pallas kernels for 0% -> 4%
where the time goes in v2:
time: 183 us; the launch traced here: 180 us
  starting transfers between devices  87.8 us (48%)
  blocking collectives  41.4 us (23%)
  waiting for transfers between devices  35.2 us (19%)
  Pallas kernels  13.1 us (7%)
  local copies, waits for them, and re-layouts  1.89 us (1%)
    all_to_all x4, starting transfers between devices, exchange(): return lax.all_to_all(array, axis, split_axis=0, concat_axis=0, tiled=True)  41.7 us
    all_to_all x2, blocking collectives, exchange(): return lax.all_to_all(array, axis, split_axis=0, concat_axis=0, tiled=True)  41.4 us
    all_to_all x4, waiting for transfers between devices, exchange(): return lax.all_to_all(array, axis, split_axis=0, concat_axis=0, tiled=True)  34 us
    ppermute x6, starting transfers between devices, give_back(): lax.ppermute(array, 'x', [(i, (i - k) % x_count) for i in range(x_count)])  20.3 us
    ppermute x6, starting transfers between devices, spread(): lax.ppermute(array, 'x', [(i, (i + k) % x_count) for i in range(x_count)])  19.5 us
    pallas_call x8, Pallas kernels, call(): pl.pallas_call(kernel, out_shape=outs, in_specs=[pl.BlockSpec(memory_spac...  13.1 us
    ppermute x3, starting transfers between devices, local(): weights = own + [lax.ppermute(w, 'core', swap) for w in own]  6.25 us
  transfers between devices with their start and end apart: 19, of which 6 were waited for; matrix products, arithmetic and copies ran while one was open for 0% of the time, Pallas kernels for 4%

profile of v2, /device:TPU:6, one launch (start us, length us, event | category | flops | bytes accessed | tf_op | source)
XLA Modules:
  0.0 180.4 jit_solution(8484392867898548759)
XLA Ops:
  0.7 1.7 payload.1
  2.3 7.1 %all-to-all-start = ((bf16[8,8,1920]{2,1,0:T(8,128)(2,1)}), bf16[8,8,1920]{2,1,0:T(8,128)(2,1)S(1)}, u32[]{:S(2)}, u32[]{:S(2)}) async-start(bf16[8,8,1920]{2,1,0:T(8,128)(2,1)} %bitcast.41), calls=%async_computation | async-start | bytes 491520 | tf_op jit(solution)/shard_map/all_to_all | solution.py:227
  9.4 11.5 %all-to-all-done = bf16[8,8,1920]{2,1,0:T(8,128)(2,1)S(1)} async-done(((bf16[8,8,1920]{2,1,0:T(8,128)(2,1)}), bf16[8,8,1920]{2,1,0:T(8,128)(2,1)S(1)}, u32[]{:S(2)}, u32[]{:S(2)}) %all-to-all-start) | async-done | bytes 245792 | tf_op jit(solution)/shard_map/all_to_all | solution.py:227
  21.0 1.3 dispatch.1
  23.0 18.9 %all-to-all-start.1 = ((bf16[16,8,896]{2,1,0:T(8,128)(2,1)}), bf16[16,8,896]{2,1,0:T(8,128)(2,1)S(1)}, u32[]{:S(2)}, u32[]{:S(2)}) async-start(bf16[16,8,896]{2,1,0:T(8,128)(2,1)} %bitcast.3), calls=%async_computation.1 | async-start | bytes 458752 | tf_op jit(solution)/shard_map/all_to_all | solution.py:227
  41.8 1.9 %collective-permute-start.3 = (bf16[3584,128]{1,0:T(8,128)(2,1)S(1)}, bf16[3584,128]{1,0:T(8,128)(2,1)S(1)}, u32[]{:S(2)}, u32[]{:S(2)}) collective-permute-start(bf16[3584,128]{1,0:T(8,128)(2,1)S(1)} %bitcast.16), channel_id=1, source_target_pairs={{0,128},{128,0},{1,129},{129,1},{2,130},{130,2},{3,131},{131,3},{4... | collective-permute-start | bytes 2752520 | tf_op jit(solution)/shard_map/ppermute | solution.py:313
  43.8 2.4 %collective-permute-start.4 = (bf16[3584,128]{1,0:T(8,128)(2,1)}, bf16[3584,128]{1,0:T(8,128)(2,1)}, u32[]{:S(2)}, u32[]{:S(2)}) collective-permute-start(bf16[3584,128]{1,0:T(8,128)(2,1)} %bitcast.19), channel_id=1, source_target_pairs={{0,128},{128,0},{1,129},{129,1},{2,130},{130,2},{3,131},{131,3},{4... | collective-permute-start | bytes 2752520 | tf_op jit(solution)/shard_map/ppermute | solution.py:313
  46.2 11.7 %all-to-all-done.1 = bf16[16,8,896]{2,1,0:T(8,128)(2,1)S(1)} async-done(((bf16[16,8,896]{2,1,0:T(8,128)(2,1)}), bf16[16,8,896]{2,1,0:T(8,128)(2,1)S(1)}, u32[]{:S(2)}, u32[]{:S(2)}) %all-to-all-start.1) | async-done | bytes 229408 | tf_op jit(solution)/shard_map/all_to_all | solution.py:227
  57.9 4.8 %all-to-all-start.2 = ((bf16[16,8,896]{2,1,0:T(8,128)(2,1)}), bf16[16,8,896]{2,1,0:T(8,128)(2,1)S(1)}, u32[]{:S(2)}, u32[]{:S(2)}) async-start(bf16[16,8,896]{2,1,0:T(8,128)(2,1)} %bitcast.40), calls=%async_computation.2 | async-start | bytes 458752 | tf_op jit(solution)/shard_map/all_to_all | solution.py:227
  62.8 1.9 %collective-permute-start.5 = (bf16[128,3584]{1,0:T(8,128)(2,1)}, bf16[128,3584]{1,0:T(8,128)(2,1)}, u32[]{:S(2)}, u32[]{:S(2)}) collective-permute-start(bf16[128,3584]{1,0:T(8,128)(2,1)} %bitcast.22), channel_id=1, source_target_pairs={{0,128},{128,0},{1,129},{129,1},{2,130},{130,2},{3,131},{131,3},{4... | collective-permute-start | bytes 2752520 | tf_op jit(solution)/shard_map/ppermute | solution.py:313
  64.7 2.7 %collective-permute-start.2 = (bf16[128,896]{1,0:T(8,128)(2,1)S(1)}, bf16[128,896]{1,0:T(8,128)(2,1)}, u32[]{:S(2)}, u32[]{:S(2)}) collective-permute-start(bf16[128,896]{1,0:T(8,128)(2,1)S(1)} %bitcast.35), channel_id=1, source_target_pairs={{0,768},{256,0},{512,256},{768,512},{1,769},{257,1},{513,257},{769... | collective-permute-start | bytes 688136 | tf_op jit(solution)/shard_map/ppermute | solution.py:279
  67.5 3.0 %collective-permute-start.1 = (bf16[128,896]{1,0:T(8,128)(2,1)S(1)}, bf16[128,896]{1,0:T(8,128)(2,1)}, u32[]{:S(2)}, u32[]{:S(2)}) collective-permute-start(bf16[128,896]{1,0:T(8,128)(2,1)S(1)} %bitcast.36), channel_id=1, source_target_pairs={{0,512},{256,768},{512,0},{768,256},{1,513},{257,769},{513,1},{769... | collective-permute-start | bytes 688136 | tf_op jit(solution)/shard_map/ppermute | solution.py:279
  70.5 4.0 %collective-permute-start = (bf16[128,896]{1,0:T(8,128)(2,1)S(1)}, bf16[128,896]{1,0:T(8,128)(2,1)}, u32[]{:S(2)}, u32[]{:S(2)}) collective-permute-start(bf16[128,896]{1,0:T(8,128)(2,1)S(1)} %bitcast.37), channel_id=1, source_target_pairs={{0,256},{256,512},{512,768},{768,0},{1,257},{257,513},{513,769},{7... | collective-permute-start | bytes 688136 | tf_op jit(solution)/shard_map/ppermute | solution.py:279
  74.5 3.9 %all-to-all-done.2 = bf16[16,8,896]{2,1,0:T(8,128)(2,1)S(1)} async-done(((bf16[16,8,896]{2,1,0:T(8,128)(2,1)}), bf16[16,8,896]{2,1,0:T(8,128)(2,1)S(1)}, u32[]{:S(2)}, u32[]{:S(2)}) %all-to-all-start.2) | async-done | bytes 229408 | tf_op jit(solution)/shard_map/all_to_all | solution.py:227
  78.4 2.7 %collective-permute-start.8 = (bf16[128,896]{1,0:T(8,128)(2,1)S(1)}, bf16[128,896]{1,0:T(8,128)(2,1)S(1)}, u32[]{:S(2)}, u32[]{:S(2)}) collective-permute-start(bf16[128,896]{1,0:T(8,128)(2,1)S(1)} %bitcast.31), channel_id=1, source_target_pairs={{0,768},{256,0},{512,256},{768,512},{1,769},{257,1},{513,257},{769... | collective-permute-start | bytes 688136 | tf_op jit(solution)/shard_map/ppermute | solution.py:279
  81.2 3.0 %collective-permute-start.7 = (bf16[128,896]{1,0:T(8,128)(2,1)S(1)}, bf16[128,896]{1,0:T(8,128)(2,1)S(1)}, u32[]{:S(2)}, u32[]{:S(2)}) collective-permute-start(bf16[128,896]{1,0:T(8,128)(2,1)S(1)} %bitcast.32), channel_id=1, source_target_pairs={{0,512},{256,768},{512,0},{768,256},{1,513},{257,769},{513,1},{769... | collective-permute-start | bytes 688136 | tf_op jit(solution)/shard_map/ppermute | solution.py:279
  84.2 4.0 %collective-permute-start.6 = (bf16[128,896]{1,0:T(8,128)(2,1)S(1)}, bf16[128,896]{1,0:T(8,128)(2,1)S(1)}, u32[]{:S(2)}, u32[]{:S(2)}) collective-permute-start(bf16[128,896]{1,0:T(8,128)(2,1)S(1)} %bitcast.33), channel_id=1, source_target_pairs={{0,256},{256,512},{512,768},{768,0},{1,257},{257,513},{513,769},{7... | collective-permute-start | bytes 688136 | tf_op jit(solution)/shard_map/ppermute | solution.py:279
  88.2 1.2 copy-done.2
  89.4 3.8 %forward.1 = (f32[128,896]{1,0:T(8,128)S(1)}, bf16[128,896]{1,0:T(8,128)(2,1)S(1)}, bf16[128,896]{1,0:T(8,128)(2,1)S(1)}, bf16[128,896]{1,0:T(8,128)(2,1)S(1)}, ...) custom-call(bf16[128,896]{1,0:T(8,128)(2,1)S(1)} %bitcast.38, bf16[128,896]{1,0:T(8,128)(2,1)} %collective-permute-done.refs_1_, ...), custom_call_target="tpu_custom_call" | custom-call | flops 704643072 | bytes 7831552 | tf_op jit(solution)/shard_map/forward/pallas_call | solution.py:238
  93.2 2.0 %collective-permute-start.9 = (bf16[128,896]{1,0:T(8,128)(2,1)S(1)}, bf16[128,896]{1,0:T(8,128)(2,1)S(1)}, u32[]{:S(2)}, u32[]{:S(2)}) collective-permute-start(bf16[128,896]{1,0:T(8,128)(2,1)S(1)} %get-tuple-element.26), channel_id=1, source_target_pairs={{0,768},{256,0},{512,256},{768,512},{1,769},{257,1},{513,257},{769... | collective-permute-start | bytes 688136 | tf_op jit(solution)/shard_map/ppermute | solution.py:285
  95.2 4.2 %collective-permute-start.10 = (bf16[128,896]{1,0:T(8,128)(2,1)S(1)}, bf16[128,896]{1,0:T(8,128)(2,1)S(1)}, u32[]{:S(2)}, u32[]{:S(2)}) collective-permute-start(bf16[128,896]{1,0:T(8,128)(2,1)S(1)} %get-tuple-element.27), channel_id=1, source_target_pairs={{0,512},{256,768},{512,0},{768,256},{1,513},{257,769},{513,1},{769... | collective-permute-start | bytes 688136 | tf_op jit(solution)/shard_map/ppermute | solution.py:285
  99.4 4.3 %collective-permute-start.11 = (bf16[128,896]{1,0:T(8,128)(2,1)S(1)}, bf16[128,896]{1,0:T(8,128)(2,1)S(1)}, u32[]{:S(2)}, u32[]{:S(2)}) collective-permute-start(bf16[128,896]{1,0:T(8,128)(2,1)S(1)} %get-tuple-element.28), channel_id=1, source_target_pairs={{0,256},{256,512},{512,768},{768,0},{1,257},{257,513},{513,769},{7... | collective-permute-start | bytes 688136 | tf_op jit(solution)/shard_map/ppermute | solution.py:285
  103.7 3.6 %backward.1 = (f32[128,896]{1,0:T(8,128)S(1)}, bf16[128,896]{1,0:T(8,128)(2,1)S(1)}, bf16[128,896]{1,0:T(8,128)(2,1)S(1)}, bf16[128,896]{1,0:T(8,128)(2,1)S(1)}) custom-call(bf16[128,896]{1,0:T(8,128)(2,1)S(1)} %bitcast.34, bf16[128,896]{1,0:T(8,128)(2,1)S(1)} %collective-permute-done.6.refs_1_, bf16[128,896]{1,0:T(8,128)(2,1)S(1)} %collective-permute-done.7.refs_2_, ...), custom_call_target="tpu_custom_call" | custom-call | flops 704643072 | bytes 7831552 | tf_op jit(solution)/shard_map/backward/pallas_call | solution.py:238
  108.1 1.0 total_out.1
  109.1 10.9 %all-to-all-start.3 = ((bf16[16,8,896]{2,1,0:T(8,128)(2,1)}), bf16[16,8,896]{2,1,0:T(8,128)(2,1)S(1)}, u32[]{:S(2)}, u32[]{:S(2)}) async-start(bf16[16,8,896]{2,1,0:T(8,128)(2,1)} %bitcast.10), calls=%async_computation.3 | async-start | bytes 458752 | tf_op jit(solution)/shard_map/all_to_all | solution.py:227
  120.0 2.8 %collective-permute-start.12 = (bf16[128,896]{1,0:T(8,128)(2,1)}, bf16[128,896]{1,0:T(8,128)(2,1)S(1)}, u32[]{:S(2)}, u32[]{:S(2)}) collective-permute-start(bf16[128,896]{1,0:T(8,128)(2,1)} %copy-done.7), channel_id=1, source_target_pairs={{0,768},{256,0},{512,256},{768,512},{1,769},{257,1},{513,257},{769... | collective-permute-start | bytes 688136 | tf_op jit(solution)/shard_map/ppermute | solution.py:285
  122.9 5.1 %collective-permute-start.13 = (bf16[128,896]{1,0:T(8,128)(2,1)}, bf16[128,896]{1,0:T(8,128)(2,1)S(1)}, u32[]{:S(2)}, u32[]{:S(2)}) collective-permute-start(bf16[128,896]{1,0:T(8,128)(2,1)} %copy-done.6), channel_id=1, source_target_pairs={{0,512},{256,768},{512,0},{768,256},{1,513},{257,769},{513,1},{769... | collective-permute-start | bytes 688136 | tf_op jit(solution)/shard_map/ppermute | solution.py:285
  128.0 1.9 %collective-permute-start.14 = (bf16[128,896]{1,0:T(8,128)(2,1)S(1)}, bf16[128,896]{1,0:T(8,128)(2,1)S(1)}, u32[]{:S(2)}, u32[]{:S(2)}) collective-permute-start(bf16[128,896]{1,0:T(8,128)(2,1)S(1)} %get-tuple-element.32), channel_id=1, source_target_pairs={{0,256},{256,512},{512,768},{768,0},{1,257},{257,513},{513,769},{7... | collective-permute-start | bytes 688136 | tf_op jit(solution)/shard_map/ppermute | solution.py:285
  129.9 6.9 %all-to-all-done.3 = bf16[16,8,896]{2,1,0:T(8,128)(2,1)S(1)} async-done(((bf16[16,8,896]{2,1,0:T(8,128)(2,1)}), bf16[16,8,896]{2,1,0:T(8,128)(2,1)S(1)}, u32[]{:S(2)}, u32[]{:S(2)}) %all-to-all-start.3) | async-done | bytes 229408 | tf_op jit(solution)/shard_map/all_to_all | solution.py:227
  137.5 28.4 %all_to_all.67 = bf16[16,8,896]{2,1,0:T(8,128)(2,1)S(1)} all-to-all(bf16[16,8,896]{2,1,0:T(8,128)(2,1)S(1)} %bitcast.39), channel_id=1, replica_groups=mesh['x'=4,'core'=2,'node'=8,'local'=16] {'local'}, dimensions={0} | all-to-all | bytes 458752 | tf_op jit(solution)/shard_map/all_to_all | solution.py:227
  165.8 0.9 combine.1
  166.7 13.1 %all_to_all.68 = bf16[8,8,1920]{2,1,0:T(8,128)(2,1)S(1)} all-to-all(bf16[8,8,1920]{2,1,0:T(8,128)(2,1)S(1)} %bitcast.27), channel_id=1, replica_groups=mesh['x'=4,'core'=2,'node'=8,'local'=16] {'node'}, dimensions={0} | all-to-all | bytes 491520 | tf_op jit(solution)/shard_map/all_to_all | solution.py:227
  (32 shorter events, 2.9 us)
Async XLA Ops:
  0.6 41.2 %copy-start = (bf16[1,3584,128]{2,1,0:T(8,128)(2,1)S(1)}, bf16[1,3584,128]{2,1,0:T(8,128)(2,1)}, u32[]{:S(2)}) copy-start(bf16[1,3584,128]{2,1,0:T(8,128)(2,1)} %param.13) | copy-start | bytes 2752516
  0.6 87.6 %copy-start.1 = (bf16[1,3584,128]{2,1,0:T(8,128)(2,1)S(1)}, bf16[1,3584,128]{2,1,0:T(8,128)(2,1)}, u32[]{:S(2)}) copy-start(bf16[1,3584,128]{2,1,0:T(8,128)(2,1)} %param.14) | copy-start | bytes 2752516
  2.3 18.6 %all-to-all-start = ((bf16[8,8,1920]{2,1,0:T(8,128)(2,1)}), bf16[8,8,1920]{2,1,0:T(8,128)(2,1)S(1)}, u32[]{:S(2)}, u32[]{:S(2)}) async-start(bf16[8,8,1920]{2,1,0:T(8,128)(2,1)} %bitcast.41), calls=%async_computation | async-start | bytes 491520 | tf_op jit(solution)/shard_map/all_to_all | solution.py:227
  22.3 0.7 copy-start.5
  23.0 35.0 %all-to-all-start.1 = ((bf16[16,8,896]{2,1,0:T(8,128)(2,1)}), bf16[16,8,896]{2,1,0:T(8,128)(2,1)S(1)}, u32[]{:S(2)}, u32[]{:S(2)}) async-start(bf16[16,8,896]{2,1,0:T(8,128)(2,1)} %bitcast.3), calls=%async_computation.1 | async-start | bytes 458752 | tf_op jit(solution)/shard_map/all_to_all | solution.py:227
  41.8 28.6 %collective-permute-start.3 = (bf16[3584,128]{1,0:T(8,128)(2,1)S(1)}, bf16[3584,128]{1,0:T(8,128)(2,1)S(1)}, u32[]{:S(2)}, u32[]{:S(2)}) collective-permute-start(bf16[3584,128]{1,0:T(8,128)(2,1)S(1)} %bitcast.16), channel_id=1, source_target_pairs={{0,128},{128,0},{1,129},{129,1},{2,130},{130,2},{3,131},{131,3},{4... | collective-permute-start | bytes 2752520 | tf_op jit(solution)/shard_map/ppermute | solution.py:313
  43.8 30.7 %collective-permute-start.4 = (bf16[3584,128]{1,0:T(8,128)(2,1)}, bf16[3584,128]{1,0:T(8,128)(2,1)}, u32[]{:S(2)}, u32[]{:S(2)}) collective-permute-start(bf16[3584,128]{1,0:T(8,128)(2,1)} %bitcast.19), channel_id=1, source_target_pairs={{0,128},{128,0},{1,129},{129,1},{2,130},{130,2},{3,131},{131,3},{4... | collective-permute-start | bytes 2752520 | tf_op jit(solution)/shard_map/ppermute | solution.py:313
  57.9 20.5 %all-to-all-start.2 = ((bf16[16,8,896]{2,1,0:T(8,128)(2,1)}), bf16[16,8,896]{2,1,0:T(8,128)(2,1)S(1)}, u32[]{:S(2)}, u32[]{:S(2)}) async-start(bf16[16,8,896]{2,1,0:T(8,128)(2,1)} %bitcast.40), calls=%async_computation.2 | async-start | bytes 458752 | tf_op jit(solution)/shard_map/all_to_all | solution.py:227
  62.8 18.4 %collective-permute-start.5 = (bf16[128,3584]{1,0:T(8,128)(2,1)}, bf16[128,3584]{1,0:T(8,128)(2,1)}, u32[]{:S(2)}, u32[]{:S(2)}) collective-permute-start(bf16[128,3584]{1,0:T(8,128)(2,1)} %bitcast.22), channel_id=1, source_target_pairs={{0,128},{128,0},{1,129},{129,1},{2,130},{130,2},{3,131},{131,3},{4... | collective-permute-start | bytes 2752520 | tf_op jit(solution)/shard_map/ppermute | solution.py:313
  64.7 19.5 %collective-permute-start.2 = (bf16[128,896]{1,0:T(8,128)(2,1)S(1)}, bf16[128,896]{1,0:T(8,128)(2,1)}, u32[]{:S(2)}, u32[]{:S(2)}) collective-permute-start(bf16[128,896]{1,0:T(8,128)(2,1)S(1)} %bitcast.35), channel_id=1, source_target_pairs={{0,768},{256,0},{512,256},{768,512},{1,769},{257,1},{513,257},{769... | collective-permute-start | bytes 688136 | tf_op jit(solution)/shard_map/ppermute | solution.py:279
  67.5 20.7 %collective-permute-start.1 = (bf16[128,896]{1,0:T(8,128)(2,1)S(1)}, bf16[128,896]{1,0:T(8,128)(2,1)}, u32[]{:S(2)}, u32[]{:S(2)}) collective-permute-start(bf16[128,896]{1,0:T(8,128)(2,1)S(1)} %bitcast.36), channel_id=1, source_target_pairs={{0,512},{256,768},{512,0},{768,256},{1,513},{257,769},{513,1},{769... | collective-permute-start | bytes 688136 | tf_op jit(solution)/shard_map/ppermute | solution.py:279
  70.5 17.7 %collective-permute-start = (bf16[128,896]{1,0:T(8,128)(2,1)S(1)}, bf16[128,896]{1,0:T(8,128)(2,1)}, u32[]{:S(2)}, u32[]{:S(2)}) collective-permute-start(bf16[128,896]{1,0:T(8,128)(2,1)S(1)} %bitcast.37), channel_id=1, source_target_pairs={{0,256},{256,512},{512,768},{768,0},{1,257},{257,513},{513,769},{7... | collective-permute-start | bytes 688136 | tf_op jit(solution)/shard_map/ppermute | solution.py:279
  78.4 21.0 %collective-permute-start.8 = (bf16[128,896]{1,0:T(8,128)(2,1)S(1)}, bf16[128,896]{1,0:T(8,128)(2,1)S(1)}, u32[]{:S(2)}, u32[]{:S(2)}) collective-permute-start(bf16[128,896]{1,0:T(8,128)(2,1)S(1)} %bitcast.31), channel_id=1, source_target_pairs={{0,768},{256,0},{512,256},{768,512},{1,769},{257,1},{513,257},{769... | collective-permute-start | bytes 688136 | tf_op jit(solution)/shard_map/ppermute | solution.py:279
  81.2 22.5 %collective-permute-start.7 = (bf16[128,896]{1,0:T(8,128)(2,1)S(1)}, bf16[128,896]{1,0:T(8,128)(2,1)S(1)}, u32[]{:S(2)}, u32[]{:S(2)}) collective-permute-start(bf16[128,896]{1,0:T(8,128)(2,1)S(1)} %bitcast.32), channel_id=1, source_target_pairs={{0,512},{256,768},{512,0},{768,256},{1,513},{257,769},{513,1},{769... | collective-permute-start | bytes 688136 | tf_op jit(solution)/shard_map/ppermute | solution.py:279
  84.2 19.5 %collective-permute-start.6 = (bf16[128,896]{1,0:T(8,128)(2,1)S(1)}, bf16[128,896]{1,0:T(8,128)(2,1)S(1)}, u32[]{:S(2)}, u32[]{:S(2)}) collective-permute-start(bf16[128,896]{1,0:T(8,128)(2,1)S(1)} %bitcast.33), channel_id=1, source_target_pairs={{0,256},{256,512},{512,768},{768,0},{1,257},{257,513},{513,769},{7... | collective-permute-start | bytes 688136 | tf_op jit(solution)/shard_map/ppermute | solution.py:279
  88.2 1.2 copy-start.2
  93.2 14.2 %collective-permute-start.9 = (bf16[128,896]{1,0:T(8,128)(2,1)S(1)}, bf16[128,896]{1,0:T(8,128)(2,1)S(1)}, u32[]{:S(2)}, u32[]{:S(2)}) collective-permute-start(bf16[128,896]{1,0:T(8,128)(2,1)S(1)} %get-tuple-element.26), channel_id=1, source_target_pairs={{0,768},{256,0},{512,256},{768,512},{1,769},{257,1},{513,257},{769... | collective-permute-start | bytes 688136 | tf_op jit(solution)/shard_map/ppermute | solution.py:285
  95.2 12.2 %collective-permute-start.10 = (bf16[128,896]{1,0:T(8,128)(2,1)S(1)}, bf16[128,896]{1,0:T(8,128)(2,1)S(1)}, u32[]{:S(2)}, u32[]{:S(2)}) collective-permute-start(bf16[128,896]{1,0:T(8,128)(2,1)S(1)} %get-tuple-element.27), channel_id=1, source_target_pairs={{0,512},{256,768},{512,0},{768,256},{1,513},{257,769},{513,1},{769... | collective-permute-start | bytes 688136 | tf_op jit(solution)/shard_map/ppermute | solution.py:285
  99.4 8.8 %collective-permute-start.11 = (bf16[128,896]{1,0:T(8,128)(2,1)S(1)}, bf16[128,896]{1,0:T(8,128)(2,1)S(1)}, u32[]{:S(2)}, u32[]{:S(2)}) collective-permute-start(bf16[128,896]{1,0:T(8,128)(2,1)S(1)} %get-tuple-element.28), channel_id=1, source_target_pairs={{0,256},{256,512},{512,768},{768,0},{1,257},{257,513},{513,769},{7... | collective-permute-start | bytes 688136 | tf_op jit(solution)/shard_map/ppermute | solution.py:285
  107.3 1.8 copy-start.3
  107.4 1.8 copy-start.6
  107.4 1.8 copy-start.7
  109.1 28.1 %copy-start.4 = (f32[128,896]{1,0:T(8,128)S(1)}, f32[128,896]{1,0:T(8,128)}, u32[]{:S(2)}) copy-start(f32[128,896]{1,0:T(8,128)} %copy-done.3) | copy-start | bytes 1376260
  109.1 27.6 %all-to-all-start.3 = ((bf16[16,8,896]{2,1,0:T(8,128)(2,1)}), bf16[16,8,896]{2,1,0:T(8,128)(2,1)S(1)}, u32[]{:S(2)}, u32[]{:S(2)}) async-start(bf16[16,8,896]{2,1,0:T(8,128)(2,1)} %bitcast.10), calls=%async_computation.3 | async-start | bytes 458752 | tf_op jit(solution)/shard_map/all_to_all | solution.py:227
  120.0 16.8 %collective-permute-start.12 = (bf16[128,896]{1,0:T(8,128)(2,1)}, bf16[128,896]{1,0:T(8,128)(2,1)S(1)}, u32[]{:S(2)}, u32[]{:S(2)}) collective-permute-start(bf16[128,896]{1,0:T(8,128)(2,1)} %copy-done.7), channel_id=1, source_target_pairs={{0,768},{256,0},{512,256},{768,512},{1,769},{257,1},{513,257},{769... | collective-permute-start | bytes 688136 | tf_op jit(solution)/shard_map/ppermute | solution.py:285
  122.9 13.9 %collective-permute-start.13 = (bf16[128,896]{1,0:T(8,128)(2,1)}, bf16[128,896]{1,0:T(8,128)(2,1)S(1)}, u32[]{:S(2)}, u32[]{:S(2)}) collective-permute-start(bf16[128,896]{1,0:T(8,128)(2,1)} %copy-done.6), channel_id=1, source_target_pairs={{0,512},{256,768},{512,0},{768,256},{1,513},{257,769},{513,1},{769... | collective-permute-start | bytes 688136 | tf_op jit(solution)/shard_map/ppermute | solution.py:285
  128.0 9.2 %collective-permute-start.14 = (bf16[128,896]{1,0:T(8,128)(2,1)S(1)}, bf16[128,896]{1,0:T(8,128)(2,1)S(1)}, u32[]{:S(2)}, u32[]{:S(2)}) collective-permute-start(bf16[128,896]{1,0:T(8,128)(2,1)S(1)} %get-tuple-element.32), channel_id=1, source_target_pairs={{0,256},{256,512},{512,768},{768,0},{1,257},{257,513},{513,769},{7... | collective-permute-start | bytes 688136 | tf_op jit(solution)/shard_map/ppermute | solution.py:285

commit v3 on v2

v3 whole, which is shorter than its diff:
```python
import functools

import jax
import jax.numpy as jnp
import numpy as np
from jax import lax
from jax.experimental import pallas as pl
from jax.experimental.pallas import tpu as pltpu
from jax.sharding import Mesh, PartitionSpec as P


BF = jnp.bfloat16
F32 = jnp.float32
LANES = 128
VMEM = pl.BlockSpec(memory_space=pltpu.VMEM)
MIB = 1024 * 1024


def dot(left_side, right_side, left_dim=1, right_dim=0):
    return lax.dot_general(
        left_side,
        right_side,
        (((left_dim,), (right_dim,)), ((), ())),
        preferred_element_type=F32,
    )


def iota(shape, dim):
    return lax.broadcasted_iota(jnp.int32, shape, dim)


def payload_kernel(tok_ref, cot_ref, ids_ref, groups_ref, weight_ref, out_ref, block_ref):
    tok_rows, width = tok_ref.shape
    half = width // 2
    lane = iota((tok_rows, LANES), 1)
    info = jnp.zeros((tok_rows, LANES), F32)
    place = 0
    for ref in (ids_ref, groups_ref, weight_ref):
        values = ref[...].astype(F32)
        for k in range(values.shape[1]):
            info = info + jnp.where(lane == place, values[:, k : k + 1], 0.0)
            place += 1
    for h in range(2):
        for kind, ref in enumerate((tok_ref, cot_ref)):
            at = pl.ds((2 * h + kind) * tok_rows, tok_rows)
            block_ref[at, :half] = ref[:, h * half : (h + 1) * half].astype(F32)
            block_ref[at, half:] = info
    block = block_ref[...].astype(BF)
    size = block.shape[0]
    for y in range(out_ref.shape[0] // size):
        out_ref[y * size : (y + 1) * size, :] = block


def routing(info, me, top_count, limit, local_count):
    shape = (info.shape[0], 8 * local_count)
    col = iota(shape, 1)
    row = iota(shape, 0)
    target = (me * local_count + (col >> 3)).astype(F32)
    listed = jnp.zeros((info.shape[0], 1), F32)
    for j in range(limit):
        match = info[:, top_count + j : top_count + j + 1] == me.astype(F32)
        listed = jnp.maximum(listed, match.astype(F32))
    first_weight = top_count + limit
    hit = jnp.zeros(shape, F32)
    weight = jnp.zeros(shape, F32)
    picks = []
    for k in range(top_count):
        match = (info[:, k : k + 1] == target).astype(F32) * listed
        picks.append(match)
        hit = hit + match
        weight = weight + match * info[:, first_weight + k : first_weight + k + 1]
    return row, col, hit, weight, picks


def placed(hit, col):
    rows = hit.shape[0]
    earlier = (iota((rows, rows), 1) < iota((rows, rows), 0)).astype(F32).astype(BF)
    before = dot(earlier, hit.astype(BF))
    return jnp.where(before == (col & 1).astype(F32), hit, 0.0)


def dispatch_kernel(top_count, limit, local_count, me_ref, rows_ref, out_ref):
    half = out_ref.shape[1]
    info = rows_ref[:, half:].astype(F32)
    row, col, hit, weight, _ = routing(info, me_ref[0], top_count, limit, local_count)
    same = ((row >> 1) & 3) == ((col >> 1) & 3)
    place = placed(jnp.where(same, hit, 0.0), col)
    scatter = jnp.where(((col >> 1) & 1) == 1, place * weight, place).astype(BF)
    out_ref[...] = dot(scatter, rows_ref[:, :half], 0, 0).astype(BF)


def plain_order(local_count):
    size = 8 * local_count
    i = iota((size, size), 0)
    quarter = i // (2 * local_count)
    rest = i % (2 * local_count)
    where = (rest >> 1) * 8 + quarter * 2 + (rest & 1)
    return (where == iota((size, size), 1)).astype(F32).astype(BF)


def join_kernel(*refs):
    gate_up, down = refs[6:]
    part = refs[0].shape[1]
    for c in range(2):
        for kind in range(2):
            gate_up[:, pl.ds((2 * kind + c) * part, part)] = refs[3 * c + kind][...]
        down[pl.ds(c * part, part), :] = refs[3 * c + 2][...]


def expert_kernel(local_count, blocks, *refs):
    rows, outs = refs[:blocks], refs[blocks + 2 :]
    gate_up, down = refs[blocks : blocks + 2]
    slots = 2 * local_count
    half = rows[0].shape[1]
    hidden_size = down.shape[0]
    order = plain_order(local_count)
    plain = [dot(order, ref[...]).astype(BF) for ref in rows]

    def every(h, kind):
        first = (2 * h + kind) * slots
        return jnp.concatenate([block[first : first + slots] for block in plain], axis=0)

    pre = dot(every(0, 0), gate_up[:half, :]) + dot(every(1, 0), gate_up[half:, :])
    gate_pre, up_pre = pre[:, :hidden_size], pre[:, hidden_size:]
    sig = 1.0 / (1.0 + jnp.exp(-gate_pre))
    active = gate_pre * sig
    hidden = (active * up_pre).astype(BF)
    grad_hidden = dot(every(0, 1), down[:, :half], 1, 1) + dot(every(1, 1), down[:, half:], 1, 1)
    grad_gate = (grad_hidden * up_pre * sig * (1.0 + gate_pre * (1.0 - sig))).astype(BF)
    grad_up = (grad_hidden * active).astype(BF)
    grads = jnp.concatenate([grad_gate, grad_up], axis=1)
    for h in range(2):
        cols = pl.ds(h * half, half)
        for kind, value in enumerate((dot(hidden, down[:, cols]), dot(grads, gate_up[cols, :], 1, 1))):
            at = pl.ds((2 * h + kind) * slots, slots)
            for b, ref in enumerate(outs):
                ref[at, :] = value[b * slots : (b + 1) * slots].astype(ref.dtype)


def near_sum_kernel(*refs):
    refs[-1][...] = sum(ref[...].astype(F32) for ref in refs[:-1])


def total_kernel(local_count, *refs):
    total = sum(ref[...].astype(F32) for ref in refs[:-1]).astype(BF)
    refs[-1][...] = dot(plain_order(local_count), total, 0, 0).astype(BF)


def combine_kernel(top_count, limit, local_count, me_ref, rows_ref, back_ref, out_ref):
    half = back_ref.shape[1]
    info = rows_ref[:, half:].astype(F32)
    row, col, hit, weight, picks = routing(info, me_ref[0], top_count, limit, local_count)
    same = ((row >> 1) & 3) == ((col >> 1) & 3)
    place = placed(jnp.where(same, hit, 0.0), col)
    gather = jnp.where(((col >> 1) & 1) == 0, place * weight, place).astype(BF)
    out_ref[:, :half] = dot(gather, back_ref[...]).astype(BF)
    crossed = (((row >> 1) & 3) == ((col >> 1) & 3) + 1) & (((row >> 1) & 1) == 1)
    place = placed(jnp.where(crossed, hit, 0.0), col)
    pair_sum = dot(rows_ref[:, :half], back_ref[...], 1, 1) * place
    lane = iota((info.shape[0], LANES), 1)
    route = jnp.zeros((info.shape[0], LANES), F32)
    for k in range(top_count):
        value = jnp.sum(pair_sum * picks[k], axis=1, keepdims=True)
        route = route + jnp.where(lane == k, value, 0.0)
    out_ref[:, half:] = route.astype(BF)


def home_kernel(rows_ref, mixed_ref, grad_ref, route_ref, sum_ref):
    tok_rows, width = mixed_ref.shape
    half = width // 2
    size = 4 * tok_rows
    rows = rows_ref[...].astype(F32)
    total = rows[:size]
    for y in range(1, rows_ref.shape[0] // size):
        total = total + rows[y * size : (y + 1) * size]
    sum_ref[...] = total
    for h in range(2):
        cols = slice(h * half, (h + 1) * half)
        first = 2 * h * tok_rows
        mixed_ref[:, cols] = sum_ref[first : first + tok_rows, :half].astype(BF)
        grad_ref[:, cols] = sum_ref[first + tok_rows : first + 2 * tok_rows, :half].astype(BF)
    info = sum_ref[tok_rows : 2 * tok_rows, half:] + sum_ref[3 * tok_rows : 4 * tok_rows, half:]
    route_ref[...] = info[:, : route_ref.shape[1]].astype(BF)


def exchange(array, axis):
    return lax.all_to_all(array, axis, split_axis=0, concat_axis=0, tiled=True)


def after(array, earlier):
    return lax.optimization_barrier((array, earlier))[0]


def call(kernel, outs, name, *args, scratch=(), smem=0, vmem=8, flops=0):
    single = isinstance(outs, jax.ShapeDtypeStruct)
    arrays = args + ((outs,) if single else outs)
    cost = pl.CostEstimate(
        flops=flops,
        bytes_accessed=sum(a.size * a.dtype.itemsize for a in arrays),
        transcendentals=0,
    )
    return pl.pallas_call(
        kernel,
        out_shape=outs,
        in_specs=[pl.BlockSpec(memory_space=pltpu.SMEM)] * smem + [VMEM] * (len(args) - smem),
        out_specs=VMEM if single else (VMEM,) * len(outs),
        scratch_shapes=scratch,
        compiler_params=pltpu.CompilerParams(vmem_limit_bytes=vmem * MIB),
        cost_estimate=cost,
        name=name,
    )(*args)


def local(tokens, cotangent, expert_ids, node_groups, route_weight, w_gate, w_up, w_down):
    x_count = lax.axis_size("x")
    node_count = lax.axis_size("node")
    local_count = lax.axis_size("local")
    tok_rows, width = tokens.shape
    top_count = expert_ids.shape[1]
    limit = node_groups.shape[1]
    half = width // 2
    hid_part = w_gate.shape[2]
    node_rows = 4 * tok_rows * node_count
    swap = [(0, 1), (1, 0)]
    me = lax.axis_index("node").reshape(1).astype(jnp.int32)
    sizes = (top_count, limit, local_count)

    def shape(rows, cols, dtype=BF):
        return jax.ShapeDtypeStruct((rows, cols), dtype)

    slot_shape = shape(8 * local_count, half)
    node_shape = shape(node_rows, half + LANES)
    block_scratch = [pltpu.VMEM((4 * tok_rows, half + LANES), F32)]

    def turn(array, k):
        return lax.ppermute(array, "x", [(i, (i + k) % x_count) for i in range(x_count)])

    payload = call(
        payload_kernel,
        node_shape,
        "payload",
        tokens,
        cotangent,
        expert_ids,
        node_groups,
        route_weight,
        scratch=block_scratch,
        vmem=56,
    )
    gathered = exchange(payload, "node")
    send = call(
        functools.partial(dispatch_kernel, *sizes), slot_shape, "dispatch", me, gathered, smem=1, vmem=44
    )

    own = [w_gate[0], w_up[0], w_down[0]]
    joined = call(
        join_kernel,
        (shape(width, 4 * hid_part), shape(2 * hid_part, width)),
        "join",
        *own,
        *[lax.ppermute(w, "core", swap) for w in own],
        vmem=20,
    )

    mine = after(exchange(send, "local"), joined[0])

    def experts(name, dtype, *blocks):
        return call(
            functools.partial(expert_kernel, local_count, len(blocks)),
            tuple(shape(*block.shape, dtype) for block in blocks),
            name,
            *blocks,
            *joined,
            vmem=16,
            flops=12 * len(blocks) * 2 * local_count * width * 2 * hid_part,
        )

    others = {k: turn(mine, k) for k in range(1, x_count)}
    (my_part,) = experts("mine", F32, mine)
    near = [k for k in others if k in (1, x_count - 1)]
    far = [k for k in others if k not in near]
    results = {}
    last = my_part
    for name, group in (("near", near), ("far", far)):
        if group:
            first, *rest = [others[k] for k in group]
            done = experts(name, BF, after(first, last), *rest)
            last = done[0]
            results[name] = [turn(part, -k) for k, part in zip(group, done)]
    near_sum = call(
        near_sum_kernel, shape(8 * local_count, half, F32), "near_sum", my_part, *results["near"]
    )
    total = call(
        functools.partial(total_kernel, local_count),
        slot_shape,
        "total",
        near_sum,
        *results.get("far", []),
    )
    back = exchange(total, "local")
    combined = call(
        functools.partial(combine_kernel, *sizes), node_shape, "combine", me, gathered, back, smem=1
    )
    home = exchange(combined, "node")
    return call(
        home_kernel,
        (shape(tok_rows, width), shape(tok_rows, width), shape(tok_rows, top_count)),
        "home",
        home,
        scratch=block_scratch,
    )


def solution(mesh):
    shape = mesh.devices.shape
    split = Mesh(
        np.asarray(mesh.devices).reshape((shape[0] // 2, 2) + shape[1:]),
        ("x", "core", "node", "local"),
    )
    row_spec = P(("x", "core", "node", "local"), None)
    return jax.shard_map(
        local,
        mesh=split,
        in_specs=(
            row_spec,
            row_spec,
            row_spec,
            row_spec,
            row_spec,
            P(("node", "local"), None, ("x", "core")),
            P(("node", "local"), None, ("x", "core")),
            P(("node", "local"), ("x", "core"), None),
        ),
        out_specs=(row_spec, row_spec, row_spec),
        check_vma=False,
    )
```

time: 183 us -> 160 us (0.87)
  starting transfers between devices: 87.8 us -> 51.6 us
  blocking collectives: 41.4 us -> 48.1 us
  local copies, waits for them, and re-layouts: 1.89 us -> 7.34 us
  Pallas kernels: 13.1 us -> 15.3 us
    ppermute x15 -> x9, starting transfers between devices: 46.1 us -> 25.6 us  [the longest x6 19.4 us: turn(): lax.ppermute(array, 'x', [(i, (i + k) % x_count) for i in range(x_count)])]
    all_to_all x4 -> x2, starting transfers between devices: 41.7 us -> 26 us  [exchange(): return lax.all_to_all(array, axis, split_axis=0, concat_axis=0, tiled=True)]
    all_to_all x4 -> x2, waiting for transfers between devices: 34 us -> 20.3 us  [exchange(): return lax.all_to_all(array, axis, split_axis=0, concat_axis=0, tiled=True)]
    ppermute x15 -> x9, waiting for transfers between devices: 1.2 us -> 13.7 us  [the longest x6 11.1 us: turn(): lax.ppermute(array, 'x', [(i, (i + k) % x_count) for i in range(x_count)])]
    all_to_all x2, blocking collectives: 41.4 us -> 48.1 us  [exchange(): return lax.all_to_all(array, axis, split_axis=0, concat_axis=0, tiled=True)]
    unnamed x16 -> x10, local copies, waits for them, and re-layouts: 1.89 us -> 7.34 us
    pallas_call x8 -> x10, Pallas kernels: 13.1 us -> 15.3 us  [call(): pl.pallas_call(kernel, out_shape=outs, in_specs=[pl.BlockSpec(memory_spac...]
  transfers between devices with their start and end apart: 19 -> 11, of which waited for: 6 -> 8; matrix products, arithmetic and copies ran while one was open for 0% -> 0% of each run, Pallas kernels for 4% -> 7%
where the time goes in v3:
time: 160 us; the launch traced here: 157 us
  starting transfers between devices  51.6 us (32%)
  blocking collectives  48.1 us (30%)
  waiting for transfers between devices  34.1 us (21%)
  Pallas kernels  15.3 us (10%)
  local copies, waits for them, and re-layouts  7.34 us (5%)
    all_to_all x2, blocking collectives, exchange(): return lax.all_to_all(array, axis, split_axis=0, concat_axis=0, tiled=True)  48.1 us
    all_to_all x2, starting transfers between devices, exchange(): return lax.all_to_all(array, axis, split_axis=0, concat_axis=0, tiled=True)  26 us
    all_to_all x2, waiting for transfers between devices, exchange(): return lax.all_to_all(array, axis, split_axis=0, concat_axis=0, tiled=True)  20.3 us
    ppermute x6, starting transfers between devices, turn(): lax.ppermute(array, 'x', [(i, (i + k) % x_count) for i in range(x_count)])  19.4 us
    pallas_call x10, Pallas kernels, call(): pl.pallas_call(kernel, out_shape=outs, in_specs=[pl.BlockSpec(memory_spac...  15.3 us
    ppermute x6, waiting for transfers between devices, turn(): lax.ppermute(array, 'x', [(i, (i + k) % x_count) for i in range(x_count)])  11.1 us
    unnamed x10, local copies, waits for them, and re-layouts  7.34 us
    ppermute x3, starting transfers between devices, local(): lax.ppermute(w, 'core', swap)  6.25 us
  transfers between devices with their start and end apart: 11, of which 8 were waited for; matrix products, arithmetic and copies ran while one was open for 0% of the time, Pallas kernels for 7%

profile of v3, /device:TPU:6, one launch (start us, length us, event | category | flops | bytes accessed | tf_op | source)
XLA Modules:
  0.0 157.1 jit_solution(13606873915125755536)
XLA Ops:
  0.6 1.6 payload.1
  2.2 7.1 %all-to-all-start = ((bf16[8,8,1920]{2,1,0:T(8,128)(2,1)}), bf16[8,8,1920]{2,1,0:T(8,128)(2,1)S(1)}, u32[]{:S(2)}, u32[]{:S(2)}) async-start(bf16[8,8,1920]{2,1,0:T(8,128)(2,1)} %bitcast.28), calls=%async_computation | async-start | bytes 491520 | tf_op jit(solution)/shard_map/all_to_all | solution.py:187
  9.3 11.5 %all-to-all-done = bf16[8,8,1920]{2,1,0:T(8,128)(2,1)S(1)} async-done(((bf16[8,8,1920]{2,1,0:T(8,128)(2,1)}), bf16[8,8,1920]{2,1,0:T(8,128)(2,1)S(1)}, u32[]{:S(2)}, u32[]{:S(2)}) %all-to-all-start) | async-done | bytes 245792 | tf_op jit(solution)/shard_map/all_to_all | solution.py:187
  20.8 1.4 dispatch.1
  22.2 18.9 %all-to-all-start.1 = ((bf16[16,8,1792]{2,1,0:T(8,128)(2,1)}), bf16[16,8,1792]{2,1,0:T(8,128)(2,1)S(1)}, u32[]{:S(2)}, u32[]{:S(2)}) async-start(bf16[16,8,1792]{2,1,0:T(8,128)(2,1)} %bitcast.3), calls=%async_computation.1 | async-start | bytes 917504 | tf_op jit(solution)/shard_map/all_to_all | solution.py:187
  41.1 1.9 %collective-permute-start = (bf16[3584,128]{1,0:T(8,128)(2,1)}, bf16[3584,128]{1,0:T(8,128)(2,1)S(1)}, u32[]{:S(2)}, u32[]{:S(2)}) collective-permute-start(bf16[3584,128]{1,0:T(8,128)(2,1)} %bitcast.22), channel_id=1, source_target_pairs={{0,128},{128,0},{1,129},{129,1},{2,130},{130,2},{3,131},{131,3},{4... | collective-permute-start | bytes 2752520 | tf_op jit(solution)/shard_map/ppermute | solution.py:261
  43.0 2.4 %collective-permute-start.1 = (bf16[3584,128]{1,0:T(8,128)(2,1)}, bf16[3584,128]{1,0:T(8,128)(2,1)S(1)}, u32[]{:S(2)}, u32[]{:S(2)}) collective-permute-start(bf16[3584,128]{1,0:T(8,128)(2,1)} %bitcast.24), channel_id=1, source_target_pairs={{0,128},{128,0},{1,129},{129,1},{2,130},{130,2},{3,131},{131,3},{4... | collective-permute-start | bytes 2752520 | tf_op jit(solution)/shard_map/ppermute | solution.py:261
  45.4 1.9 %collective-permute-start.2 = (bf16[128,3584]{1,0:T(8,128)(2,1)}, bf16[128,3584]{1,0:T(8,128)(2,1)S(1)}, u32[]{:S(2)}, u32[]{:S(2)}) collective-permute-start(bf16[128,3584]{1,0:T(8,128)(2,1)} %bitcast.26), channel_id=1, source_target_pairs={{0,128},{128,0},{1,129},{129,1},{2,130},{130,2},{3,131},{131,3},{4... | collective-permute-start | bytes 2752520 | tf_op jit(solution)/shard_map/ppermute | solution.py:261
  47.7 2.3 %collective-permute-done.2.refs_5_ = bf16[128,3584]{1,0:T(8,128)(2,1)S(1)} collective-permute-done((bf16[128,3584]{1,0:T(8,128)(2,1)}, bf16[128,3584]{1,0:T(8,128)(2,1)S(1)}, u32[]{:S(2)}, u32[]{:S(2)}) %collective-permute-start.2) | collective-permute-done | bytes 917536 | tf_op jit(solution)/shard_map/ppermute | solution.py:261
  50.0 1.2 copy-done.2
  51.2 1.2 copy-done.3
  52.4 1.2 copy-done.4
  53.5 0.7 join.1
  54.3 1.8 %copy-done = bf16[3584,512]{1,0:T(8,128)(2,1)} copy-done((bf16[3584,512]{1,0:T(8,128)(2,1)}, bf16[3584,512]{1,0:T(8,128)(2,1)S(1)}, u32[]{:S(2)}) %copy-start) | copy-done | bytes 3670040
  56.1 8.8 %all-to-all-done.1 = bf16[16,8,1792]{2,1,0:T(8,128)(2,1)S(1)} async-done(((bf16[16,8,1792]{2,1,0:T(8,128)(2,1)}), bf16[16,8,1792]{2,1,0:T(8,128)(2,1)S(1)}, u32[]{:S(2)}, u32[]{:S(2)}) %all-to-all-start.1) | async-done | bytes 458784 | tf_op jit(solution)/shard_map/all_to_all | solution.py:187
  64.9 2.4 %collective-permute-start.3 = (bf16[128,1792]{1,0:T(8,128)(2,1)S(1)}, bf16[128,1792]{1,0:T(8,128)(2,1)S(1)}, u32[]{:S(2)}, u32[]{:S(2)}) collective-permute-start(bf16[128,1792]{1,0:T(8,128)(2,1)S(1)} %bitcast.16), channel_id=1, source_target_pairs={{0,256},{256,512},{512,768},{768,0},{1,257},{257,513},{513,769},{7... | collective-permute-start | bytes 1376264 | tf_op jit(solution)/shard_map/ppermute | solution.py:236
  67.3 3.4 %collective-permute-start.4 = (bf16[128,1792]{1,0:T(8,128)(2,1)S(1)}, bf16[128,1792]{1,0:T(8,128)(2,1)S(1)}, u32[]{:S(2)}, u32[]{:S(2)}) collective-permute-start(bf16[128,1792]{1,0:T(8,128)(2,1)S(1)} %bitcast.17), channel_id=1, source_target_pairs={{0,768},{256,0},{512,256},{768,512},{1,769},{257,1},{513,257},{769... | collective-permute-start | bytes 1376264 | tf_op jit(solution)/shard_map/ppermute | solution.py:236
  70.7 3.3 %collective-permute-start.7 = (bf16[128,1792]{1,0:T(8,128)(2,1)S(1)}, bf16[128,1792]{1,0:T(8,128)(2,1)S(1)}, u32[]{:S(2)}, u32[]{:S(2)}) collective-permute-start(bf16[128,1792]{1,0:T(8,128)(2,1)S(1)} %bitcast.18), channel_id=1, source_target_pairs={{0,512},{256,768},{512,0},{768,256},{1,513},{257,769},{513,1},{769... | collective-permute-start | bytes 1376264 | tf_op jit(solution)/shard_map/ppermute | solution.py:236
  74.1 2.0 %copy-done.1 = bf16[3584,512]{1,0:T(8,128)(2,1)S(1)} copy-done((bf16[3584,512]{1,0:T(8,128)(2,1)S(1)}, bf16[3584,512]{1,0:T(8,128)(2,1)}, u32[]{:S(2)}) %copy-start.1) | copy-done | bytes 3670040
  76.1 3.1 %mine.1.refs_0_ = f32[128,1792]{1,0:T(8,128)S(1)} custom-call(bf16[128,1792]{1,0:T(8,128)(2,1)S(1)} %bitcast.19, bf16[3584,512]{1,0:T(8,128)(2,1)S(1)} %copy-done.1, bf16[256,3584]{1,0:T(8,128)(2,1)S(1)} %get-tuple-element.12.refs_2_.refs_3_), custom_call_target="tpu_custom_call" | custom-call | flops 352321536 | bytes 6881280 | tf_op jit(solution)/shard_map/mine/pallas_call | solution.py:202
  79.2 2.5 %collective-permute-done.4.refs_1_ = bf16[128,1792]{1,0:T(8,128)(2,1)S(1)} collective-permute-done((bf16[128,1792]{1,0:T(8,128)(2,1)S(1)}, bf16[128,1792]{1,0:T(8,128)(2,1)S(1)}, u32[]{:S(2)}, u32[]{:S(2)}) %collective-permute-start.4) | collective-permute-done | bytes 458784 | tf_op jit(solution)/shard_map/ppermute | solution.py:236
  81.7 3.5 %near.1 = (bf16[128,1792]{1,0:T(8,128)(2,1)S(1)}, bf16[128,1792]{1,0:T(8,128)(2,1)S(1)}) custom-call(bf16[128,1792]{1,0:T(8,128)(2,1)S(1)} %collective-permute-done.3.refs_0_, bf16[128,1792]{1,0:T(8,128)(2,1)S(1)} %collective-permute-done.4.refs_1_, bf16[3584,512]{1,0:T(8,128)(2,1)S(1)} %copy-done.1, bf16[256,3584]{1,0:T(8,128)(2,1)S(1)} %get-tuple-element.12.refs_2_.refs_3_), custom_call_target="tpu_custom_call" | custom-call | flops 704643072 | bytes 7340032 | tf_op jit(solution)/shard_map/near/pallas_call | solution.py:202
  85.1 2.8 %collective-permute-start.5 = (bf16[128,1792]{1,0:T(8,128)(2,1)S(1)}, bf16[128,1792]{1,0:T(8,128)(2,1)S(1)}, u32[]{:S(2)}, u32[]{:S(2)}) collective-permute-start(bf16[128,1792]{1,0:T(8,128)(2,1)S(1)} %get-tuple-element.14), channel_id=1, source_target_pairs={{0,768},{256,0},{512,256},{768,512},{1,769},{257,1},{513,257},{769... | collective-permute-start | bytes 1376264 | tf_op jit(solution)/shard_map/ppermute | solution.py:236
  88.0 1.5 collective-permute-done.7.refs_0_
  89.5 2.7 %collective-permute-start.6 = (bf16[128,1792]{1,0:T(8,128)(2,1)S(1)}, bf16[128,1792]{1,0:T(8,128)(2,1)S(1)}, u32[]{:S(2)}, u32[]{:S(2)}) collective-permute-start(bf16[128,1792]{1,0:T(8,128)(2,1)S(1)} %get-tuple-element.15), channel_id=1, source_target_pairs={{0,256},{256,512},{512,768},{768,0},{1,257},{257,513},{513,769},{7... | collective-permute-start | bytes 1376264 | tf_op jit(solution)/shard_map/ppermute | solution.py:236
  92.2 3.1 %far.1 = bf16[128,1792]{1,0:T(8,128)(2,1)S(1)} custom-call(bf16[128,1792]{1,0:T(8,128)(2,1)S(1)} %collective-permute-done.7.refs_0_, bf16[3584,512]{1,0:T(8,128)(2,1)S(1)} %copy-done.1, bf16[256,3584]{1,0:T(8,128)(2,1)S(1)} %get-tuple-element.12.refs_2_.refs_3_), custom_call_target="tpu_custom_call" | custom-call | flops 352321536 | bytes 6422528 | tf_op jit(solution)/shard_map/far/pallas_call | solution.py:202
  95.3 4.7 %collective-permute-start.8 = (bf16[128,1792]{1,0:T(8,128)(2,1)S(1)}, bf16[128,1792]{1,0:T(8,128)(2,1)S(1)}, u32[]{:S(2)}, u32[]{:S(2)}) collective-permute-start(bf16[128,1792]{1,0:T(8,128)(2,1)S(1)} %far.1), channel_id=1, source_target_pairs={{0,512},{256,768},{512,0},{768,256},{1,513},{257,769},{513,1},{769... | collective-permute-start | bytes 1376264 | tf_op jit(solution)/shard_map/ppermute | solution.py:236
  100.0 1.0 collective-permute-done.6.refs_2_
  101.1 6.1 %collective-permute-done.8.refs_1_ = bf16[128,1792]{1,0:T(8,128)(2,1)S(1)} collective-permute-done((bf16[128,1792]{1,0:T(8,128)(2,1)S(1)}, bf16[128,1792]{1,0:T(8,128)(2,1)S(1)}, u32[]{:S(2)}, u32[]{:S(2)}) %collective-permute-start.8) | collective-permute-done | bytes 458784 | tf_op jit(solution)/shard_map/ppermute | solution.py:236
  107.6 33.0 %all_to_all.45 = bf16[16,8,1792]{2,1,0:T(8,128)(2,1)S(1)} all-to-all(bf16[16,8,1792]{2,1,0:T(8,128)(2,1)S(1)} %bitcast.14), channel_id=1, replica_groups=mesh['x'=4,'core'=2,'node'=8,'local'=16] {'local'}, dimensions={0} | all-to-all | bytes 917504 | tf_op jit(solution)/shard_map/all_to_all | solution.py:187
  140.6 0.8 combine.1
  141.4 15.0 %all_to_all.46 = bf16[8,8,1920]{2,1,0:T(8,128)(2,1)S(1)} all-to-all(bf16[8,8,1920]{2,1,0:T(8,128)(2,1)S(1)} %bitcast.21), channel_id=1, replica_groups=mesh['x'=4,'core'=2,'node'=8,'local'=16] {'node'}, dimensions={0} | all-to-all | bytes 491520 | tf_op jit(solution)/shard_map/all_to_all | solution.py:187
  (12 shorter events, 1.5 us)
Async XLA Ops:
  2.2 18.6 %all-to-all-start = ((bf16[8,8,1920]{2,1,0:T(8,128)(2,1)}), bf16[8,8,1920]{2,1,0:T(8,128)(2,1)S(1)}, u32[]{:S(2)}, u32[]{:S(2)}) async-start(bf16[8,8,1920]{2,1,0:T(8,128)(2,1)} %bitcast.28), calls=%async_computation | async-start | bytes 491520 | tf_op jit(solution)/shard_map/all_to_all | solution.py:187
  22.2 42.7 %all-to-all-start.1 = ((bf16[16,8,1792]{2,1,0:T(8,128)(2,1)}), bf16[16,8,1792]{2,1,0:T(8,128)(2,1)S(1)}, u32[]{:S(2)}, u32[]{:S(2)}) async-start(bf16[16,8,1792]{2,1,0:T(8,128)(2,1)} %bitcast.3), calls=%async_computation.1 | async-start | bytes 917504 | tf_op jit(solution)/shard_map/all_to_all | solution.py:187
  41.1 6.3 %collective-permute-start = (bf16[3584,128]{1,0:T(8,128)(2,1)}, bf16[3584,128]{1,0:T(8,128)(2,1)S(1)}, u32[]{:S(2)}, u32[]{:S(2)}) collective-permute-start(bf16[3584,128]{1,0:T(8,128)(2,1)} %bitcast.22), channel_id=1, source_target_pairs={{0,128},{128,0},{1,129},{129,1},{2,130},{130,2},{3,131},{131,3},{4... | collective-permute-start | bytes 2752520 | tf_op jit(solution)/shard_map/ppermute | solution.py:261
  43.0 4.7 %collective-permute-start.1 = (bf16[3584,128]{1,0:T(8,128)(2,1)}, bf16[3584,128]{1,0:T(8,128)(2,1)S(1)}, u32[]{:S(2)}, u32[]{:S(2)}) collective-permute-start(bf16[3584,128]{1,0:T(8,128)(2,1)} %bitcast.24), channel_id=1, source_target_pairs={{0,128},{128,0},{1,129},{129,1},{2,130},{130,2},{3,131},{131,3},{4... | collective-permute-start | bytes 2752520 | tf_op jit(solution)/shard_map/ppermute | solution.py:261
  45.4 4.6 %collective-permute-start.2 = (bf16[128,3584]{1,0:T(8,128)(2,1)}, bf16[128,3584]{1,0:T(8,128)(2,1)S(1)}, u32[]{:S(2)}, u32[]{:S(2)}) collective-permute-start(bf16[128,3584]{1,0:T(8,128)(2,1)} %bitcast.26), channel_id=1, source_target_pairs={{0,128},{128,0},{1,129},{129,1},{2,130},{130,2},{3,131},{131,3},{4... | collective-permute-start | bytes 2752520 | tf_op jit(solution)/shard_map/ppermute | solution.py:261
  50.0 1.2 copy-start.2
  51.2 1.2 copy-start.3
  52.4 1.2 copy-start.4
  54.3 1.8 %copy-start = (bf16[3584,512]{1,0:T(8,128)(2,1)}, bf16[3584,512]{1,0:T(8,128)(2,1)S(1)}, u32[]{:S(2)}) copy-start(bf16[3584,512]{1,0:T(8,128)(2,1)S(1)} %get-tuple-element.10.refs_1_.refs_2_) | copy-start | bytes 11010052
  64.9 14.3 %collective-permute-start.3 = (bf16[128,1792]{1,0:T(8,128)(2,1)S(1)}, bf16[128,1792]{1,0:T(8,128)(2,1)S(1)}, u32[]{:S(2)}, u32[]{:S(2)}) collective-permute-start(bf16[128,1792]{1,0:T(8,128)(2,1)S(1)} %bitcast.16), channel_id=1, source_target_pairs={{0,256},{256,512},{512,768},{768,0},{1,257},{257,513},{513,769},{7... | collective-permute-start | bytes 1376264 | tf_op jit(solution)/shard_map/ppermute | solution.py:236
  67.3 14.4 %collective-permute-start.4 = (bf16[128,1792]{1,0:T(8,128)(2,1)S(1)}, bf16[128,1792]{1,0:T(8,128)(2,1)S(1)}, u32[]{:S(2)}, u32[]{:S(2)}) collective-permute-start(bf16[128,1792]{1,0:T(8,128)(2,1)S(1)} %bitcast.17), channel_id=1, source_target_pairs={{0,768},{256,0},{512,256},{768,512},{1,769},{257,1},{513,257},{769... | collective-permute-start | bytes 1376264 | tf_op jit(solution)/shard_map/ppermute | solution.py:236
  70.7 18.8 %collective-permute-start.7 = (bf16[128,1792]{1,0:T(8,128)(2,1)S(1)}, bf16[128,1792]{1,0:T(8,128)(2,1)S(1)}, u32[]{:S(2)}, u32[]{:S(2)}) collective-permute-start(bf16[128,1792]{1,0:T(8,128)(2,1)S(1)} %bitcast.18), channel_id=1, source_target_pairs={{0,512},{256,768},{512,0},{768,256},{1,513},{257,769},{513,1},{769... | collective-permute-start | bytes 1376264 | tf_op jit(solution)/shard_map/ppermute | solution.py:236
  74.0 2.0 %copy-start.1 = (bf16[3584,512]{1,0:T(8,128)(2,1)S(1)}, bf16[3584,512]{1,0:T(8,128)(2,1)}, u32[]{:S(2)}) copy-start(bf16[3584,512]{1,0:T(8,128)(2,1)} %copy-done) | copy-start | bytes 11010052
  85.1 15.9 %collective-permute-start.5 = (bf16[128,1792]{1,0:T(8,128)(2,1)S(1)}, bf16[128,1792]{1,0:T(8,128)(2,1)S(1)}, u32[]{:S(2)}, u32[]{:S(2)}) collective-permute-start(bf16[128,1792]{1,0:T(8,128)(2,1)S(1)} %get-tuple-element.14), channel_id=1, source_target_pairs={{0,768},{256,0},{512,256},{768,512},{1,769},{257,1},{513,257},{769... | collective-permute-start | bytes 1376264 | tf_op jit(solution)/shard_map/ppermute | solution.py:236
  89.5 11.5 %collective-permute-start.6 = (bf16[128,1792]{1,0:T(8,128)(2,1)S(1)}, bf16[128,1792]{1,0:T(8,128)(2,1)S(1)}, u32[]{:S(2)}, u32[]{:S(2)}) collective-permute-start(bf16[128,1792]{1,0:T(8,128)(2,1)S(1)} %get-tuple-element.15), channel_id=1, source_target_pairs={{0,256},{256,512},{512,768},{768,0},{1,257},{257,513},{513,769},{7... | collective-permute-start | bytes 1376264 | tf_op jit(solution)/shard_map/ppermute | solution.py:236
  95.3 11.9 %collective-permute-start.8 = (bf16[128,1792]{1,0:T(8,128)(2,1)S(1)}, bf16[128,1792]{1,0:T(8,128)(2,1)S(1)}, u32[]{:S(2)}, u32[]{:S(2)}) collective-permute-start(bf16[128,1792]{1,0:T(8,128)(2,1)S(1)} %far.1), channel_id=1, source_target_pairs={{0,512},{256,768},{512,0},{768,256},{1,513},{257,769},{513,1},{769... | collective-permute-start | bytes 1376264 | tf_op jit(solution)/shard_map/ppermute | solution.py:236

commit v4 on v3

--- a/solution.py
+++ b/solution.py
@@ -275,10 +275,11 @@
             flops=12 * len(blocks) * 2 * local_count * width * 2 * hid_part,
         )
 
-    others = {k: turn(mine, k) for k in range(1, x_count)}
+    near = sorted({1, x_count - 1})
+    far = [k for k in range(1, x_count) if k not in near]
+    others = {k: turn(mine, k) for k in near}
     (my_part,) = experts("mine", F32, mine)
-    near = [k for k in others if k in (1, x_count - 1)]
-    far = [k for k in others if k not in near]
+    others.update({k: turn(after(mine, my_part), k) for k in far})
     results = {}
     last = my_part
     for name, group in (("near", near), ("far", far)):

time: 160 us -> 160 us (level)
  waiting for transfers between devices: 34.1 us -> 40.9 us
  blocking collectives: 48.1 us -> 43.5 us
  starting transfers between devices: 51.6 us -> 49.9 us
    ppermute x6, waiting for transfers between devices: 11.1 us -> 18 us  [turn(): lax.ppermute(array, 'x', [(i, (i + k) % x_count) for i in range(x_count)])]
    all_to_all x2, blocking collectives: 48.1 us -> 43.5 us  [exchange(): return lax.all_to_all(array, axis, split_axis=0, concat_axis=0, tiled=True)]
    ppermute x6, starting transfers between devices: 19.4 us -> 17.7 us  [turn(): lax.ppermute(array, 'x', [(i, (i + k) % x_count) for i in range(x_count)])]
where the time goes in v4:
time: 160 us; the launch traced here: 158 us
  starting transfers between devices  49.9 us (31%)
  blocking collectives  43.5 us (27%)
  waiting for transfers between devices  40.9 us (26%)
  Pallas kernels  15.3 us (10%)
  local copies, waits for them, and re-layouts  7.34 us (5%)
    all_to_all x2, blocking collectives, exchange(): return lax.all_to_all(array, axis, split_axis=0, concat_axis=0, tiled=True)  43.5 us
    all_to_all x2, starting transfers between devices, exchange(): return lax.all_to_all(array, axis, split_axis=0, concat_axis=0, tiled=True)  26 us
    all_to_all x2, waiting for transfers between devices, exchange(): return lax.all_to_all(array, axis, split_axis=0, concat_axis=0, tiled=True)  20.3 us
    ppermute x6, waiting for transfers between devices, turn(): lax.ppermute(array, 'x', [(i, (i + k) % x_count) for i in range(x_count)])  18 us
    ppermute x6, starting transfers between devices, turn(): lax.ppermute(array, 'x', [(i, (i + k) % x_count) for i in range(x_count)])  17.7 us
    pallas_call x10, Pallas kernels, call(): pl.pallas_call(kernel, out_shape=outs, in_specs=[pl.BlockSpec(memory_spac...  15.3 us
    unnamed x10, local copies, waits for them, and re-layouts  7.34 us
    ppermute x3, starting transfers between devices, local(): lax.ppermute(w, 'core', swap)  6.25 us
  transfers between devices with their start and end apart: 11, of which 8 were waited for; matrix products, arithmetic and copies ran while one was open for 0% of the time, Pallas kernels for 7%

profile of v4, /device:TPU:6, one launch (start us, length us, event | category | flops | bytes accessed | tf_op | source)
XLA Modules:
  0.0 157.7 jit_solution(14101682837581770528)
XLA Ops:
  0.6 1.6 payload.1
  2.2 7.1 %all-to-all-start = ((bf16[8,8,1920]{2,1,0:T(8,128)(2,1)}), bf16[8,8,1920]{2,1,0:T(8,128)(2,1)S(1)}, u32[]{:S(2)}, u32[]{:S(2)}) async-start(bf16[8,8,1920]{2,1,0:T(8,128)(2,1)} %bitcast.28), calls=%async_computation | async-start | bytes 491520 | tf_op jit(solution)/shard_map/all_to_all | solution.py:187
  9.3 11.5 %all-to-all-done = bf16[8,8,1920]{2,1,0:T(8,128)(2,1)S(1)} async-done(((bf16[8,8,1920]{2,1,0:T(8,128)(2,1)}), bf16[8,8,1920]{2,1,0:T(8,128)(2,1)S(1)}, u32[]{:S(2)}, u32[]{:S(2)}) %all-to-all-start) | async-done | bytes 245792 | tf_op jit(solution)/shard_map/all_to_all | solution.py:187
  20.8 1.4 dispatch.1
  22.2 18.9 %all-to-all-start.1 = ((bf16[16,8,1792]{2,1,0:T(8,128)(2,1)}), bf16[16,8,1792]{2,1,0:T(8,128)(2,1)S(1)}, u32[]{:S(2)}, u32[]{:S(2)}) async-start(bf16[16,8,1792]{2,1,0:T(8,128)(2,1)} %bitcast.3), calls=%async_computation.1 | async-start | bytes 917504 | tf_op jit(solution)/shard_map/all_to_all | solution.py:187
  41.1 1.9 %collective-permute-start = (bf16[3584,128]{1,0:T(8,128)(2,1)}, bf16[3584,128]{1,0:T(8,128)(2,1)S(1)}, u32[]{:S(2)}, u32[]{:S(2)}) collective-permute-start(bf16[3584,128]{1,0:T(8,128)(2,1)} %bitcast.22), channel_id=1, source_target_pairs={{0,128},{128,0},{1,129},{129,1},{2,130},{130,2},{3,131},{131,3},{4... | collective-permute-start | bytes 2752520 | tf_op jit(solution)/shard_map/ppermute | solution.py:261
  43.0 2.4 %collective-permute-start.1 = (bf16[3584,128]{1,0:T(8,128)(2,1)}, bf16[3584,128]{1,0:T(8,128)(2,1)S(1)}, u32[]{:S(2)}, u32[]{:S(2)}) collective-permute-start(bf16[3584,128]{1,0:T(8,128)(2,1)} %bitcast.24), channel_id=1, source_target_pairs={{0,128},{128,0},{1,129},{129,1},{2,130},{130,2},{3,131},{131,3},{4... | collective-permute-start | bytes 2752520 | tf_op jit(solution)/shard_map/ppermute | solution.py:261
  45.4 1.9 %collective-permute-start.2 = (bf16[128,3584]{1,0:T(8,128)(2,1)}, bf16[128,3584]{1,0:T(8,128)(2,1)S(1)}, u32[]{:S(2)}, u32[]{:S(2)}) collective-permute-start(bf16[128,3584]{1,0:T(8,128)(2,1)} %bitcast.26), channel_id=1, source_target_pairs={{0,128},{128,0},{1,129},{129,1},{2,130},{130,2},{3,131},{131,3},{4... | collective-permute-start | bytes 2752520 | tf_op jit(solution)/shard_map/ppermute | solution.py:261
  47.7 2.3 %collective-permute-done.2.refs_5_ = bf16[128,3584]{1,0:T(8,128)(2,1)S(1)} collective-permute-done((bf16[128,3584]{1,0:T(8,128)(2,1)}, bf16[128,3584]{1,0:T(8,128)(2,1)S(1)}, u32[]{:S(2)}, u32[]{:S(2)}) %collective-permute-start.2) | collective-permute-done | bytes 917536 | tf_op jit(solution)/shard_map/ppermute | solution.py:261
  50.0 1.2 copy-done.2
  51.2 1.2 copy-done.3
  52.4 1.2 copy-done.4
  53.5 0.7 join.1
  54.3 1.8 %copy-done = bf16[3584,512]{1,0:T(8,128)(2,1)} copy-done((bf16[3584,512]{1,0:T(8,128)(2,1)}, bf16[3584,512]{1,0:T(8,128)(2,1)S(1)}, u32[]{:S(2)}) %copy-start) | copy-done | bytes 3670040
  56.1 8.8 %all-to-all-done.1 = bf16[16,8,1792]{2,1,0:T(8,128)(2,1)S(1)} async-done(((bf16[16,8,1792]{2,1,0:T(8,128)(2,1)}), bf16[16,8,1792]{2,1,0:T(8,128)(2,1)S(1)}, u32[]{:S(2)}, u32[]{:S(2)}) %all-to-all-start.1) | async-done | bytes 458784 | tf_op jit(solution)/shard_map/all_to_all | solution.py:187
  64.9 2.4 %collective-permute-start.3 = (bf16[128,1792]{1,0:T(8,128)(2,1)S(1)}, bf16[128,1792]{1,0:T(8,128)(2,1)S(1)}, u32[]{:S(2)}, u32[]{:S(2)}) collective-permute-start(bf16[128,1792]{1,0:T(8,128)(2,1)S(1)} %bitcast.16), channel_id=1, source_target_pairs={{0,256},{256,512},{512,768},{768,0},{1,257},{257,513},{513,769},{7... | collective-permute-start | bytes 1376264 | tf_op jit(solution)/shard_map/ppermute | solution.py:236
  67.3 3.4 %collective-permute-start.4 = (bf16[128,1792]{1,0:T(8,128)(2,1)S(1)}, bf16[128,1792]{1,0:T(8,128)(2,1)S(1)}, u32[]{:S(2)}, u32[]{:S(2)}) collective-permute-start(bf16[128,1792]{1,0:T(8,128)(2,1)S(1)} %bitcast.17), channel_id=1, source_target_pairs={{0,768},{256,0},{512,256},{768,512},{1,769},{257,1},{513,257},{769... | collective-permute-start | bytes 1376264 | tf_op jit(solution)/shard_map/ppermute | solution.py:236
  70.7 2.0 %copy-done.1 = bf16[3584,512]{1,0:T(8,128)(2,1)S(1)} copy-done((bf16[3584,512]{1,0:T(8,128)(2,1)S(1)}, bf16[3584,512]{1,0:T(8,128)(2,1)}, u32[]{:S(2)}) %copy-start.1) | copy-done | bytes 3670040
  72.8 3.1 %mine.1.refs_0_ = f32[128,1792]{1,0:T(8,128)S(1)} custom-call(bf16[128,1792]{1,0:T(8,128)(2,1)S(1)} %bitcast.18, bf16[3584,512]{1,0:T(8,128)(2,1)S(1)} %copy-done.1, bf16[256,3584]{1,0:T(8,128)(2,1)S(1)} %get-tuple-element.13.refs_2_.refs_3_), custom_call_target="tpu_custom_call" | custom-call | flops 352321536 | bytes 6881280 | tf_op jit(solution)/shard_map/mine/pallas_call | solution.py:202
  75.9 3.3 %collective-permute-start.7 = (bf16[128,1792]{1,0:T(8,128)(2,1)S(1)}, bf16[128,1792]{1,0:T(8,128)(2,1)S(1)}, u32[]{:S(2)}, u32[]{:S(2)}) collective-permute-start(bf16[128,1792]{1,0:T(8,128)(2,1)S(1)} %bitcast.19), channel_id=1, source_target_pairs={{0,512},{256,768},{512,0},{768,256},{1,513},{257,769},{513,1},{769... | collective-permute-start | bytes 1376264 | tf_op jit(solution)/shard_map/ppermute | solution.py:236
  79.2 7.6 %collective-permute-done.4.refs_1_ = bf16[128,1792]{1,0:T(8,128)(2,1)S(1)} collective-permute-done((bf16[128,1792]{1,0:T(8,128)(2,1)S(1)}, bf16[128,1792]{1,0:T(8,128)(2,1)S(1)}, u32[]{:S(2)}, u32[]{:S(2)}) %collective-permute-start.4) | collective-permute-done | bytes 458784 | tf_op jit(solution)/shard_map/ppermute | solution.py:236
  86.9 3.5 %near.1 = (bf16[128,1792]{1,0:T(8,128)(2,1)S(1)}, bf16[128,1792]{1,0:T(8,128)(2,1)S(1)}) custom-call(bf16[128,1792]{1,0:T(8,128)(2,1)S(1)} %collective-permute-done.3.refs_0_, bf16[128,1792]{1,0:T(8,128)(2,1)S(1)} %collective-permute-done.4.refs_1_, bf16[3584,512]{1,0:T(8,128)(2,1)S(1)} %copy-done.1, bf16[256,3584]{1,0:T(8,128)(2,1)S(1)} %get-tuple-element.13.refs_2_.refs_3_), custom_call_target="tpu_custom_call" | custom-call | flops 704643072 | bytes 7340032 | tf_op jit(solution)/shard_map/near/pallas_call | solution.py:202
  90.3 1.9 %collective-permute-start.5 = (bf16[128,1792]{1,0:T(8,128)(2,1)S(1)}, bf16[128,1792]{1,0:T(8,128)(2,1)S(1)}, u32[]{:S(2)}, u32[]{:S(2)}) collective-permute-start(bf16[128,1792]{1,0:T(8,128)(2,1)S(1)} %get-tuple-element.15), channel_id=1, source_target_pairs={{0,768},{256,0},{512,256},{768,512},{1,769},{257,1},{513,257},{769... | collective-permute-start | bytes 1376264 | tf_op jit(solution)/shard_map/ppermute | solution.py:236
  92.8 4.6 %collective-permute-start.6 = (bf16[128,1792]{1,0:T(8,128)(2,1)S(1)}, bf16[128,1792]{1,0:T(8,128)(2,1)S(1)}, u32[]{:S(2)}, u32[]{:S(2)}) collective-permute-start(bf16[128,1792]{1,0:T(8,128)(2,1)S(1)} %get-tuple-element.16), channel_id=1, source_target_pairs={{0,256},{256,512},{512,768},{768,0},{1,257},{257,513},{513,769},{7... | collective-permute-start | bytes 1376264 | tf_op jit(solution)/shard_map/ppermute | solution.py:236
  97.4 3.1 %far.1 = bf16[128,1792]{1,0:T(8,128)(2,1)S(1)} custom-call(bf16[128,1792]{1,0:T(8,128)(2,1)S(1)} %collective-permute-done.7.refs_0_, bf16[3584,512]{1,0:T(8,128)(2,1)S(1)} %copy-done.1, bf16[256,3584]{1,0:T(8,128)(2,1)S(1)} %get-tuple-element.13.refs_2_.refs_3_), custom_call_target="tpu_custom_call" | custom-call | flops 352321536 | bytes 6422528 | tf_op jit(solution)/shard_map/far/pallas_call | solution.py:202
  100.5 1.9 %collective-permute-start.8 = (bf16[128,1792]{1,0:T(8,128)(2,1)S(1)}, bf16[128,1792]{1,0:T(8,128)(2,1)S(1)}, u32[]{:S(2)}, u32[]{:S(2)}) collective-permute-start(bf16[128,1792]{1,0:T(8,128)(2,1)S(1)} %far.1), channel_id=1, source_target_pairs={{0,512},{256,768},{512,0},{768,256},{1,513},{257,769},{513,1},{769... | collective-permute-start | bytes 1376264 | tf_op jit(solution)/shard_map/ppermute | solution.py:236
  102.5 3.4 %collective-permute-done.5.refs_1_ = bf16[128,1792]{1,0:T(8,128)(2,1)S(1)} collective-permute-done((bf16[128,1792]{1,0:T(8,128)(2,1)S(1)}, bf16[128,1792]{1,0:T(8,128)(2,1)S(1)}, u32[]{:S(2)}, u32[]{:S(2)}) %collective-permute-start.5) | collective-permute-done | bytes 458784 | tf_op jit(solution)/shard_map/ppermute | solution.py:236
  106.0 6.4 %collective-permute-done.8.refs_1_ = bf16[128,1792]{1,0:T(8,128)(2,1)S(1)} collective-permute-done((bf16[128,1792]{1,0:T(8,128)(2,1)S(1)}, bf16[128,1792]{1,0:T(8,128)(2,1)S(1)}, u32[]{:S(2)}, u32[]{:S(2)}) %collective-permute-start.8) | collective-permute-done | bytes 458784 | tf_op jit(solution)/shard_map/ppermute | solution.py:236
  112.8 28.5 %all_to_all.45 = bf16[16,8,1792]{2,1,0:T(8,128)(2,1)S(1)} all-to-all(bf16[16,8,1792]{2,1,0:T(8,128)(2,1)S(1)} %bitcast.14), channel_id=1, replica_groups=mesh['x'=4,'core'=2,'node'=8,'local'=16] {'local'}, dimensions={0} | all-to-all | bytes 917504 | tf_op jit(solution)/shard_map/all_to_all | solution.py:187
  141.3 0.8 combine.1
  142.0 15.0 %all_to_all.46 = bf16[8,8,1920]{2,1,0:T(8,128)(2,1)S(1)} all-to-all(bf16[8,8,1920]{2,1,0:T(8,128)(2,1)S(1)} %bitcast.21), channel_id=1, replica_groups=mesh['x'=4,'core'=2,'node'=8,'local'=16] {'node'}, dimensions={0} | all-to-all | bytes 491520 | tf_op jit(solution)/shard_map/all_to_all | solution.py:187
  157.1 0.7 home.1
  (12 shorter events, 1.3 us)
Async XLA Ops:
  2.2 18.6 %all-to-all-start = ((bf16[8,8,1920]{2,1,0:T(8,128)(2,1)}), bf16[8,8,1920]{2,1,0:T(8,128)(2,1)S(1)}, u32[]{:S(2)}, u32[]{:S(2)}) async-start(bf16[8,8,1920]{2,1,0:T(8,128)(2,1)} %bitcast.28), calls=%async_computation | async-start | bytes 491520 | tf_op jit(solution)/shard_map/all_to_all | solution.py:187
  22.2 42.7 %all-to-all-start.1 = ((bf16[16,8,1792]{2,1,0:T(8,128)(2,1)}), bf16[16,8,1792]{2,1,0:T(8,128)(2,1)S(1)}, u32[]{:S(2)}, u32[]{:S(2)}) async-start(bf16[16,8,1792]{2,1,0:T(8,128)(2,1)} %bitcast.3), calls=%async_computation.1 | async-start | bytes 917504 | tf_op jit(solution)/shard_map/all_to_all | solution.py:187
  41.1 6.3 %collective-permute-start = (bf16[3584,128]{1,0:T(8,128)(2,1)}, bf16[3584,128]{1,0:T(8,128)(2,1)S(1)}, u32[]{:S(2)}, u32[]{:S(2)}) collective-permute-start(bf16[3584,128]{1,0:T(8,128)(2,1)} %bitcast.22), channel_id=1, source_target_pairs={{0,128},{128,0},{1,129},{129,1},{2,130},{130,2},{3,131},{131,3},{4... | collective-permute-start | bytes 2752520 | tf_op jit(solution)/shard_map/ppermute | solution.py:261
  43.0 4.7 %collective-permute-start.1 = (bf16[3584,128]{1,0:T(8,128)(2,1)}, bf16[3584,128]{1,0:T(8,128)(2,1)S(1)}, u32[]{:S(2)}, u32[]{:S(2)}) collective-permute-start(bf16[3584,128]{1,0:T(8,128)(2,1)} %bitcast.24), channel_id=1, source_target_pairs={{0,128},{128,0},{1,129},{129,1},{2,130},{130,2},{3,131},{131,3},{4... | collective-permute-start | bytes 2752520 | tf_op jit(solution)/shard_map/ppermute | solution.py:261
  45.4 4.6 %collective-permute-start.2 = (bf16[128,3584]{1,0:T(8,128)(2,1)}, bf16[128,3584]{1,0:T(8,128)(2,1)S(1)}, u32[]{:S(2)}, u32[]{:S(2)}) collective-permute-start(bf16[128,3584]{1,0:T(8,128)(2,1)} %bitcast.26), channel_id=1, source_target_pairs={{0,128},{128,0},{1,129},{129,1},{2,130},{130,2},{3,131},{131,3},{4... | collective-permute-start | bytes 2752520 | tf_op jit(solution)/shard_map/ppermute | solution.py:261
  50.0 1.2 copy-start.2
  51.2 1.2 copy-start.3
  52.4 1.2 copy-start.4
  54.3 1.8 %copy-start = (bf16[3584,512]{1,0:T(8,128)(2,1)}, bf16[3584,512]{1,0:T(8,128)(2,1)S(1)}, u32[]{:S(2)}) copy-start(bf16[3584,512]{1,0:T(8,128)(2,1)S(1)} %get-tuple-element.11.refs_1_.refs_2_) | copy-start | bytes 11010052
  64.9 14.3 %collective-permute-start.3 = (bf16[128,1792]{1,0:T(8,128)(2,1)S(1)}, bf16[128,1792]{1,0:T(8,128)(2,1)S(1)}, u32[]{:S(2)}, u32[]{:S(2)}) collective-permute-start(bf16[128,1792]{1,0:T(8,128)(2,1)S(1)} %bitcast.16), channel_id=1, source_target_pairs={{0,256},{256,512},{512,768},{768,0},{1,257},{257,513},{513,769},{7... | collective-permute-start | bytes 1376264 | tf_op jit(solution)/shard_map/ppermute | solution.py:236
  67.3 19.6 %collective-permute-start.4 = (bf16[128,1792]{1,0:T(8,128)(2,1)S(1)}, bf16[128,1792]{1,0:T(8,128)(2,1)S(1)}, u32[]{:S(2)}, u32[]{:S(2)}) collective-permute-start(bf16[128,1792]{1,0:T(8,128)(2,1)S(1)} %bitcast.17), channel_id=1, source_target_pairs={{0,768},{256,0},{512,256},{768,512},{1,769},{257,1},{513,257},{769... | collective-permute-start | bytes 1376264 | tf_op jit(solution)/shard_map/ppermute | solution.py:236
  70.7 2.0 %copy-start.1 = (bf16[3584,512]{1,0:T(8,128)(2,1)S(1)}, bf16[3584,512]{1,0:T(8,128)(2,1)}, u32[]{:S(2)}) copy-start(bf16[3584,512]{1,0:T(8,128)(2,1)} %copy-done) | copy-start | bytes 11010052
  75.9 16.9 %collective-permute-start.7 = (bf16[128,1792]{1,0:T(8,128)(2,1)S(1)}, bf16[128,1792]{1,0:T(8,128)(2,1)S(1)}, u32[]{:S(2)}, u32[]{:S(2)}) collective-permute-start(bf16[128,1792]{1,0:T(8,128)(2,1)S(1)} %bitcast.19), channel_id=1, source_target_pairs={{0,512},{256,768},{512,0},{768,256},{1,513},{257,769},{513,1},{769... | collective-permute-start | bytes 1376264 | tf_op jit(solution)/shard_map/ppermute | solution.py:236
  90.3 15.6 %collective-permute-start.5 = (bf16[128,1792]{1,0:T(8,128)(2,1)S(1)}, bf16[128,1792]{1,0:T(8,128)(2,1)S(1)}, u32[]{:S(2)}, u32[]{:S(2)}) collective-permute-start(bf16[128,1792]{1,0:T(8,128)(2,1)S(1)} %get-tuple-element.15), channel_id=1, source_target_pairs={{0,768},{256,0},{512,256},{768,512},{1,769},{257,1},{513,257},{769... | collective-permute-start | bytes 1376264 | tf_op jit(solution)/shard_map/ppermute | solution.py:236
  92.8 13.2 %collective-permute-start.6 = (bf16[128,1792]{1,0:T(8,128)(2,1)S(1)}, bf16[128,1792]{1,0:T(8,128)(2,1)S(1)}, u32[]{:S(2)}, u32[]{:S(2)}) collective-permute-start(bf16[128,1792]{1,0:T(8,128)(2,1)S(1)} %get-tuple-element.16), channel_id=1, source_target_pairs={{0,256},{256,512},{512,768},{768,0},{1,257},{257,513},{513,769},{7... | collective-permute-start | bytes 1376264 | tf_op jit(solution)/shard_map/ppermute | solution.py:236
  100.5 11.9 %collective-permute-start.8 = (bf16[128,1792]{1,0:T(8,128)(2,1)S(1)}, bf16[128,1792]{1,0:T(8,128)(2,1)S(1)}, u32[]{:S(2)}, u32[]{:S(2)}) collective-permute-start(bf16[128,1792]{1,0:T(8,128)(2,1)S(1)} %far.1), channel_id=1, source_target_pairs={{0,512},{256,768},{512,0},{768,256},{1,513},{257,769},{513,1},{769... | collective-permute-start | bytes 1376264 | tf_op jit(solution)/shard_map/ppermute | solution.py:236

commit v5 on v4

--- a/solution.py
+++ b/solution.py
@@ -191,12 +191,12 @@
     return lax.optimization_barrier((array, earlier))[0]
 
 
-def call(kernel, outs, name, *args, scratch=(), smem=0, vmem=8, flops=0):
+def call(kernel, outs, name, *args, scratch=(), smem=0, vmem=8, flops=0, light=False):
     single = isinstance(outs, jax.ShapeDtypeStruct)
     arrays = args + ((outs,) if single else outs)
     cost = pl.CostEstimate(
         flops=flops,
-        bytes_accessed=sum(a.size * a.dtype.itemsize for a in arrays),
+        bytes_accessed=0 if light else sum(a.size * a.dtype.itemsize for a in arrays),
         transcendentals=0,
     )
     return pl.pallas_call(
@@ -264,7 +264,7 @@
 
     mine = after(exchange(send, "local"), joined[0])
 
-    def experts(name, dtype, *blocks):
+    def experts(name, dtype, *blocks, light=False):
         return call(
             functools.partial(expert_kernel, local_count, len(blocks)),
             tuple(shape(*block.shape, dtype) for block in blocks),
@@ -272,7 +272,8 @@
             *blocks,
             *joined,
             vmem=16,
-            flops=12 * len(blocks) * 2 * local_count * width * 2 * hid_part,
+            flops=0 if light else 12 * len(blocks) * 2 * local_count * width * 2 * hid_part,
+            light=light,
         )
 
     near = sorted({1, x_count - 1})
@@ -285,11 +286,16 @@
     for name, group in (("near", near), ("far", far)):
         if group:
             first, *rest = [others[k] for k in group]
-            done = experts(name, BF, after(first, last), *rest)
+            done = experts(name, BF, after(first, last), *rest, light=name == "far")
             last = done[0]
             results[name] = [turn(part, -k) for k, part in zip(group, done)]
     near_sum = call(
-        near_sum_kernel, shape(8 * local_count, half, F32), "near_sum", my_part, *results["near"]
+        near_sum_kernel,
+        shape(8 * local_count, half, F32),
+        "near_sum",
+        my_part,
+        *results["near"],
+        flops=4 * 10**9,
     )
     total = call(
         functools.partial(total_kernel, local_count),

time: 160 us -> 159 us (level)
  transfers between devices with their start and end apart: 11 -> 11, of which waited for: 8 -> 7; matrix products, arithmetic and copies ran while one was open for 0% -> 0% of each run, Pallas kernels for 7% -> 7%
where the time goes in v5:
time: 159 us; the launch traced here: 158 us
  starting transfers between devices  50.4 us (32%)
  blocking collectives  43.5 us (27%)
  waiting for transfers between devices  40.4 us (25%)
  Pallas kernels  15.3 us (10%)
  local copies, waits for them, and re-layouts  7.34 us (5%)
    all_to_all x2, blocking collectives, exchange(): return lax.all_to_all(array, axis, split_axis=0, concat_axis=0, tiled=True)  43.5 us
    all_to_all x2, starting transfers between devices, exchange(): return lax.all_to_all(array, axis, split_axis=0, concat_axis=0, tiled=True)  26 us
    all_to_all x2, waiting for transfers between devices, exchange(): return lax.all_to_all(array, axis, split_axis=0, concat_axis=0, tiled=True)  20.3 us
    ppermute x6, starting transfers between devices, turn(): lax.ppermute(array, 'x', [(i, (i + k) % x_count) for i in range(x_count)])  18.1 us
    ppermute x6, waiting for transfers between devices, turn(): lax.ppermute(array, 'x', [(i, (i + k) % x_count) for i in range(x_count)])  17.5 us
    pallas_call x10, Pallas kernels, call(): pl.pallas_call(kernel, out_shape=outs, in_specs=[pl.BlockSpec(memory_spac...  15.3 us
    unnamed x10, local copies, waits for them, and re-layouts  7.34 us
    ppermute x3, starting transfers between devices, local(): lax.ppermute(w, 'core', swap)  6.25 us
  transfers between devices with their start and end apart: 11, of which 7 were waited for; matrix products, arithmetic and copies ran while one was open for 0% of the time, Pallas kernels for 7%

profile of v5, /device:TPU:6, one launch (start us, length us, event | category | flops | bytes accessed | tf_op | source)
XLA Modules:
  0.0 157.7 jit_solution(8089789952575979073)
XLA Ops:
  0.6 1.6 payload.1
  2.2 7.1 %all-to-all-start = ((bf16[8,8,1920]{2,1,0:T(8,128)(2,1)}), bf16[8,8,1920]{2,1,0:T(8,128)(2,1)S(1)}, u32[]{:S(2)}, u32[]{:S(2)}) async-start(bf16[8,8,1920]{2,1,0:T(8,128)(2,1)} %bitcast.28), calls=%async_computation | async-start | bytes 491520 | tf_op jit(solution)/shard_map/all_to_all | solution.py:187
  9.3 11.5 %all-to-all-done = bf16[8,8,1920]{2,1,0:T(8,128)(2,1)S(1)} async-done(((bf16[8,8,1920]{2,1,0:T(8,128)(2,1)}), bf16[8,8,1920]{2,1,0:T(8,128)(2,1)S(1)}, u32[]{:S(2)}, u32[]{:S(2)}) %all-to-all-start) | async-done | bytes 245792 | tf_op jit(solution)/shard_map/all_to_all | solution.py:187
  20.8 1.4 dispatch.1
  22.2 18.9 %all-to-all-start.1 = ((bf16[16,8,1792]{2,1,0:T(8,128)(2,1)}), bf16[16,8,1792]{2,1,0:T(8,128)(2,1)S(1)}, u32[]{:S(2)}, u32[]{:S(2)}) async-start(bf16[16,8,1792]{2,1,0:T(8,128)(2,1)} %bitcast.3), calls=%async_computation.1 | async-start | bytes 917504 | tf_op jit(solution)/shard_map/all_to_all | solution.py:187
  41.1 1.9 %collective-permute-start = (bf16[3584,128]{1,0:T(8,128)(2,1)}, bf16[3584,128]{1,0:T(8,128)(2,1)S(1)}, u32[]{:S(2)}, u32[]{:S(2)}) collective-permute-start(bf16[3584,128]{1,0:T(8,128)(2,1)} %bitcast.22), channel_id=1, source_target_pairs={{0,128},{128,0},{1,129},{129,1},{2,130},{130,2},{3,131},{131,3},{4... | collective-permute-start | bytes 2752520 | tf_op jit(solution)/shard_map/ppermute | solution.py:261
  43.0 2.4 %collective-permute-start.1 = (bf16[3584,128]{1,0:T(8,128)(2,1)}, bf16[3584,128]{1,0:T(8,128)(2,1)S(1)}, u32[]{:S(2)}, u32[]{:S(2)}) collective-permute-start(bf16[3584,128]{1,0:T(8,128)(2,1)} %bitcast.24), channel_id=1, source_target_pairs={{0,128},{128,0},{1,129},{129,1},{2,130},{130,2},{3,131},{131,3},{4... | collective-permute-start | bytes 2752520 | tf_op jit(solution)/shard_map/ppermute | solution.py:261
  45.4 1.9 %collective-permute-start.2 = (bf16[128,3584]{1,0:T(8,128)(2,1)}, bf16[128,3584]{1,0:T(8,128)(2,1)S(1)}, u32[]{:S(2)}, u32[]{:S(2)}) collective-permute-start(bf16[128,3584]{1,0:T(8,128)(2,1)} %bitcast.26), channel_id=1, source_target_pairs={{0,128},{128,0},{1,129},{129,1},{2,130},{130,2},{3,131},{131,3},{4... | collective-permute-start | bytes 2752520 | tf_op jit(solution)/shard_map/ppermute | solution.py:261
  47.7 2.3 %collective-permute-done.2.refs_5_ = bf16[128,3584]{1,0:T(8,128)(2,1)S(1)} collective-permute-done((bf16[128,3584]{1,0:T(8,128)(2,1)}, bf16[128,3584]{1,0:T(8,128)(2,1)S(1)}, u32[]{:S(2)}, u32[]{:S(2)}) %collective-permute-start.2) | collective-permute-done | bytes 917536 | tf_op jit(solution)/shard_map/ppermute | solution.py:261
  50.0 1.2 copy-done.2
  51.2 1.2 copy-done.3
  52.4 1.2 copy-done.4
  53.5 0.7 join.1
  54.3 1.8 %copy-done = bf16[3584,512]{1,0:T(8,128)(2,1)} copy-done((bf16[3584,512]{1,0:T(8,128)(2,1)}, bf16[3584,512]{1,0:T(8,128)(2,1)S(1)}, u32[]{:S(2)}) %copy-start) | copy-done | bytes 3670040
  56.1 8.8 %all-to-all-done.1 = bf16[16,8,1792]{2,1,0:T(8,128)(2,1)S(1)} async-done(((bf16[16,8,1792]{2,1,0:T(8,128)(2,1)}), bf16[16,8,1792]{2,1,0:T(8,128)(2,1)S(1)}, u32[]{:S(2)}, u32[]{:S(2)}) %all-to-all-start.1) | async-done | bytes 458784 | tf_op jit(solution)/shard_map/all_to_all | solution.py:187
  64.9 2.4 %collective-permute-start.3 = (bf16[128,1792]{1,0:T(8,128)(2,1)S(1)}, bf16[128,1792]{1,0:T(8,128)(2,1)S(1)}, u32[]{:S(2)}, u32[]{:S(2)}) collective-permute-start(bf16[128,1792]{1,0:T(8,128)(2,1)S(1)} %bitcast.16), channel_id=1, source_target_pairs={{0,256},{256,512},{512,768},{768,0},{1,257},{257,513},{513,769},{7... | collective-permute-start | bytes 1376264 | tf_op jit(solution)/shard_map/ppermute | solution.py:236
  67.3 3.4 %collective-permute-start.4 = (bf16[128,1792]{1,0:T(8,128)(2,1)S(1)}, bf16[128,1792]{1,0:T(8,128)(2,1)S(1)}, u32[]{:S(2)}, u32[]{:S(2)}) collective-permute-start(bf16[128,1792]{1,0:T(8,128)(2,1)S(1)} %bitcast.17), channel_id=1, source_target_pairs={{0,768},{256,0},{512,256},{768,512},{1,769},{257,1},{513,257},{769... | collective-permute-start | bytes 1376264 | tf_op jit(solution)/shard_map/ppermute | solution.py:236
  70.7 2.0 %copy-done.1 = bf16[3584,512]{1,0:T(8,128)(2,1)S(1)} copy-done((bf16[3584,512]{1,0:T(8,128)(2,1)S(1)}, bf16[3584,512]{1,0:T(8,128)(2,1)}, u32[]{:S(2)}) %copy-start.1) | copy-done | bytes 3670040
  72.8 3.1 %mine.1.refs_0_ = f32[128,1792]{1,0:T(8,128)S(1)} custom-call(bf16[128,1792]{1,0:T(8,128)(2,1)S(1)} %bitcast.18, bf16[3584,512]{1,0:T(8,128)(2,1)S(1)} %copy-done.1, bf16[256,3584]{1,0:T(8,128)(2,1)S(1)} %get-tuple-element.13.refs_2_.refs_3_), custom_call_target="tpu_custom_call" | custom-call | flops 352321536 | bytes 6881280 | tf_op jit(solution)/shard_map/mine/pallas_call | solution.py:202
  75.9 3.3 %collective-permute-start.7 = (bf16[128,1792]{1,0:T(8,128)(2,1)S(1)}, bf16[128,1792]{1,0:T(8,128)(2,1)S(1)}, u32[]{:S(2)}, u32[]{:S(2)}) collective-permute-start(bf16[128,1792]{1,0:T(8,128)(2,1)S(1)} %bitcast.19), channel_id=1, source_target_pairs={{0,512},{256,768},{512,0},{768,256},{1,513},{257,769},{513,1},{769... | collective-permute-start | bytes 1376264 | tf_op jit(solution)/shard_map/ppermute | solution.py:236
  79.2 7.6 %collective-permute-done.4.refs_1_ = bf16[128,1792]{1,0:T(8,128)(2,1)S(1)} collective-permute-done((bf16[128,1792]{1,0:T(8,128)(2,1)S(1)}, bf16[128,1792]{1,0:T(8,128)(2,1)S(1)}, u32[]{:S(2)}, u32[]{:S(2)}) %collective-permute-start.4) | collective-permute-done | bytes 458784 | tf_op jit(solution)/shard_map/ppermute | solution.py:236
  86.9 3.5 %near.1 = (bf16[128,1792]{1,0:T(8,128)(2,1)S(1)}, bf16[128,1792]{1,0:T(8,128)(2,1)S(1)}) custom-call(bf16[128,1792]{1,0:T(8,128)(2,1)S(1)} %collective-permute-done.3.refs_0_, bf16[128,1792]{1,0:T(8,128)(2,1)S(1)} %collective-permute-done.4.refs_1_, bf16[3584,512]{1,0:T(8,128)(2,1)S(1)} %copy-done.1, bf16[256,3584]{1,0:T(8,128)(2,1)S(1)} %get-tuple-element.13.refs_2_.refs_3_), custom_call_target="tpu_custom_call" | custom-call | flops 704643072 | bytes 7340032 | tf_op jit(solution)/shard_map/near/pallas_call | solution.py:202
  90.3 1.9 %collective-permute-start.5 = (bf16[128,1792]{1,0:T(8,128)(2,1)S(1)}, bf16[128,1792]{1,0:T(8,128)(2,1)S(1)}, u32[]{:S(2)}, u32[]{:S(2)}) collective-permute-start(bf16[128,1792]{1,0:T(8,128)(2,1)S(1)} %get-tuple-element.15), channel_id=1, source_target_pairs={{0,768},{256,0},{512,256},{768,512},{1,769},{257,1},{513,257},{769... | collective-permute-start | bytes 1376264 | tf_op jit(solution)/shard_map/ppermute | solution.py:236
  92.3 5.1 %collective-permute-start.6 = (bf16[128,1792]{1,0:T(8,128)(2,1)S(1)}, bf16[128,1792]{1,0:T(8,128)(2,1)S(1)}, u32[]{:S(2)}, u32[]{:S(2)}) collective-permute-start(bf16[128,1792]{1,0:T(8,128)(2,1)S(1)} %get-tuple-element.16), channel_id=1, source_target_pairs={{0,256},{256,512},{512,768},{768,0},{1,257},{257,513},{513,769},{7... | collective-permute-start | bytes 1376264 | tf_op jit(solution)/shard_map/ppermute | solution.py:236
  97.4 3.1 %far.1 = bf16[128,1792]{1,0:T(8,128)(2,1)S(1)} custom-call(bf16[128,1792]{1,0:T(8,128)(2,1)S(1)} %collective-permute-done.7.refs_0_, bf16[3584,512]{1,0:T(8,128)(2,1)S(1)} %copy-done.1, bf16[256,3584]{1,0:T(8,128)(2,1)S(1)} %get-tuple-element.13.refs_2_.refs_3_), custom_call_target="tpu_custom_call" | custom-call | tf_op jit(solution)/shard_map/far/pallas_call | solution.py:202
  100.5 1.9 %collective-permute-start.8 = (bf16[128,1792]{1,0:T(8,128)(2,1)S(1)}, bf16[128,1792]{1,0:T(8,128)(2,1)S(1)}, u32[]{:S(2)}, u32[]{:S(2)}) collective-permute-start(bf16[128,1792]{1,0:T(8,128)(2,1)S(1)} %far.1), channel_id=1, source_target_pairs={{0,512},{256,768},{512,0},{768,256},{1,513},{257,769},{513,1},{769... | collective-permute-start | bytes 1376264 | tf_op jit(solution)/shard_map/ppermute | solution.py:236
  102.5 2.0 %collective-permute-done.5.refs_1_ = bf16[128,1792]{1,0:T(8,128)(2,1)S(1)} collective-permute-done((bf16[128,1792]{1,0:T(8,128)(2,1)S(1)}, bf16[128,1792]{1,0:T(8,128)(2,1)S(1)}, u32[]{:S(2)}, u32[]{:S(2)}) %collective-permute-start.5) | collective-permute-done | bytes 458784 | tf_op jit(solution)/shard_map/ppermute | solution.py:236
  104.6 7.8 %collective-permute-done.8.refs_1_ = bf16[128,1792]{1,0:T(8,128)(2,1)S(1)} collective-permute-done((bf16[128,1792]{1,0:T(8,128)(2,1)S(1)}, bf16[128,1792]{1,0:T(8,128)(2,1)S(1)}, u32[]{:S(2)}, u32[]{:S(2)}) %collective-permute-start.8) | collective-permute-done | bytes 458784 | tf_op jit(solution)/shard_map/ppermute | solution.py:236
  112.8 28.5 %all_to_all.45 = bf16[16,8,1792]{2,1,0:T(8,128)(2,1)S(1)} all-to-all(bf16[16,8,1792]{2,1,0:T(8,128)(2,1)S(1)} %bitcast.14), channel_id=1, replica_groups=mesh['x'=4,'core'=2,'node'=8,'local'=16] {'local'}, dimensions={0} | all-to-all | bytes 917504 | tf_op jit(solution)/shard_map/all_to_all | solution.py:187
  141.3 0.8 combine.1
  142.0 15.0 %all_to_all.46 = bf16[8,8,1920]{2,1,0:T(8,128)(2,1)S(1)} all-to-all(bf16[8,8,1920]{2,1,0:T(8,128)(2,1)S(1)} %bitcast.21), channel_id=1, replica_groups=mesh['x'=4,'core'=2,'node'=8,'local'=16] {'node'}, dimensions={0} | all-to-all | bytes 491520 | tf_op jit(solution)/shard_map/all_to_all | solution.py:187
  157.1 0.7 home.1
  (12 shorter events, 0.8 us)
Async XLA Ops:
  2.2 18.6 %all-to-all-start = ((bf16[8,8,1920]{2,1,0:T(8,128)(2,1)}), bf16[8,8,1920]{2,1,0:T(8,128)(2,1)S(1)}, u32[]{:S(2)}, u32[]{:S(2)}) async-start(bf16[8,8,1920]{2,1,0:T(8,128)(2,1)} %bitcast.28), calls=%async_computation | async-start | bytes 491520 | tf_op jit(solution)/shard_map/all_to_all | solution.py:187
  22.2 42.7 %all-to-all-start.1 = ((bf16[16,8,1792]{2,1,0:T(8,128)(2,1)}), bf16[16,8,1792]{2,1,0:T(8,128)(2,1)S(1)}, u32[]{:S(2)}, u32[]{:S(2)}) async-start(bf16[16,8,1792]{2,1,0:T(8,128)(2,1)} %bitcast.3), calls=%async_computation.1 | async-start | bytes 917504 | tf_op jit(solution)/shard_map/all_to_all | solution.py:187
  41.1 6.3 %collective-permute-start = (bf16[3584,128]{1,0:T(8,128)(2,1)}, bf16[3584,128]{1,0:T(8,128)(2,1)S(1)}, u32[]{:S(2)}, u32[]{:S(2)}) collective-permute-start(bf16[3584,128]{1,0:T(8,128)(2,1)} %bitcast.22), channel_id=1, source_target_pairs={{0,128},{128,0},{1,129},{129,1},{2,130},{130,2},{3,131},{131,3},{4... | collective-permute-start | bytes 2752520 | tf_op jit(solution)/shard_map/ppermute | solution.py:261
  43.0 4.7 %collective-permute-start.1 = (bf16[3584,128]{1,0:T(8,128)(2,1)}, bf16[3584,128]{1,0:T(8,128)(2,1)S(1)}, u32[]{:S(2)}, u32[]{:S(2)}) collective-permute-start(bf16[3584,128]{1,0:T(8,128)(2,1)} %bitcast.24), channel_id=1, source_target_pairs={{0,128},{128,0},{1,129},{129,1},{2,130},{130,2},{3,131},{131,3},{4... | collective-permute-start | bytes 2752520 | tf_op jit(solution)/shard_map/ppermute | solution.py:261
  45.4 4.6 %collective-permute-start.2 = (bf16[128,3584]{1,0:T(8,128)(2,1)}, bf16[128,3584]{1,0:T(8,128)(2,1)S(1)}, u32[]{:S(2)}, u32[]{:S(2)}) collective-permute-start(bf16[128,3584]{1,0:T(8,128)(2,1)} %bitcast.26), channel_id=1, source_target_pairs={{0,128},{128,0},{1,129},{129,1},{2,130},{130,2},{3,131},{131,3},{4... | collective-permute-start | bytes 2752520 | tf_op jit(solution)/shard_map/ppermute | solution.py:261
  50.0 1.2 copy-start.2
  51.2 1.2 copy-start.3
  52.4 1.2 copy-start.4
  54.3 1.8 %copy-start = (bf16[3584,512]{1,0:T(8,128)(2,1)}, bf16[3584,512]{1,0:T(8,128)(2,1)S(1)}, u32[]{:S(2)}) copy-start(bf16[3584,512]{1,0:T(8,128)(2,1)S(1)} %get-tuple-element.11.refs_1_.refs_2_) | copy-start | bytes 11010052
  64.9 14.3 %collective-permute-start.3 = (bf16[128,1792]{1,0:T(8,128)(2,1)S(1)}, bf16[128,1792]{1,0:T(8,128)(2,1)S(1)}, u32[]{:S(2)}, u32[]{:S(2)}) collective-permute-start(bf16[128,1792]{1,0:T(8,128)(2,1)S(1)} %bitcast.16), channel_id=1, source_target_pairs={{0,256},{256,512},{512,768},{768,0},{1,257},{257,513},{513,769},{7... | collective-permute-start | bytes 1376264 | tf_op jit(solution)/shard_map/ppermute | solution.py:236
  67.3 19.6 %collective-permute-start.4 = (bf16[128,1792]{1,0:T(8,128)(2,1)S(1)}, bf16[128,1792]{1,0:T(8,128)(2,1)S(1)}, u32[]{:S(2)}, u32[]{:S(2)}) collective-permute-start(bf16[128,1792]{1,0:T(8,128)(2,1)S(1)} %bitcast.17), channel_id=1, source_target_pairs={{0,768},{256,0},{512,256},{768,512},{1,769},{257,1},{513,257},{769... | collective-permute-start | bytes 1376264 | tf_op jit(solution)/shard_map/ppermute | solution.py:236
  70.7 2.0 %copy-start.1 = (bf16[3584,512]{1,0:T(8,128)(2,1)S(1)}, bf16[3584,512]{1,0:T(8,128)(2,1)}, u32[]{:S(2)}) copy-start(bf16[3584,512]{1,0:T(8,128)(2,1)} %copy-done) | copy-start | bytes 11010052
  75.9 21.5 %collective-permute-start.7 = (bf16[128,1792]{1,0:T(8,128)(2,1)S(1)}, bf16[128,1792]{1,0:T(8,128)(2,1)S(1)}, u32[]{:S(2)}, u32[]{:S(2)}) collective-permute-start(bf16[128,1792]{1,0:T(8,128)(2,1)S(1)} %bitcast.19), channel_id=1, source_target_pairs={{0,512},{256,768},{512,0},{768,256},{1,513},{257,769},{513,1},{769... | collective-permute-start | bytes 1376264 | tf_op jit(solution)/shard_map/ppermute | solution.py:236
  90.3 14.1 %collective-permute-start.5 = (bf16[128,1792]{1,0:T(8,128)(2,1)S(1)}, bf16[128,1792]{1,0:T(8,128)(2,1)S(1)}, u32[]{:S(2)}, u32[]{:S(2)}) collective-permute-start(bf16[128,1792]{1,0:T(8,128)(2,1)S(1)} %get-tuple-element.15), channel_id=1, source_target_pairs={{0,768},{256,0},{512,256},{768,512},{1,769},{257,1},{513,257},{769... | collective-permute-start | bytes 1376264 | tf_op jit(solution)/shard_map/ppermute | solution.py:236
  92.3 12.2 %collective-permute-start.6 = (bf16[128,1792]{1,0:T(8,128)(2,1)S(1)}, bf16[128,1792]{1,0:T(8,128)(2,1)S(1)}, u32[]{:S(2)}, u32[]{:S(2)}) collective-permute-start(bf16[128,1792]{1,0:T(8,128)(2,1)S(1)} %get-tuple-element.16), channel_id=1, source_target_pairs={{0,256},{256,512},{512,768},{768,0},{1,257},{257,513},{513,769},{7... | collective-permute-start | bytes 1376264 | tf_op jit(solution)/shard_map/ppermute | solution.py:236
  100.5 11.9 %collective-permute-start.8 = (bf16[128,1792]{1,0:T(8,128)(2,1)S(1)}, bf16[128,1792]{1,0:T(8,128)(2,1)S(1)}, u32[]{:S(2)}, u32[]{:S(2)}) collective-permute-start(bf16[128,1792]{1,0:T(8,128)(2,1)S(1)} %far.1), channel_id=1, source_target_pairs={{0,512},{256,768},{512,0},{768,256},{1,513},{257,769},{513,1},{769... | collective-permute-start | bytes 1376264 | tf_op jit(solution)/shard_map/ppermute | solution.py:236

commit v6 on v5

--- a/solution.py
+++ b/solution.py
@@ -99,20 +99,23 @@
 
 
 def join_kernel(*refs):
-    gate_up, down = refs[6:]
+    gate_up, down = refs[6:8], refs[8:10]
     part = refs[0].shape[1]
-    for c in range(2):
-        for kind in range(2):
-            gate_up[:, pl.ds((2 * kind + c) * part, part)] = refs[3 * c + kind][...]
-        down[pl.ds(c * part, part), :] = refs[3 * c + 2][...]
+    half = gate_up[0].shape[0]
+    for h in range(2):
+        at = pl.ds(h * half, half)
+        for c in range(2):
+            for kind in range(2):
+                gate_up[h][:, pl.ds((2 * kind + c) * part, part)] = refs[3 * c + kind][at, :]
+            down[h][pl.ds(c * part, part), :] = refs[3 * c + 2][:, at]
 
 
 def expert_kernel(local_count, blocks, *refs):
-    rows, outs = refs[:blocks], refs[blocks + 2 :]
-    gate_up, down = refs[blocks : blocks + 2]
+    rows, outs = refs[:blocks], refs[blocks + 4 :]
+    gate_up, down = refs[blocks : blocks + 2], refs[blocks + 2 : blocks + 4]
     slots = 2 * local_count
     half = rows[0].shape[1]
-    hidden_size = down.shape[0]
+    hidden_size = down[0].shape[0]
     order = plain_order(local_count)
     plain = [dot(order, ref[...]).astype(BF) for ref in rows]
 
@@ -120,18 +123,17 @@
         first = (2 * h + kind) * slots
         return jnp.concatenate([block[first : first + slots] for block in plain], axis=0)
 
-    pre = dot(every(0, 0), gate_up[:half, :]) + dot(every(1, 0), gate_up[half:, :])
+    pre = dot(every(0, 0), gate_up[0][...]) + dot(every(1, 0), gate_up[1][...])
     gate_pre, up_pre = pre[:, :hidden_size], pre[:, hidden_size:]
     sig = 1.0 / (1.0 + jnp.exp(-gate_pre))
     active = gate_pre * sig
     hidden = (active * up_pre).astype(BF)
-    grad_hidden = dot(every(0, 1), down[:, :half], 1, 1) + dot(every(1, 1), down[:, half:], 1, 1)
+    grad_hidden = dot(every(0, 1), down[0][...], 1, 1) + dot(every(1, 1), down[1][...], 1, 1)
     grad_gate = (grad_hidden * up_pre * sig * (1.0 + gate_pre * (1.0 - sig))).astype(BF)
     grad_up = (grad_hidden * active).astype(BF)
     grads = jnp.concatenate([grad_gate, grad_up], axis=1)
     for h in range(2):
-        cols = pl.ds(h * half, half)
-        for kind, value in enumerate((dot(hidden, down[:, cols]), dot(grads, gate_up[cols, :], 1, 1))):
+        for kind, value in enumerate((dot(hidden, down[h][...]), dot(grads, gate_up[h][...], 1, 1))):
             at = pl.ds((2 * h + kind) * slots, slots)
             for b, ref in enumerate(outs):
                 ref[at, :] = value[b * slots : (b + 1) * slots].astype(ref.dtype)
@@ -255,7 +257,7 @@
     own = [w_gate[0], w_up[0], w_down[0]]
     joined = call(
         join_kernel,
-        (shape(width, 4 * hid_part), shape(2 * hid_part, width)),
+        (shape(half, 4 * hid_part),) * 2 + (shape(2 * hid_part, half),) * 2,
         "join",
         *own,
         *[lax.ppermute(w, "core", swap) for w in own],

time: 159 us -> 158 us (level)
  waiting for transfers between devices: 40.4 us -> 37.3 us
    ppermute x6, waiting for transfers between devices: 17.5 us -> 14.8 us  [turn(): lax.ppermute(array, 'x', [(i, (i + k) % x_count) for i in range(x_count)])]
    unnamed x10 -> x18, local copies, waits for them, and re-layouts: 7.34 us -> 8.42 us
where the time goes in v6:
time: 158 us; the launch traced here: 157 us
  starting transfers between devices  50.4 us (32%)
  blocking collectives  45 us (28%)
  waiting for transfers between devices  37.3 us (24%)
  Pallas kernels  15.4 us (10%)
  local copies, waits for them, and re-layouts  8.42 us (5%)
    all_to_all x2, blocking collectives, exchange(): return lax.all_to_all(array, axis, split_axis=0, concat_axis=0, tiled=True)  45 us
    all_to_all x2, starting transfers between devices, exchange(): return lax.all_to_all(array, axis, split_axis=0, concat_axis=0, tiled=True)  26 us
    all_to_all x2, waiting for transfers between devices, exchange(): return lax.all_to_all(array, axis, split_axis=0, concat_axis=0, tiled=True)  19.9 us
    ppermute x6, starting transfers between devices, turn(): lax.ppermute(array, 'x', [(i, (i + k) % x_count) for i in range(x_count)])  18.1 us
    pallas_call x10, Pallas kernels, call(): pl.pallas_call(kernel, out_shape=outs, in_specs=[pl.BlockSpec(memory_spac...  15.4 us
    ppermute x6, waiting for transfers between devices, turn(): lax.ppermute(array, 'x', [(i, (i + k) % x_count) for i in range(x_count)])  14.8 us
    unnamed x18, local copies, waits for them, and re-layouts  8.42 us
    ppermute x3, starting transfers between devices, local(): lax.ppermute(w, 'core', swap)  6.25 us
  transfers between devices with their start and end apart: 11, of which 7 were waited for; matrix products, arithmetic and copies ran while one was open for 0% of the time, Pallas kernels for 7%

profile of v6, /device:TPU:6, one launch (start us, length us, event | category | flops | bytes accessed | tf_op | source)
XLA Modules:
  0.0 157.3 jit_solution(16243989275424373041)
XLA Ops:
  0.7 1.7 %payload.1 = bf16[64,1920]{1,0:T(8,128)(2,1)} custom-call(bf16[2,3584]{1,0:T(2,128)(2,1)} %tok_ref.1, bf16[2,3584]{1,0:T(2,128)(2,1)} %cot_ref.1, s32[2,8]{1,0:T(2,128)} %ids_ref.1, s32[2,4]{1,0:T(2,128)} %groups_ref.1, bf16[2,8]{1,0:T(2,128)(2,1)} %weight_ref.1), custom_call_target="tpu_custom_call" | custom-call | bytes 274560 | tf_op jit(solution)/shard_map/payload/pallas_call | solution.py:204
  2.3 7.1 %all-to-all-start = ((bf16[8,8,1920]{2,1,0:T(8,128)(2,1)}), bf16[8,8,1920]{2,1,0:T(8,128)(2,1)S(1)}, u32[]{:S(2)}, u32[]{:S(2)}) async-start(bf16[8,8,1920]{2,1,0:T(8,128)(2,1)} %bitcast.28), calls=%async_computation | async-start | bytes 491520 | tf_op jit(solution)/shard_map/all_to_all | solution.py:189
  9.4 11.5 %all-to-all-done = bf16[8,8,1920]{2,1,0:T(8,128)(2,1)S(1)} async-done(((bf16[8,8,1920]{2,1,0:T(8,128)(2,1)}), bf16[8,8,1920]{2,1,0:T(8,128)(2,1)S(1)}, u32[]{:S(2)}, u32[]{:S(2)}) %all-to-all-start) | async-done | bytes 245792 | tf_op jit(solution)/shard_map/all_to_all | solution.py:189
  21.0 1.4 dispatch.1
  22.4 18.9 %all-to-all-start.1 = ((bf16[16,8,1792]{2,1,0:T(8,128)(2,1)}), bf16[16,8,1792]{2,1,0:T(8,128)(2,1)S(1)}, u32[]{:S(2)}, u32[]{:S(2)}) async-start(bf16[16,8,1792]{2,1,0:T(8,128)(2,1)} %bitcast.3), calls=%async_computation.1 | async-start | bytes 917504 | tf_op jit(solution)/shard_map/all_to_all | solution.py:189
  41.2 1.9 %collective-permute-start = (bf16[3584,128]{1,0:T(8,128)(2,1)S(1)}, bf16[3584,128]{1,0:T(8,128)(2,1)S(1)}, u32[]{:S(2)}, u32[]{:S(2)}) collective-permute-start(bf16[3584,128]{1,0:T(8,128)(2,1)S(1)} %bitcast.22), channel_id=1, source_target_pairs={{0,128},{128,0},{1,129},{129,1},{2,130},{130,2},{3,131},{131,3},{4... | collective-permute-start | bytes 2752520 | tf_op jit(solution)/shard_map/ppermute | solution.py:263
  43.2 2.4 %collective-permute-start.1 = (bf16[3584,128]{1,0:T(8,128)(2,1)S(1)}, bf16[3584,128]{1,0:T(8,128)(2,1)S(1)}, u32[]{:S(2)}, u32[]{:S(2)}) collective-permute-start(bf16[3584,128]{1,0:T(8,128)(2,1)S(1)} %bitcast.24), channel_id=1, source_target_pairs={{0,128},{128,0},{1,129},{129,1},{2,130},{130,2},{3,131},{131,3},{4... | collective-permute-start | bytes 2752520 | tf_op jit(solution)/shard_map/ppermute | solution.py:263
  45.6 1.9 %collective-permute-start.2 = (bf16[128,3584]{1,0:T(8,128)(2,1)}, bf16[128,3584]{1,0:T(8,128)(2,1)S(1)}, u32[]{:S(2)}, u32[]{:S(2)}) collective-permute-start(bf16[128,3584]{1,0:T(8,128)(2,1)} %bitcast.26), channel_id=1, source_target_pairs={{0,128},{128,0},{1,129},{129,1},{2,130},{130,2},{3,131},{131,3},{4... | collective-permute-start | bytes 2752520 | tf_op jit(solution)/shard_map/ppermute | solution.py:263
  47.7 2.5 %collective-permute-done.2.refs_5_ = bf16[128,3584]{1,0:T(8,128)(2,1)S(1)} collective-permute-done((bf16[128,3584]{1,0:T(8,128)(2,1)}, bf16[128,3584]{1,0:T(8,128)(2,1)S(1)}, u32[]{:S(2)}, u32[]{:S(2)}) %collective-permute-start.2) | collective-permute-done | bytes 917536 | tf_op jit(solution)/shard_map/ppermute | solution.py:263
  50.2 1.2 copy-done.5
  51.4 1.2 copy-done.7
  52.5 1.2 copy-done.8
  54.5 1.3 copy-done
  55.7 0.9 copy-done.2
  56.7 8.4 %all-to-all-done.1 = bf16[16,8,1792]{2,1,0:T(8,128)(2,1)S(1)} async-done(((bf16[16,8,1792]{2,1,0:T(8,128)(2,1)}), bf16[16,8,1792]{2,1,0:T(8,128)(2,1)S(1)}, u32[]{:S(2)}, u32[]{:S(2)}) %all-to-all-start.1) | async-done | bytes 458784 | tf_op jit(solution)/shard_map/all_to_all | solution.py:189
  65.0 2.4 %collective-permute-start.3 = (bf16[128,1792]{1,0:T(8,128)(2,1)S(1)}, bf16[128,1792]{1,0:T(8,128)(2,1)S(1)}, u32[]{:S(2)}, u32[]{:S(2)}) collective-permute-start(bf16[128,1792]{1,0:T(8,128)(2,1)S(1)} %bitcast.16), channel_id=1, source_target_pairs={{0,256},{256,512},{512,768},{768,0},{1,257},{257,513},{513,769},{7... | collective-permute-start | bytes 1376264 | tf_op jit(solution)/shard_map/ppermute | solution.py:238
  67.4 3.5 %collective-permute-start.4 = (bf16[128,1792]{1,0:T(8,128)(2,1)S(1)}, bf16[128,1792]{1,0:T(8,128)(2,1)S(1)}, u32[]{:S(2)}, u32[]{:S(2)}) collective-permute-start(bf16[128,1792]{1,0:T(8,128)(2,1)S(1)} %bitcast.17), channel_id=1, source_target_pairs={{0,768},{256,0},{512,256},{768,512},{1,769},{257,1},{513,257},{769... | collective-permute-start | bytes 1376264 | tf_op jit(solution)/shard_map/ppermute | solution.py:238
  70.9 1.5 copy-done.1
  72.4 1.2 copy-done.3
  73.5 3.1 %mine.1.refs_0_ = f32[128,1792]{1,0:T(8,128)S(1)} custom-call(bf16[128,1792]{1,0:T(8,128)(2,1)S(1)} %bitcast.18, bf16[1792,512]{1,0:T(8,128)(2,1)S(1)} %get-tuple-element.13.refs_1_.refs_2_, bf16[1792,512]{1,0:T(8,128)(2,1)S(1)} %copy-done.1, bf16[256,1792]{1,0:T(8,128)(2,1)S(1)} %get-tuple-element.16.refs_3_.refs_4_, bf16[256,1792]{1,0:T(8,128)(2,1)S(1)} %copy-done.3), custom_call_target="tpu_custom_call" | custom-call | flops 352321536 | bytes 6881280 | tf_op jit(solution)/shard_map/mine/pallas_call | solution.py:204
  76.7 3.3 %collective-permute-start.7 = (bf16[128,1792]{1,0:T(8,128)(2,1)S(1)}, bf16[128,1792]{1,0:T(8,128)(2,1)S(1)}, u32[]{:S(2)}, u32[]{:S(2)}) collective-permute-start(bf16[128,1792]{1,0:T(8,128)(2,1)S(1)} %bitcast.19), channel_id=1, source_target_pairs={{0,512},{256,768},{512,0},{768,256},{1,513},{257,769},{513,1},{769... | collective-permute-start | bytes 1376264 | tf_op jit(solution)/shard_map/ppermute | solution.py:238
  80.0 4.9 %collective-permute-done.4.refs_1_ = bf16[128,1792]{1,0:T(8,128)(2,1)S(1)} collective-permute-done((bf16[128,1792]{1,0:T(8,128)(2,1)S(1)}, bf16[128,1792]{1,0:T(8,128)(2,1)S(1)}, u32[]{:S(2)}, u32[]{:S(2)}) %collective-permute-start.4) | collective-permute-done | bytes 458784 | tf_op jit(solution)/shard_map/ppermute | solution.py:238
  85.0 3.5 %near.1 = (bf16[128,1792]{1,0:T(8,128)(2,1)S(1)}, bf16[128,1792]{1,0:T(8,128)(2,1)S(1)}) custom-call(bf16[128,1792]{1,0:T(8,128)(2,1)S(1)} %collective-permute-done.3.refs_0_, bf16[128,1792]{1,0:T(8,128)(2,1)S(1)} %collective-permute-done.4.refs_1_, bf16[1792,512]{1,0:T(8,128)(2,1)S(1)} %get-tuple-element.13.refs_1_.refs_2_, ...), custom_call_target="tpu_custom_call" | custom-call | flops 704643072 | bytes 7340032 | tf_op jit(solution)/shard_map/near/pallas_call | solution.py:204
  88.4 1.9 %collective-permute-start.5 = (bf16[128,1792]{1,0:T(8,128)(2,1)S(1)}, bf16[128,1792]{1,0:T(8,128)(2,1)S(1)}, u32[]{:S(2)}, u32[]{:S(2)}) collective-permute-start(bf16[128,1792]{1,0:T(8,128)(2,1)S(1)} %get-tuple-element.19), channel_id=1, source_target_pairs={{0,768},{256,0},{512,256},{768,512},{1,769},{257,1},{513,257},{769... | collective-permute-start | bytes 1376264 | tf_op jit(solution)/shard_map/ppermute | solution.py:238
  90.4 5.1 %collective-permute-start.6 = (bf16[128,1792]{1,0:T(8,128)(2,1)S(1)}, bf16[128,1792]{1,0:T(8,128)(2,1)S(1)}, u32[]{:S(2)}, u32[]{:S(2)}) collective-permute-start(bf16[128,1792]{1,0:T(8,128)(2,1)S(1)} %get-tuple-element.20), channel_id=1, source_target_pairs={{0,256},{256,512},{512,768},{768,0},{1,257},{257,513},{513,769},{7... | collective-permute-start | bytes 1376264 | tf_op jit(solution)/shard_map/ppermute | solution.py:238
  95.5 3.1 %far.1 = bf16[128,1792]{1,0:T(8,128)(2,1)S(1)} custom-call(bf16[128,1792]{1,0:T(8,128)(2,1)S(1)} %collective-permute-done.7.refs_0_, bf16[1792,512]{1,0:T(8,128)(2,1)S(1)} %get-tuple-element.13.refs_1_.refs_2_, bf16[1792,512]{1,0:T(8,128)(2,1)S(1)} %copy-done.1, bf16[256,1792]{1,0:T(8,128)(2,1)S(1)} %get-tuple-element.16.refs_3_.refs_4_, ...), custom_call_target="tpu_custom_call" | custom-call | tf_op jit(solution)/shard_map/far/pallas_call | solution.py:204
  98.6 1.9 %collective-permute-start.8 = (bf16[128,1792]{1,0:T(8,128)(2,1)S(1)}, bf16[128,1792]{1,0:T(8,128)(2,1)S(1)}, u32[]{:S(2)}, u32[]{:S(2)}) collective-permute-start(bf16[128,1792]{1,0:T(8,128)(2,1)S(1)} %far.1), channel_id=1, source_target_pairs={{0,512},{256,768},{512,0},{768,256},{1,513},{257,769},{513,1},{769... | collective-permute-start | bytes 1376264 | tf_op jit(solution)/shard_map/ppermute | solution.py:238
  100.6 3.5 %collective-permute-done.5.refs_1_ = bf16[128,1792]{1,0:T(8,128)(2,1)S(1)} collective-permute-done((bf16[128,1792]{1,0:T(8,128)(2,1)S(1)}, bf16[128,1792]{1,0:T(8,128)(2,1)S(1)}, u32[]{:S(2)}, u32[]{:S(2)}) %collective-permute-start.5) | collective-permute-done | bytes 458784 | tf_op jit(solution)/shard_map/ppermute | solution.py:238
  104.2 6.3 %collective-permute-done.8.refs_1_ = bf16[128,1792]{1,0:T(8,128)(2,1)S(1)} collective-permute-done((bf16[128,1792]{1,0:T(8,128)(2,1)S(1)}, bf16[128,1792]{1,0:T(8,128)(2,1)S(1)}, u32[]{:S(2)}, u32[]{:S(2)}) %collective-permute-start.8) | collective-permute-done | bytes 458784 | tf_op jit(solution)/shard_map/ppermute | solution.py:238
  110.9 29.9 %all_to_all.45 = bf16[16,8,1792]{2,1,0:T(8,128)(2,1)S(1)} all-to-all(bf16[16,8,1792]{2,1,0:T(8,128)(2,1)S(1)} %bitcast.14), channel_id=1, replica_groups=mesh['x'=4,'core'=2,'node'=8,'local'=16] {'local'}, dimensions={0} | all-to-all | bytes 917504 | tf_op jit(solution)/shard_map/all_to_all | solution.py:189
  140.8 0.8 combine.1
  141.6 15.1 %all_to_all.46 = bf16[8,8,1920]{2,1,0:T(8,128)(2,1)S(1)} all-to-all(bf16[8,8,1920]{2,1,0:T(8,128)(2,1)S(1)} %bitcast.21), channel_id=1, replica_groups=mesh['x'=4,'core'=2,'node'=8,'local'=16] {'node'}, dimensions={0} | all-to-all | bytes 491520 | tf_op jit(solution)/shard_map/all_to_all | solution.py:189
  (20 shorter events, 2.0 us)
Async XLA Ops:
  0.6 40.6 %copy-start.4 = (bf16[1,3584,128]{2,1,0:T(8,128)(2,1)S(1)}, bf16[1,3584,128]{2,1,0:T(8,128)(2,1)}, u32[]{:S(2)}) copy-start(bf16[1,3584,128]{2,1,0:T(8,128)(2,1)} %param.13) | copy-start | bytes 2752516
  0.6 42.5 %copy-start.6 = (bf16[1,3584,128]{2,1,0:T(8,128)(2,1)S(1)}, bf16[1,3584,128]{2,1,0:T(8,128)(2,1)}, u32[]{:S(2)}) copy-start(bf16[1,3584,128]{2,1,0:T(8,128)(2,1)} %param.14) | copy-start | bytes 2752516
  2.3 18.6 %all-to-all-start = ((bf16[8,8,1920]{2,1,0:T(8,128)(2,1)}), bf16[8,8,1920]{2,1,0:T(8,128)(2,1)S(1)}, u32[]{:S(2)}, u32[]{:S(2)}) async-start(bf16[8,8,1920]{2,1,0:T(8,128)(2,1)} %bitcast.28), calls=%async_computation | async-start | bytes 491520 | tf_op jit(solution)/shard_map/all_to_all | solution.py:189
  22.4 42.7 %all-to-all-start.1 = ((bf16[16,8,1792]{2,1,0:T(8,128)(2,1)}), bf16[16,8,1792]{2,1,0:T(8,128)(2,1)S(1)}, u32[]{:S(2)}, u32[]{:S(2)}) async-start(bf16[16,8,1792]{2,1,0:T(8,128)(2,1)} %bitcast.3), calls=%async_computation.1 | async-start | bytes 917504 | tf_op jit(solution)/shard_map/all_to_all | solution.py:189
  41.2 6.3 %collective-permute-start = (bf16[3584,128]{1,0:T(8,128)(2,1)S(1)}, bf16[3584,128]{1,0:T(8,128)(2,1)S(1)}, u32[]{:S(2)}, u32[]{:S(2)}) collective-permute-start(bf16[3584,128]{1,0:T(8,128)(2,1)S(1)} %bitcast.22), channel_id=1, source_target_pairs={{0,128},{128,0},{1,129},{129,1},{2,130},{130,2},{3,131},{131,3},{4... | collective-permute-start | bytes 2752520 | tf_op jit(solution)/shard_map/ppermute | solution.py:263
  43.2 4.5 %collective-permute-start.1 = (bf16[3584,128]{1,0:T(8,128)(2,1)S(1)}, bf16[3584,128]{1,0:T(8,128)(2,1)S(1)}, u32[]{:S(2)}, u32[]{:S(2)}) collective-permute-start(bf16[3584,128]{1,0:T(8,128)(2,1)S(1)} %bitcast.24), channel_id=1, source_target_pairs={{0,128},{128,0},{1,129},{129,1},{2,130},{130,2},{3,131},{131,3},{4... | collective-permute-start | bytes 2752520 | tf_op jit(solution)/shard_map/ppermute | solution.py:263
  45.6 4.6 %collective-permute-start.2 = (bf16[128,3584]{1,0:T(8,128)(2,1)}, bf16[128,3584]{1,0:T(8,128)(2,1)S(1)}, u32[]{:S(2)}, u32[]{:S(2)}) collective-permute-start(bf16[128,3584]{1,0:T(8,128)(2,1)} %bitcast.26), channel_id=1, source_target_pairs={{0,128},{128,0},{1,129},{129,1},{2,130},{130,2},{3,131},{131,3},{4... | collective-permute-start | bytes 2752520 | tf_op jit(solution)/shard_map/ppermute | solution.py:263
  50.2 1.2 copy-start.5
  51.4 1.2 copy-start.7
  52.5 1.2 copy-start.8
  54.5 1.3 copy-start
  55.7 0.9 copy-start.2
  65.0 15.0 %collective-permute-start.3 = (bf16[128,1792]{1,0:T(8,128)(2,1)S(1)}, bf16[128,1792]{1,0:T(8,128)(2,1)S(1)}, u32[]{:S(2)}, u32[]{:S(2)}) collective-permute-start(bf16[128,1792]{1,0:T(8,128)(2,1)S(1)} %bitcast.16), channel_id=1, source_target_pairs={{0,256},{256,512},{512,768},{768,0},{1,257},{257,513},{513,769},{7... | collective-permute-start | bytes 1376264 | tf_op jit(solution)/shard_map/ppermute | solution.py:238
  67.4 17.6 %collective-permute-start.4 = (bf16[128,1792]{1,0:T(8,128)(2,1)S(1)}, bf16[128,1792]{1,0:T(8,128)(2,1)S(1)}, u32[]{:S(2)}, u32[]{:S(2)}) collective-permute-start(bf16[128,1792]{1,0:T(8,128)(2,1)S(1)} %bitcast.17), channel_id=1, source_target_pairs={{0,768},{256,0},{512,256},{768,512},{1,769},{257,1},{513,257},{769... | collective-permute-start | bytes 1376264 | tf_op jit(solution)/shard_map/ppermute | solution.py:238
  70.9 1.5 copy-start.1
  72.4 1.2 copy-start.3
  76.7 18.8 %collective-permute-start.7 = (bf16[128,1792]{1,0:T(8,128)(2,1)S(1)}, bf16[128,1792]{1,0:T(8,128)(2,1)S(1)}, u32[]{:S(2)}, u32[]{:S(2)}) collective-permute-start(bf16[128,1792]{1,0:T(8,128)(2,1)S(1)} %bitcast.19), channel_id=1, source_target_pairs={{0,512},{256,768},{512,0},{768,256},{1,513},{257,769},{513,1},{769... | collective-permute-start | bytes 1376264 | tf_op jit(solution)/shard_map/ppermute | solution.py:238
  88.4 15.7 %collective-permute-start.5 = (bf16[128,1792]{1,0:T(8,128)(2,1)S(1)}, bf16[128,1792]{1,0:T(8,128)(2,1)S(1)}, u32[]{:S(2)}, u32[]{:S(2)}) collective-permute-start(bf16[128,1792]{1,0:T(8,128)(2,1)S(1)} %get-tuple-element.19), channel_id=1, source_target_pairs={{0,768},{256,0},{512,256},{768,512},{1,769},{257,1},{513,257},{769... | collective-permute-start | bytes 1376264 | tf_op jit(solution)/shard_map/ppermute | solution.py:238
  90.4 13.8 %collective-permute-start.6 = (bf16[128,1792]{1,0:T(8,128)(2,1)S(1)}, bf16[128,1792]{1,0:T(8,128)(2,1)S(1)}, u32[]{:S(2)}, u32[]{:S(2)}) collective-permute-start(bf16[128,1792]{1,0:T(8,128)(2,1)S(1)} %get-tuple-element.20), channel_id=1, source_target_pairs={{0,256},{256,512},{512,768},{768,0},{1,257},{257,513},{513,769},{7... | collective-permute-start | bytes 1376264 | tf_op jit(solution)/shard_map/ppermute | solution.py:238
  98.6 11.9 %collective-permute-start.8 = (bf16[128,1792]{1,0:T(8,128)(2,1)S(1)}, bf16[128,1792]{1,0:T(8,128)(2,1)S(1)}, u32[]{:S(2)}, u32[]{:S(2)}) collective-permute-start(bf16[128,1792]{1,0:T(8,128)(2,1)S(1)} %far.1), channel_id=1, source_target_pairs={{0,512},{256,768},{512,0},{768,256},{1,513},{257,769},{513,1},{769... | collective-permute-start | bytes 1376264 | tf_op jit(solution)/shard_map/ppermute | solution.py:238
